TPU v7x, 512 devices: a whole 4x8x8 slice. The times are simulated.
512 devices in a mesh: tp: 8 (over y), fsdp: 64 (over z, x, core).
Axes of the slice: x: 4, y: 8, z: 8, core: 2. Of those that a mesh axis runs over, the one named last changes fastest.
Arguments:
- decoded: bfloat16 [8192, 4096], P('fsdp', 'tp'), may hold values from -6 to 6
- lengths: int32 [64, 8], P('fsdp'), may hold values from 1 to 32, 128 in all within a row
- destination: int32 [8192, 1], P('fsdp'), may hold values from 0 to 63; in each aligned block of 128 rows (0 to 127, 128 to 255, ...) at most 2 rows name the same one
- attn_gain: bfloat16 [4096], replicated, may hold values from 0.099609375 to 1.8984375
- query_weight: bfloat16 [4096, 4096], P('fsdp', 'tp'), may hold values from -1.5625 to 1.5625, as said below
- key_weight: bfloat16 [4096, 256], P('fsdp'), may hold values from -0.0625 to 0.0625, as said below
- value_weight: bfloat16 [4096, 256], P('fsdp'), may hold values from -0.09375 to 0.09375
- out_weight: bfloat16 [4096, 4096], P('tp', 'fsdp'), may hold values from -0.09375 to 0.09375
- final_gain: bfloat16 [4096], P('tp'), may hold values from 0.099609375 to 1.8984375
- head_weight: bfloat16 [4096], P('tp'), may hold values from -0.09375 to 0.09375
Outputs:
- hidden: bfloat16 [8192, 4096], P('fsdp', 'tp')
- rewards: float32 [512], P('fsdp')
Inputs may be any that keep to these rules, and one draw needn't show every extreme that they name: `destination`: in each decode group's 128 rows every reward shard is named by exactly 2 rows. Each decode group's 8 lengths add up to 128; in each group the longest is 32. `query_weight`: entries of order one over the square root of 4096. `key_weight`: entries of order one over the square root of 4096.
All inputs are finite; a program needn't handle non-finite values.
Results may differ from a plain program's by a relative error of at most 0.017.
Values may be sent and summed in bfloat16 or wider, within the bound.
No kernel may reach another device: no remote copies, remote signals or barrier semaphores. Data moves between devices by JAX's collectives and lax.ppermute only.
A program may use at most 64 MiB of HBM per device.

v0:
```python
import math

import jax
import jax.numpy as jnp
from jax import lax
from jax.sharding import PartitionSpec as P

D = 4096
HD = 128
QH = 32
KVH = 2
LMAX = 32


norm_eps = 1e-06
rope_base = 1000000.0
neg_fill = -1e30


def rotate(heads_in, positions):
    half_size = heads_in.shape[-1] // 2
    frequency = rope_base ** (
        -(jnp.arange(half_size, dtype=jnp.float32) * 2.0 / heads_in.shape[-1])
    )
    angles = positions.astype(jnp.float32)[:, None] * frequency[None, :]
    cosine = jnp.cos(angles)[:, None, :]
    sine_part = jnp.sin(angles)[:, None, :]
    front_half = heads_in[..., :half_size]
    back_half = heads_in[..., half_size:]
    return jnp.concatenate(
        [front_half * cosine - back_half * sine_part, back_half * cosine + front_half * sine_part],
        axis=-1,
    )


def describe(resp_lengths, row_count):
    row_index = jnp.arange(row_count, dtype=jnp.int32)
    resp_ends = jnp.cumsum(resp_lengths)
    resp_local = jnp.sum((row_index[:, None] >= resp_ends[None, :]).astype(jnp.int32), axis=1)
    resp_length = jnp.take(resp_lengths, resp_local)
    positions = row_index - (jnp.take(resp_ends, resp_local) - resp_length)
    return (resp_local, positions, positions == resp_length - 1)


def attend_picked(key_sel, value_sel, queries, query_pos):
    span = key_sel.shape[1]
    scores = jnp.einsum("shd,skd->shk", queries, key_sel, preferred_element_type=jnp.float32) * (
        1.0 / math.sqrt(queries.shape[-1])
    )
    allowed = jnp.arange(span, dtype=jnp.int32)[None, :] <= query_pos[:, None]
    scores = jnp.where(allowed[:, None, :], scores, neg_fill)
    row_max = jnp.max(scores, axis=2)
    weights = jnp.where(allowed[:, None, :], jnp.exp(scores - row_max[:, :, None]), 0.0)
    totals = jnp.sum(weights, axis=2)
    weighted = jnp.einsum(
        "shk,skd->shd", weights.astype(jnp.bfloat16), value_sel, preferred_element_type=jnp.float32
    )
    return (totals, weighted)


def score_layer(
    block_rows,
    resp_ids,
    positions,
    resp_total,
    attn_gain,
    query_weight,
    key_weight,
    value_weight,
    out_weight,
    final_gain,
    head_weight,
):
    row_count = block_rows.shape[0]
    whole = lax.all_gather(block_rows, "tp", axis=1, tiled=True)
    widened = whole.astype(jnp.float32)
    normed = (
        widened
        * lax.rsqrt(jnp.mean(widened * widened, axis=1, keepdims=True) + norm_eps)
        * attn_gain.astype(jnp.float32)
    ).astype(jnp.bfloat16)
    query_cols = jnp.dot(
        normed,
        lax.all_gather(query_weight, "fsdp", axis=0, tiled=True),
        preferred_element_type=jnp.float32,
    )
    key_all = jnp.dot(
        normed,
        lax.all_gather(key_weight, "fsdp", axis=0, tiled=True),
        preferred_element_type=jnp.float32,
    )
    value_all = jnp.dot(
        normed,
        lax.all_gather(value_weight, "fsdp", axis=0, tiled=True),
        preferred_element_type=jnp.float32,
    )
    heads_local = query_cols.shape[1] // HD
    kv_group = lax.axis_index("tp") * heads_local // (QH // KVH)
    key_rows = lax.dynamic_slice_in_dim(key_all, kv_group * HD, HD, 1)
    value_rows = lax.dynamic_slice_in_dim(value_all, kv_group * HD, HD, 1).astype(jnp.bfloat16)
    key_rows = rotate(key_rows[:, None, :], positions)[:, 0, :].astype(jnp.bfloat16)
    queries = rotate(query_cols.reshape(row_count, heads_local, HD), positions).astype(jnp.bfloat16)
    keys_every, values_every, ids_every, pos_every = (
        lax.all_gather(key_rows, "fsdp", axis=0, tiled=True),
        lax.all_gather(value_rows, "fsdp", axis=0, tiled=True),
        lax.all_gather(resp_ids, "fsdp", axis=0, tiled=True),
        lax.all_gather(positions, "fsdp", axis=0, tiled=True),
    )
    flat_slot = (ids_every * LMAX + pos_every).astype(jnp.int32)
    table = (
        jnp.zeros((resp_total * LMAX,), jnp.int32)
        .at[flat_slot]
        .set(jnp.arange(ids_every.shape[0], dtype=jnp.int32))
    )
    picks = table.reshape(resp_total, LMAX)[resp_ids]
    running_sum, weighted = attend_picked(
        keys_every[picks], values_every[picks], queries, positions
    )
    attended = (
        (weighted / running_sum[:, :, None])
        .reshape(row_count, heads_local * HD)
        .astype(jnp.bfloat16)
    )
    partial_value = jnp.dot(
        attended,
        lax.all_gather(out_weight, "fsdp", axis=1, tiled=True),
        preferred_element_type=jnp.float32,
    )
    update = lax.psum_scatter(
        partial_value.astype(jnp.bfloat16), "tp", scatter_dimension=1, tiled=True
    ).astype(jnp.float32)
    layer_rows = (block_rows.astype(jnp.float32) + update).astype(jnp.bfloat16)
    layer_wide = layer_rows.astype(jnp.float32)
    squares, product = lax.psum(
        (
            jnp.sum(layer_wide * layer_wide, axis=1),
            jnp.sum(
                layer_wide * final_gain.astype(jnp.float32) * head_weight.astype(jnp.float32),
                axis=1,
            ),
        ),
        "tp",
    )
    row_reward = lax.rsqrt(squares / D + norm_eps) * product
    return (layer_rows, row_reward)


def body(
    decoded,
    lengths,
    destination,
    attn_gain,
    query_weight,
    key_weight,
    value_weight,
    out_weight,
    final_gain,
    head_weight,
):
    row_count = decoded.shape[0]
    shard_count = lax.axis_size("fsdp")
    resp_count = lengths.shape[1]
    resp_total = shard_count * resp_count
    resp_local, positions, is_last = describe(lengths[0], row_count)
    dest_shard = destination[:, 0]
    dest_hits = (dest_shard[:, None] == jnp.arange(shard_count, dtype=jnp.int32)[None, :]).astype(
        jnp.int32
    )
    dest_rank = jnp.sum(jnp.cumsum(dest_hits, axis=0) * dest_hits, axis=1) - 1
    slot_index = dest_shard * (row_count // shard_count) + dest_rank
    send_order = (
        jnp.zeros((row_count,), jnp.int32)
        .at[slot_index]
        .set(jnp.arange(row_count, dtype=jnp.int32))
    )
    resp_ids = lax.axis_index("fsdp") * resp_count + resp_local
    labels = jnp.stack([resp_ids, positions, is_last.astype(jnp.int32)], axis=1)[send_order]
    arrived, arrived_labels = (
        lax.all_to_all(decoded[send_order], "fsdp", split_axis=0, concat_axis=0, tiled=True),
        lax.all_to_all(labels, "fsdp", split_axis=0, concat_axis=0, tiled=True),
    )
    hidden, row_reward = score_layer(
        arrived,
        arrived_labels[:, 0],
        arrived_labels[:, 1],
        resp_total,
        attn_gain,
        query_weight,
        key_weight,
        value_weight,
        out_weight,
        final_gain,
        head_weight,
    )
    picked = (
        (arrived_labels[:, 0][:, None] == jnp.arange(resp_total, dtype=jnp.int32)[None, :])
        & (arrived_labels[:, 2][:, None] == 1)
    ).astype(jnp.float32)
    rewards = lax.psum_scatter(
        jnp.sum(picked * row_reward[:, None], axis=0), "fsdp", scatter_dimension=0, tiled=True
    )
    return (hidden, rewards)


def solution(mesh):
    return jax.shard_map(
        body,
        mesh=mesh,
        in_specs=(
            P("fsdp", "tp"),
            P("fsdp", None),
            P("fsdp", None),
            P(),
            P("fsdp", "tp"),
            P("fsdp", None),
            P("fsdp", None),
            P("tp", "fsdp"),
            P("tp"),
            P("tp"),
        ),
        out_specs=(P("fsdp", "tp"), P("fsdp")),
        check_vma=False,
    )
```

profile of v0, /device:TPU:1, one launch (start us, length us, event | category | flops | bytes accessed | tf_op | source)
XLA Modules:
  0.0 779.0 jit_solution(17048294356051700935)
XLA Ops:
  13.2 5.0 add_bitcast_fusion
  19.1 25.7 %all_to_all.24 = bf16[64,2,512]{2,1,0:T(2,128)(2,1)S(1)} all-to-all(bf16[64,2,512]{2,1,0:T(2,128)(2,1)S(1)} %all_to_all.16), channel_id=1, replica_groups=mesh['tp'=8,'fsdp'=64] {'fsdp'}, dimensions={0} | all-to-all | bytes 262144 | tf_op jit(solution)/shard_map/all_to_all | solution.py:179
  47.8 5.0 fusion.33
  54.2 4.4 all-to-all-start.1
  58.7 10.0 %all-to-all-done.1 = s32[64,2,3]{2,1,0:T(2,128)S(1)} async-done(((s32[64,2,3]{2,1,0:T(2,128)}), s32[64,2,3]{2,1,0:T(2,128)S(1)}, u32[]{:S(2)}, u32[]{:S(2)}) %all-to-all-start.1) | async-done | bytes 1568 | tf_op jit(solution)/shard_map/all_to_all | solution.py:180
  68.9 8.4 %all-gather.11.cloned.1.call-done = bf16[128,4096]{1,0:T(8,128)(2,1)} async-done(((bf16[128,512]{1,0:T(8,128)(2,1)}), bf16[128,4096]{1,0:T(8,128)(2,1)}) %all-gather.11.cloned.1.call-update) | async-done | bytes 1048592 | tf_op jit(solution)/shard_map/all_gather | solution.py:75
  78.9 88.7 %all-gather.15.cloned.1.call-done = bf16[4096,256]{1,0:T(8,128)(2,1)} async-done(((bf16[64,256]{1,0:T(8,128)(2,1)}), bf16[4096,256]{1,0:T(8,128)(2,1)}) %all-gather.15.cloned.1.call-update) | async-done | bytes 2097168 | tf_op jit(solution)/shard_map/all_gather | solution.py:89
  167.5 2.4 fusion.41
  171.6 80.0 %all-gather.17.cloned.1.call-done = bf16[4096,256]{1,0:T(8,128)(2,1)} async-done(((bf16[64,256]{1,0:T(8,128)(2,1)}), bf16[4096,256]{1,0:T(8,128)(2,1)}) %all-gather.17.cloned.1.call-update) | async-done | bytes 2097168 | tf_op jit(solution)/shard_map/all_gather | solution.py:94
  251.5 2.1 fusion.39
  255.1 38.0 %all-gather.2 = s32[8192,1]{0,1:T(1,128)S(1)} all-gather(s32[128,1]{0,1:T(1,128)S(1)} %copy.29), channel_id=4, replica_groups=mesh['tp'=8,'fsdp'=64] {'fsdp'}, dimensions={0}, use_global_device_ids=true | all-gather | bytes 33280 | tf_op jit(solution)/shard_map/all_gather | solution.py:107
  293.2 37.4 %all-gather.1 = s32[8192,1]{0,1:T(1,128)S(1)} all-gather(s32[128,1]{0,1:T(1,128)S(1)} %copy.30), channel_id=3, replica_groups=mesh['tp'=8,'fsdp'=64] {'fsdp'}, dimensions={0}, use_global_device_ids=true | all-gather | bytes 33280 | tf_op jit(solution)/shard_map/all_gather | solution.py:106
  330.6 30.7 %scatter_custom_fusion.1 = s32[16384]{0:T(1024)S(1)} fusion(s32[8192]{0:T(1024)S(1)} %compare_select_fusion.1, s32[8192]{0:T(1024)S(1)} %iota.38, s32[]{:T(128)} %constant.32.clone.1), kind=kCustom, calls=%fused_computation.60 | custom fusion | bytes 65540 | tf_op jit(solution)/shard_map/scatter | solution.py:113
  363.8 3.2 copy.27
  367.1 50.5 %all-gather.13.cloned.1.call-done = bf16[4096,512]{1,0:T(8,128)(2,1)} async-done(((bf16[64,512]{1,0:T(8,128)(2,1)}), bf16[4096,512]{1,0:T(8,128)(2,1)}) %all-gather.13.cloned.1.call-update) | async-done | bytes 4194320 | tf_op jit(solution)/shard_map/all_gather | solution.py:84
  417.6 3.7 fusion.43
  422.3 12.1 %gather_fusion.3 = bf16[4096,128]{1,0:T(8,128)(2,1)S(1)} fusion(bf16[8192,128]{1,0:T(8,128)(2,1)S(1)} %copy.27, s32[4096]{0:T(1024)S(1)} %broadcast_clamp_fusion), kind=kCustom, calls=%fused_computation.3 | custom fusion | bytes 2113536 | tf_op jit(solution)/shard_map/gather | solution.py:117
  434.4 66.5 %all-gather.19.cloned.1.call-done = bf16[8192,128]{1,0:T(8,128)(2,1)} async-done(((bf16[128,128]{1,0:T(8,128)(2,1)}), bf16[8192,128]{1,0:T(8,128)(2,1)}) %all-gather.19.cloned.1.call-update) | async-done | bytes 2097168 | tf_op jit(solution)/shard_map/all_gather | solution.py:105
  501.0 12.9 %gather_fusion.4 = bf16[4096,128]{1,0:T(8,128)(2,1)S(1)} fusion(bf16[8192,128]{1,0:T(8,128)(2,1)} %all-gather.19.cloned.1.call-done, s32[4096]{0:T(1024)S(1)} %broadcast_clamp_fusion), kind=kCustom, calls=%fused_computation.4 | custom fusion | bytes 2113536 | tf_op jit(solution)/shard_map/gather | solution.py:117
  515.4 71.3 %all-gather.21.cloned.1.call-done = bf16[512,4096]{0,1:T(8,128)(2,1)} async-done(((bf16[512,64]{0,1:T(8,128)(2,1)}), bf16[512,4096]{0,1:T(8,128)(2,1)}) %all-gather.21.cloned.1.call-update) | async-done | bytes 4194320 | tf_op jit(solution)/shard_map/all_gather | solution.py:126
  586.7 4.7 convolution_convert_fusion
  593.6 31.0 %reduce-scatter.2.cloned.1.call-done = bf16[128,512]{1,0:T(8,128)(2,1)} async-done(((bf16[128,4096]{1,0:T(8,128)(2,1)}), bf16[128,512]{1,0:T(8,128)(2,1)}) %reduce-scatter.2.cloned.1.call-update) | async-done | bytes 131088 | tf_op jit(solution)/shard_map/reduce_scatter | solution.py:129
  626.3 12.2 %all-reduce.1 = (f32[128]{0:T(128)S(1)}, f32[128]{0:T(128)S(1)}) all-reduce(f32[128]{0:T(128)S(1)} %get-tuple-element.4, f32[128]{0:T(128)S(1)} %get-tuple-element.3), channel_id=1, replica_groups=mesh['tp'=8,'fsdp'=64] {'tp'}, use_global_device_ids=true, to_apply=%region_13.15 | all-reduce | flops 256 | bytes 2048 | tf_op jit(solution)/shard_map/psum | solution.py:134
  638.6 133.0 %all-reduce = f32[512]{0:T(512)S(1)} all-reduce(f32[512]{0:T(512)S(1)} %select_reduce_fusion), channel_id=6, replica_groups=mesh['tp'=8,'fsdp'=64] {'fsdp'}, use_global_device_ids=true, to_apply=%region_15.17.clone | all-reduce | flops 512 | bytes 4096
  (106 shorter events, 24.9 us)
Async XLA Ops:
  7.2 11.0 %copy-start = (bf16[128,512]{1,0:T(8,128)(2,1)S(1)}, bf16[128,512]{1,0:T(8,128)(2,1)}, u32[]{:S(2)}) copy-start(bf16[128,512]{1,0:T(8,128)(2,1)} %param.12) | copy-start | bytes 393220
  7.2 51.5 %copy-start.10 = (bf16[4096]{0:T(1024)(128)(2,1)S(1)}, bf16[4096]{0:T(1024)(128)(2,1)}, u32[]{:S(2)}) copy-start(bf16[4096]{0:T(1024)(128)(2,1)} %param.15) | copy-start | bytes 24580
  7.2 70.1 %all-gather.11.cloned.1.call-start = ((), (), s32[]{:S(2)}) async-start(), calls=%async_computation.3 | async-start | bytes 1179648 | tf_op jit(solution)/shard_map/all_gather | solution.py:75
  45.6 121.9 %all-gather.15.cloned.1.call-start = ((), (), s32[]{:S(2)}) async-start(), calls=%async_computation.5 | async-start | bytes 2129920 | tf_op jit(solution)/shard_map/all_gather | solution.py:89
  46.4 205.2 %all-gather.17.cloned.1.call-start = ((), (), s32[]{:S(2)}) async-start(), calls=%async_computation.6 | async-start | bytes 2129920 | tf_op jit(solution)/shard_map/all_gather | solution.py:94
  54.2 14.6 %all-to-all-start.1 = ((s32[64,2,3]{2,1,0:T(2,128)}), s32[64,2,3]{2,1,0:T(2,128)S(1)}, u32[]{:S(2)}, u32[]{:S(2)}) async-start(s32[64,2,3]{2,1,0:T(2,128)} %bitcast.25), calls=%async_computation.1 | async-start | bytes 131072 | tf_op jit(solution)/shard_map/all_to_all | solution.py:180
  58.6 305.2 %all-gather.23.cloned.1.call-start = ((), (), s32[]{:S(2)}) async-start(), calls=%async_computation.10 | async-start | bytes 2129920 | tf_op jit(solution)/shard_map/all_gather | solution.py:104
  58.7 192.8 %copy-start.7 = (f32[4096]{0:T(1024)}, f32[4096]{0:T(1024)S(1)}, u32[]{:S(2)}) copy-start(f32[4096]{0:T(1024)S(1)} %convert_element_type.64) | copy-start | bytes 49156
  68.7 101.2 %copy-start.3 = (s32[64,2,3]{2,1,0:T(2,128)}, s32[64,2,3]{2,1,0:T(2,128)S(1)}, u32[]{:S(2)}) copy-start(s32[64,2,3]{2,1,0:T(2,128)S(1)} %all-to-all-done.1) | copy-start | bytes 4612
  78.9 172.7 %copy-start.15 = (f32[128]{0:T(128)}, f32[128]{0:T(128)S(1)}, u32[]{:S(2)}) copy-start(f32[128]{0:T(128)S(1)} %add_rsqrt_fusion) | copy-start | bytes 1540
  78.9 172.7 %copy-start.2 = (bf16[128,4096]{1,0:T(8,128)(2,1)S(1)}, bf16[128,4096]{1,0:T(8,128)(2,1)}, u32[]{:S(2)}) copy-start(bf16[128,4096]{1,0:T(8,128)(2,1)} %all-gather.11.cloned.1.call-done) | copy-start | bytes 3145732
  170.9 246.6 %all-gather.13.cloned.1.call-start = ((), (), s32[]{:S(2)}) async-start(), calls=%async_computation.4 | async-start | bytes 4259840 | tf_op jit(solution)/shard_map/all_gather | solution.py:84
  171.5 329.4 %all-gather.19.cloned.1.call-start = ((), (), s32[]{:S(2)}) async-start(), calls=%async_computation.7 | async-start | bytes 2129920 | tf_op jit(solution)/shard_map/all_gather | solution.py:105
  254.3 332.5 %all-gather.21.cloned.1.call-start = ((), (), s32[]{:S(2)}) async-start(), calls=%async_computation.8 | async-start | bytes 4259840 | tf_op jit(solution)/shard_map/all_gather | solution.py:126
  255.0 369.6 %reduce-scatter.2.cloned.1.call-start = ((), (), s32[]{:S(2)}) async-start(), calls=%async_computation.9 | async-start | bytes 1179648 | tf_op jit(solution)/shard_map/reduce_scatter | solution.py:129
  255.1 106.3 %copy-start.11 = (s32[128,1]{0,1:T(1,128)}, s32[128,1]{0,1:T(1,128)S(1)}, u32[]{:S(2)}) copy-start(s32[128,1]{0,1:T(1,128)S(1)} %copy.30) | copy-start | bytes 1540
  363.8 53.7 %copy-start.8 = (f32[4096]{0:T(1024)S(1)}, f32[4096]{0:T(1024)}, u32[]{:S(2)}) copy-start(f32[4096]{0:T(1024)} %copy-done.7) | copy-start | bytes 49156
  363.8 53.7 %copy-start.16 = (f32[128]{0:T(128)S(1)}, f32[128]{0:T(128)}, u32[]{:S(2)}) copy-start(f32[128]{0:T(128)} %copy-done.15) | copy-start | bytes 1540
  434.4 79.4 %copy-start.5 = (f32[128,64]{1,0:T(8,128)S(1)}, f32[128,64]{1,0:T(8,128)}, u32[]{:S(2)}) copy-start(f32[128,64]{1,0:T(8,128)} %get-tuple-element.16) | copy-start | bytes 98308
  434.4 79.4 %copy-start.6 = (f32[128,64]{1,0:T(8,128)S(1)}, f32[128,64]{1,0:T(8,128)}, u32[]{:S(2)}) copy-start(f32[128,64]{1,0:T(8,128)} %get-tuple-element.17) | copy-start | bytes 98308
  434.4 79.7 %copy-start.9 = (pred[128,32]{1,0:T(8,128)(4,1)S(1)}, pred[128,32]{1,0:T(8,128)(4,1)}, u32[]{:S(2)}) copy-start(pred[128,32]{1,0:T(8,128)(4,1)} %iota_compare_fusion.1) | copy-start | bytes 12292
  586.7 6.7 copy-start.4
  586.7 37.9 %copy-start.1 = (bf16[128,512]{1,0:T(8,128)(2,1)S(1)}, bf16[128,512]{1,0:T(8,128)(2,1)}, u32[]{:S(2)}) copy-start(bf16[128,512]{1,0:T(8,128)(2,1)} %all_to_all.18) | copy-start | bytes 393220
  586.7 51.8 %copy-start.12 = (s32[128,1]{0,1:T(1,128)S(1)}, s32[128,1]{0,1:T(1,128)}, u32[]{:S(2)}) copy-start(s32[128,1]{0,1:T(1,128)} %copy-done.11) | copy-start | bytes 1540
  (2 other events, 9.5 us)
Sparse Core Ops, SparseCore 0:
  45.7 31.5 all-gather.10
  80.7 86.8 all-gather.14
  170.9 80.5 all-gather.16
  254.6 75.8 all-gather.22
  333.7 83.8 all-gather.12
  420.8 80.1 all-gather.18
  504.3 82.3 all-gather.20
  591.6 33.0 reduce-scatter.1
where the time goes:
time: 780 us; the launch traced here: 779 us
  waiting for transfers between devices  409 us (52%)
  blocking collectives  246 us (32%)
  local copies, waits for them, and re-layouts  70 us (9%)
  other arithmetic  19.6 us (3%)
  between operations  15.2 us (2%)
  matrix products  14.1 us (2%)
    unnamed x1, blocking collectives  133 us
    all_gather x1, waiting for transfers between devices, score_layer(): lax.all_gather(key_weight, 'fsdp', axis=0, tiled=True)  88.7 us
    all_gather x1, waiting for transfers between devices, score_layer(): lax.all_gather(value_weight, 'fsdp', axis=0, tiled=True)  80 us
    all_gather x1, waiting for transfers between devices, score_layer(): lax.all_gather(out_weight, 'fsdp', axis=1, tiled=True)  71.3 us
    all_gather x1, waiting for transfers between devices, score_layer(): lax.all_gather(value_rows, 'fsdp', axis=0, tiled=True)  66.5 us
    all_gather x1, waiting for transfers between devices, score_layer(): lax.all_gather(query_weight, 'fsdp', axis=0, tiled=True)  50.5 us
    all_gather x1, blocking collectives, score_layer(): lax.all_gather(positions, 'fsdp', axis=0, tiled=True)  38 us
    all_gather x1, blocking collectives, score_layer(): lax.all_gather(resp_ids, 'fsdp', axis=0, tiled=True)  37.4 us
  transfers between devices with their start and end apart: 9, of which 8 were waited for; matrix products, arithmetic and copies ran while one was open for 11% of the time, Pallas kernels for 0%

commit v1 on v0

v1 whole, which is shorter than its diff:
```python
import jax
import jax.numpy as jnp
from jax import lax
from jax.experimental import pallas as pl
from jax.experimental.pallas import tpu as pltpu
from jax.sharding import Mesh, PartitionSpec as P

D = 4096
HD = 128
QH = 32
KVH = 2
NT, NZ, NX, NC = 8, 8, 4, 2
ROWS = 128
FEAT = D // NT
BLK = 128
QW = QH * HD // NT
PW = QW + 2 * HD
HEADS = QW // HD
EXTRA = 16
RESP = 8

norm_eps = 1e-06
rope_base = 1000000.0
neg_fill = -1e30

bf16 = jnp.bfloat16
f32 = jnp.float32

VMEM = pl.BlockSpec(memory_space=pltpu.VMEM)
SMEM = pl.BlockSpec(memory_space=pltpu.SMEM)


def call(kernel, out_shape, in_specs, scratch=(), flops=0, name=None):
    return pl.pallas_call(
        kernel,
        out_shape=out_shape,
        in_specs=in_specs,
        out_specs=jax.tree.map(lambda _: VMEM, out_shape),
        scratch_shapes=list(scratch),
        compiler_params=pltpu.CompilerParams(vmem_limit_bytes=24 * 1024 * 1024),
        cost_estimate=pl.CostEstimate(flops=flops, bytes_accessed=4 << 20, transcendentals=0),
        name=name,
    )


def iota(shape, axis):
    return lax.broadcasted_iota(jnp.int32, shape, axis)


def eye_mask():
    return iota((ROWS, ROWS), 0) == iota((ROWS, ROWS), 1)


def resp_starts(lengths_ref, rows):
    end = jnp.int32(0)
    start = jnp.zeros_like(rows)
    for j in range(RESP):
        end = end + lengths_ref[0, j]
        start = jnp.where(rows >= end, end, start)
    return start


def project_kernel(core_ref, x_ref, own_ref, other_ref, gain_ref, out_ref, xs_ref, w_ref):
    first = core_ref[0] == 0
    for t in range(NT):
        own, other = own_ref[t], other_ref[t]
        w_ref[t * BLK : t * BLK + BLK // 2, :] = jnp.where(first, own, other)
        w_ref[t * BLK + BLK // 2 : (t + 1) * BLK, :] = jnp.where(first, other, own)
    eye = eye_mask()
    for g in range(NX):
        square = jnp.zeros((ROWS, BLK), f32)
        for t in range(NT):
            wide = x_ref[t * NX + g].astype(f32)
            square = square + wide * wide
            xs_ref[g * ROWS : (g + 1) * ROWS, t * BLK : (t + 1) * BLK] = (
                wide * gain_ref[t : t + 1, :].astype(f32)
            ).astype(bf16)
        total = jnp.sum(square, axis=1, keepdims=True)
        line = jnp.sum(jnp.where(eye, total, 0.0), axis=0, keepdims=True)
        high = line.astype(bf16).astype(f32)
        low = line - high
        which = iota((EXTRA, ROWS), 0)
        tail = jnp.where(which == 0, high, jnp.where(which == 1, low, 0.0)).astype(bf16)
        out_ref[g, ROWS:, :] = jnp.concatenate(
            [tail, jnp.zeros((EXTRA, PW - ROWS), bf16)], axis=1
        )
    for n in range(PW // 256):
        cols = slice(n * 256, (n + 1) * 256)
        part = jnp.dot(xs_ref[...], w_ref[:, cols], preferred_element_type=f32)
        for g in range(NX):
            out_ref[g, :ROWS, cols] = part[g * ROWS : (g + 1) * ROWS].astype(bf16)


def attend_kernel(lengths_ref, parts_ref, freq_ref, out_ref):
    eye = eye_mask()
    line = jnp.zeros((EXTRA, ROWS), f32)
    for i in range(NX):
        line = line + parts_ref[i, ROWS:, :ROWS].astype(f32)
    line = jnp.sum(line, axis=0, keepdims=True)
    total = jnp.sum(jnp.where(eye, line, 0.0), axis=1, keepdims=True)
    scale = lax.rsqrt(total * (1.0 / D) + norm_eps)

    rows = iota((ROWS, ROWS), 0)
    cols = iota((ROWS, ROWS), 1)
    start = resp_starts(lengths_ref, rows)
    allowed = (cols >= start) & (cols <= rows)
    angles = (rows - start).astype(f32) * freq_ref[...]
    cosine = jnp.cos(angles)
    sine = jnp.sin(angles)
    sine = jnp.where(cols < HD // 2, -sine, sine)

    def columns(at):
        summed = parts_ref[0, :ROWS, at : at + HD].astype(f32)
        for i in range(1, NX):
            summed = summed + parts_ref[i, :ROWS, at : at + HD].astype(f32)
        return summed * scale

    def rope(v):
        return (v * cosine + pltpu.roll(v, HD // 2, 1) * sine).astype(bf16)

    keys = rope(columns(QW))
    values = columns(QW + HD).astype(bf16)
    for h in range(HEADS):
        queries = rope(columns(h * HD))
        scores = lax.dot_general(
            queries, keys, (((1,), (1,)), ((), ())), preferred_element_type=f32
        ) * (HD**-0.5)
        scores = jnp.where(allowed, scores, neg_fill)
        top = jnp.max(scores, axis=1, keepdims=True)
        probs = jnp.where(allowed, jnp.exp(scores - top), 0.0)
        sums = jnp.sum(probs, axis=1, keepdims=True)
        weighted = jnp.dot(probs.astype(bf16), values, preferred_element_type=f32)
        out_ref[:, h * HD : (h + 1) * HD] = (weighted / sums).astype(bf16)


def output_kernel(x_ref, w_ref, out_ref):
    for n in range(NT // 2):
        part = lax.dot_general(
            x_ref[...],
            w_ref[n * 2 * BLK : (n + 1) * 2 * BLK, :],
            (((1,), (1,)), ((), ())),
            preferred_element_type=f32,
        )
        for g in range(NX):
            rows = part[g * ROWS : (g + 1) * ROWS].astype(bf16)
            out_ref[2 * n * NX + g] = rows[:, :BLK]
            out_ref[(2 * n + 1) * NX + g] = rows[:, BLK:]


def layer_kernel(lengths_ref, parts_ref, rows_ref, line_ref, final_ref, head_ref, out_ref, stat_ref):
    dest_line = line_ref[...]
    eye = eye_mask()
    dest_column = jnp.sum(jnp.where(eye, dest_line, 0), axis=1, keepdims=True)
    same = (dest_column == dest_line) & (iota((ROWS, ROWS), 0) < iota((ROWS, ROWS), 1))
    rank = jnp.sum(same.astype(jnp.int32), axis=0, keepdims=True)
    slot = dest_line * (ROWS // (NZ * NX * NC)) + rank
    order = (iota((ROWS, ROWS), 0) == slot).astype(f32).astype(bf16)

    square = jnp.zeros((ROWS, BLK), f32)
    product = jnp.zeros((ROWS, BLK), f32)
    for g in range(NX):
        cols = slice(g * BLK, (g + 1) * BLK)
        update = parts_ref[g].astype(f32)
        for t in range(1, NT):
            update = update + parts_ref[t * NX + g].astype(f32)
        layer = (rows_ref[:, cols].astype(f32) + update).astype(bf16)
        wide = layer.astype(f32)
        square = square + wide * wide
        product = product + wide * final_ref[:, cols].astype(f32) * head_ref[:, cols].astype(f32)
        out_ref[:, cols] = jnp.dot(order, layer, preferred_element_type=f32).astype(bf16)

    lane = iota((1, BLK), 1)
    last = jnp.full((1, BLK), -1, jnp.int32)
    end = jnp.int32(0)
    for j in range(RESP):
        end = end + lengths_ref[0, j]
        last = jnp.where(lane == j, end - 1, last)
    pick = iota((ROWS, BLK), 0) == last
    for at, part in ((0, square), (1, product)):
        column = jnp.sum(part, axis=1, keepdims=True)
        stat_ref[at : at + 1, :] = jnp.sum(jnp.where(pick, column, 0.0), axis=0, keepdims=True)


def body(
    decoded,
    lengths,
    destination,
    attn_gain,
    query_weight,
    key_weight,
    value_weight,
    out_weight,
    final_gain,
    head_weight,
):
    me_t, me_x, me_c = lax.axis_index("tp"), lax.axis_index("x"), lax.axis_index("core")
    fsdp = ("z", "x", "core")

    mine = out_weight.T
    theirs = lax.ppermute(mine, "core", [(0, 1), (1, 0)])
    both = jnp.where(
        me_c == 0, jnp.concatenate([mine, theirs]), jnp.concatenate([theirs, mine])
    )
    out_rows = lax.all_gather(both, "z", axis=0, tiled=True)

    sent = jnp.broadcast_to(
        decoded.reshape(ROWS, NX, BLK).transpose(1, 0, 2)[None], (NT, NX, ROWS, BLK)
    ).reshape(NT * NX, ROWS, BLK)
    tokens = lax.all_to_all(sent, ("tp", "x"), split_axis=0, concat_axis=0, tiled=True)

    kv_at = me_t // (NT // KVH) * HD
    shard = jnp.concatenate(
        [
            query_weight,
            lax.dynamic_slice_in_dim(key_weight, kv_at, HD, 1),
            lax.dynamic_slice_in_dim(value_weight, kv_at, HD, 1),
        ],
        axis=1,
    )
    own = lax.all_gather(shard, "z", axis=0, tiled=False)
    other = lax.ppermute(own, "core", [(0, 1), (1, 0)])
    gain = lax.dynamic_slice_in_dim(attn_gain.reshape(NT, NX, BLK), me_x, 1, 1)[:, 0]

    partial_sums = call(
        project_kernel,
        jax.ShapeDtypeStruct((NX, ROWS + EXTRA, PW), bf16),
        [SMEM, VMEM, VMEM, VMEM, VMEM],
        [pltpu.VMEM((NX * ROWS, NT * BLK), bf16), pltpu.VMEM((NT * BLK, PW), bf16)],
        flops=2 * 512 * 1024 * 768,
        name="project",
    )(me_c.reshape(1).astype(jnp.int32), tokens, own, other, gain)
    summands = lax.all_to_all(partial_sums, "x", split_axis=0, concat_axis=0, tiled=True)

    half = jnp.arange(HD // 2, dtype=f32)
    freq = rope_base ** (-(half * 2.0 / HD))
    freq = jnp.concatenate([freq, freq])[None]
    attended = call(
        attend_kernel,
        jax.ShapeDtypeStruct((ROWS, QW), bf16),
        [SMEM, VMEM, VMEM],
        flops=2 * 128 * 128 * 128 * 8,
        name="attend",
    )(lengths, summands, freq)

    slab = lax.all_gather(attended, "x", axis=0, tiled=True)
    products = call(
        output_kernel,
        jax.ShapeDtypeStruct((NT * NX, ROWS, BLK), bf16),
        [VMEM, VMEM],
        flops=2 * 512 * 512 * 1024,
        name="output",
    )(slab, out_rows)
    terms = lax.all_to_all(products, ("tp", "x"), split_axis=0, concat_axis=0, tiled=True)

    placed, stat = call(
        layer_kernel,
        (jax.ShapeDtypeStruct((ROWS, FEAT), bf16), jax.ShapeDtypeStruct((2, BLK), f32)),
        [SMEM, VMEM, VMEM, VMEM, VMEM, VMEM],
        flops=2 * 128 * 128 * 512,
        name="layer",
    )(
        lengths,
        terms,
        decoded,
        destination.reshape(1, ROWS),
        final_gain.reshape(1, FEAT),
        head_weight.reshape(1, FEAT),
    )
    hidden = lax.all_to_all(placed, fsdp, split_axis=0, concat_axis=0, tiled=True)
    stat = lax.psum(stat[:, :RESP], "tp")
    rewards = lax.rsqrt(stat[0] / D + norm_eps) * stat[1]
    return (hidden, rewards)


def solution(mesh):
    grid = Mesh(mesh.devices.reshape(NT, NZ, NX, NC), ("tp", "z", "x", "core"))
    fsdp = ("z", "x", "core")
    return jax.shard_map(
        body,
        mesh=grid,
        in_specs=(
            P(fsdp, "tp"),
            P(fsdp, None),
            P(fsdp, None),
            P(),
            P(fsdp, "tp"),
            P(fsdp, None),
            P(fsdp, None),
            P("tp", fsdp),
            P("tp"),
            P("tp"),
        ),
        out_specs=(P(fsdp, "tp"), P(fsdp)),
        check_vma=False,
    )
```

time: 780 us -> 165 us (0.21)
  the two profiles are of different devices: /device:TPU:1 before, /device:TPU:6 now
where the time goes in v1:
time: 165 us; the launch traced here: 164 us
  blocking collectives  61 us (37%)
  waiting for transfers between devices  38.7 us (23%)
  starting transfers between devices  37 us (22%)
  between operations  14.2 us (9%)
  Pallas kernels  6.69 us (4%)
  local copies, waits for them, and re-layouts  5.56 us (3%)
    all_gather x1, blocking collectives, body(): own = lax.all_gather(shard, 'z', axis=0, tiled=False)  32.8 us
    all_to_all x1, waiting for transfers between devices, body(): lax.all_to_all(products, ('tp', 'x'), split_axis=0, concat_axis=0, tiled=...  23.8 us
    psum x1, blocking collectives, body(): stat = lax.psum(stat[:, :RESP], 'tp')  14.7 us
    all_gather x1, blocking collectives, body(): slab = lax.all_gather(attended, 'x', axis=0, tiled=True)  13.4 us
    all_to_all x1, waiting for transfers between devices, body(): lax.all_to_all(partial_sums, 'x', split_axis=0, concat_axis=0, tiled=True)  11.5 us
    all_to_all x1, starting transfers between devices, body(): lax.all_to_all(sent, ('tp', 'x'), split_axis=0, concat_axis=0, tiled=True)  10.3 us
    all_to_all x1, starting transfers between devices, body(): lax.all_to_all(products, ('tp', 'x'), split_axis=0, concat_axis=0, tiled=...  9.8 us
    all_to_all x1, starting transfers between devices, body(): lax.all_to_all(placed, fsdp, split_axis=0, concat_axis=0, tiled=True)  7.88 us
  transfers between devices with their start and end apart: 7, of which 4 were waited for; matrix products, arithmetic and copies ran while one was open for 1% of the time, Pallas kernels for 2%

profile of v1, /device:TPU:6, one launch (start us, length us, event | category | flops | bytes accessed | tf_op | source)
XLA Modules:
  0.0 164.4 jit_solution(11676082691335173194)
XLA Ops:
  7.2 0.9 reshape.35
  8.2 1.2 broadcast_in_dim.4
  9.4 10.3 %all-to-all-start = ((bf16[32,128,128]{2,1,0:T(8,128)(2,1)}), bf16[32,128,128]{2,1,0:T(8,128)(2,1)S(1)}, u32[]{:S(2)}, u32[]{:S(2)}) async-start(bf16[32,128,128]{2,1,0:T(8,128)(2,1)} %bitcast.2), calls=%async_computation | async-start | bytes 2097152 | tf_op jit(solution)/shard_map/all_to_all | solution.py:209
  19.8 1.9 %collective-permute-start.1 = (bf16[64,512]{1,0:T(8,128)(2,1)S(1)}, bf16[64,512]{1,0:T(8,128)(2,1)S(1)}, u32[]{:S(2)}, u32[]{:S(2)}) collective-permute-start(bf16[64,512]{1,0:T(8,128)(2,1)S(1)} %bitcast.22), channel_id=1, source_target_pairs={{0,1},{1,0},{2,3},{3,2},{4,5},{5,4},{6,7},{7,6},{8,9},{9,8},{10,11... | collective-permute-start | bytes 196616 | tf_op jit(solution)/shard_map/ppermute | solution.py:200
  21.8 1.1 collective-permute-done.1
  22.9 0.7 maximum_select_fusion
  23.6 32.8 %all-gather = bf16[512,768]{1,0:T(8,128)(2,1)S(1)} all-gather(bf16[64,768]{1,0:T(8,128)(2,1)S(1)} %pad_maximum_fusion), channel_id=2, replica_groups=mesh['tp'=8,'z'=8,'x'=4,'core'=2] {'z'}, dimensions={0}, use_global_device_ids=true | all-gather | bytes 884736 | tf_op jit(solution)/shard_map/all_gather | solution.py:220
  56.5 1.9 %collective-permute-start = (bf16[8,64,768]{2,1,0:T(8,128)(2,1)S(1)}, bf16[8,64,768]{2,1,0:T(8,128)(2,1)S(1)}, u32[]{:S(2)}, u32[]{:S(2)}) collective-permute-start(bf16[8,64,768]{2,1,0:T(8,128)(2,1)S(1)} %bitcast.16), channel_id=1, source_target_pairs={{0,1},{1,0},{2,3},{3,2},{4,5},{5,4},{6,7},{7,6},{8,9},{9,8},{10,11... | collective-permute-start | bytes 2359304 | tf_op jit(solution)/shard_map/ppermute | solution.py:221
  58.4 2.2 %collective-permute-done.other_ref = bf16[8,64,768]{2,1,0:T(8,128)(2,1)S(1)} collective-permute-done((bf16[8,64,768]{2,1,0:T(8,128)(2,1)S(1)}, bf16[8,64,768]{2,1,0:T(8,128)(2,1)S(1)}, u32[]{:S(2)}, u32[]{:S(2)}) %collective-permute-start) | collective-permute-done | bytes 786464 | tf_op jit(solution)/shard_map/ppermute | solution.py:221
  60.6 2.1 %project.1 = bf16[4,144,768]{2,1,0:T(8,128)(2,1)} custom-call(s32[1]{0:T(128)} %bitcast.core_ref, bf16[32,128,128]{2,1,0:T(8,128)(2,1)S(1)} %all-to-all-done.x_ref, bf16[8,64,768]{2,1,0:T(8,128)(2,1)S(1)} %bitcast.17, bf16[8,64,768]{2,1,0:T(8,128)(2,1)S(1)} %collective-permute-done.other_ref, bf16[8,128]{1,0:T(8,128)(2,1)S(1)} %bitcast.18), custom_call_target="tpu_custom_call" | custom-call | flops 805306368 | bytes 4194304 | tf_op jit(solution)/shard_map/project/pallas_call | solution.py:224
  62.7 5.1 %all-to-all-start.1 = ((bf16[4,144,768]{2,1,0:T(8,128)(2,1)}), bf16[4,144,768]{2,1,0:T(8,128)(2,1)S(1)}, u32[]{:S(2)}, u32[]{:S(2)}) async-start(bf16[4,144,768]{2,1,0:T(8,128)(2,1)} %project.1), calls=%async_computation.1 | async-start | bytes 1769472 | tf_op jit(solution)/shard_map/all_to_all | solution.py:232
  67.9 11.5 %all-to-all-done.1.parts_ref = bf16[4,144,768]{2,1,0:T(8,128)(2,1)S(1)} async-done(((bf16[4,144,768]{2,1,0:T(8,128)(2,1)}), bf16[4,144,768]{2,1,0:T(8,128)(2,1)S(1)}, u32[]{:S(2)}, u32[]{:S(2)}) %all-to-all-start.1) | async-done | bytes 884768 | tf_op jit(solution)/shard_map/all_to_all | solution.py:232
  79.4 2.0 %attend.1 = bf16[128,512]{1,0:T(8,128)(2,1)S(1)} custom-call(s32[1,8]{1,0:T(1,128)S(1)} %copy-done.3, bf16[4,144,768]{2,1,0:T(8,128)(2,1)S(1)} %all-to-all-done.1.parts_ref, f32[1,128]{1,0:T(1,128)S(1)} %maximum_bitcast_fusion.freq_ref), custom_call_target="tpu_custom_call" | custom-call | flops 33554432 | bytes 4194304 | tf_op jit(solution)/shard_map/attend/pallas_call | solution.py:237
  81.4 13.4 %all_gather.14.x_ref = bf16[512,512]{1,0:T(8,128)(2,1)S(1)} all-gather(bf16[128,512]{1,0:T(8,128)(2,1)S(1)} %attend.1), channel_id=1, replica_groups=mesh['tp'=8,'z'=8,'x'=4,'core'=2] {'x'}, dimensions={0}, use_global_device_ids=true | all-gather | bytes 655360 | tf_op jit(solution)/shard_map/all_gather | solution.py:245
  94.8 1.2 copy-done.1
  96.0 1.7 %output.1 = bf16[32,128,128]{2,1,0:T(8,128)(2,1)} custom-call(bf16[512,512]{1,0:T(8,128)(2,1)S(1)} %all_gather.14.x_ref, bf16[1024,512]{1,0:T(8,128)(2,1)S(1)} %copy-done.1), custom_call_target="tpu_custom_call" | custom-call | flops 536870912 | bytes 4194304 | tf_op jit(solution)/shard_map/output/pallas_call | solution.py:246
  97.8 9.8 %all-to-all-start.2 = ((bf16[32,128,128]{2,1,0:T(8,128)(2,1)}), bf16[32,128,128]{2,1,0:T(8,128)(2,1)S(1)}, u32[]{:S(2)}, u32[]{:S(2)}) async-start(bf16[32,128,128]{2,1,0:T(8,128)(2,1)} %output.1), calls=%async_computation.2 | async-start | bytes 2097152 | tf_op jit(solution)/shard_map/all_to_all | solution.py:253
  107.6 0.7 copy-done.10
  108.3 23.8 %all-to-all-done.2.parts_ref = bf16[32,128,128]{2,1,0:T(8,128)(2,1)S(1)} async-done(((bf16[32,128,128]{2,1,0:T(8,128)(2,1)}), bf16[32,128,128]{2,1,0:T(8,128)(2,1)S(1)}, u32[]{:S(2)}, u32[]{:S(2)}) %all-to-all-start.2) | async-done | bytes 1048608 | tf_op jit(solution)/shard_map/all_to_all | solution.py:253
  132.1 0.9 layer.1
  133.0 0.7 all_to_all.20
  133.7 7.9 %all-to-all-start.3 = ((bf16[64,2,512]{2,1,0:T(2,128)(2,1)}), bf16[64,2,512]{2,1,0:T(2,128)(2,1)S(1)}, u32[]{:S(2)}, u32[]{:S(2)}) async-start(bf16[64,2,512]{2,1,0:T(2,128)(2,1)} %all_to_all.20), calls=%async_computation.3 | async-start | bytes 262144 | tf_op jit(solution)/shard_map/all_to_all | solution.py:269
  141.6 14.7 %psum.7 = f32[2,8]{1,0:T(2,128)S(1)} all-reduce(f32[2,8]{1,0:T(2,128)S(1)} %bitcast.19), channel_id=1, replica_groups=mesh['tp'=8,'z'=8,'x'=4,'core'=2] {'tp'}, use_global_device_ids=true, to_apply=%region_0.1 | all-reduce | flops 16 | bytes 128 | tf_op jit(solution)/shard_map/psum | solution.py:270
  156.9 0.7 all_to_all.22
  (35 shorter events, 0.8 us)
Async XLA Ops:
  7.2 51.2 %copy-start = (bf16[4096]{0:T(1024)(128)(2,1)S(1)}, bf16[4096]{0:T(1024)(128)(2,1)}, u32[]{:S(2)}) copy-start(bf16[4096]{0:T(1024)(128)(2,1)} %param.13) | copy-start | bytes 24580
  9.4 10.4 %copy-start.6 = (bf16[512,64]{0,1:T(8,128)(2,1)S(1)}, bf16[512,64]{0,1:T(8,128)(2,1)}, u32[]{:S(2)}) copy-start(bf16[512,64]{0,1:T(8,128)(2,1)} %param.17) | copy-start | bytes 196612
  9.4 12.4 %copy-start.7 = (bf16[64,256]{1,0:T(8,128)(2,1)S(1)}, bf16[64,256]{1,0:T(8,128)(2,1)}, u32[]{:S(2)}) copy-start(bf16[64,256]{1,0:T(8,128)(2,1)} %param.16) | copy-start | bytes 98308
  9.4 12.4 %copy-start.8 = (bf16[64,256]{1,0:T(8,128)(2,1)S(1)}, bf16[64,256]{1,0:T(8,128)(2,1)}, u32[]{:S(2)}) copy-start(bf16[64,256]{1,0:T(8,128)(2,1)} %param.15) | copy-start | bytes 98308
  9.4 51.3 %all-to-all-start = ((bf16[32,128,128]{2,1,0:T(8,128)(2,1)}), bf16[32,128,128]{2,1,0:T(8,128)(2,1)S(1)}, u32[]{:S(2)}, u32[]{:S(2)}) async-start(bf16[32,128,128]{2,1,0:T(8,128)(2,1)} %bitcast.2), calls=%async_computation | async-start | bytes 2097152 | tf_op jit(solution)/shard_map/all_to_all | solution.py:209
  19.7 2.1 %copy-start.5 = (bf16[64,512]{1,0:T(8,128)(2,1)S(1)}, bf16[64,512]{1,0:T(8,128)(2,1)}, u32[]{:S(2)}) copy-start(bf16[64,512]{1,0:T(8,128)(2,1)} %param.14) | copy-start | bytes 196612
  19.7 75.1 %all-gather.3.cloned.1.call-start = ((), (), s32[]{:S(2)}) async-start(), calls=%async_computation.4 | async-start | bytes 1179648 | tf_op jit(solution)/shard_map/all_gather | solution.py:204
  19.8 3.1 %collective-permute-start.1 = (bf16[64,512]{1,0:T(8,128)(2,1)S(1)}, bf16[64,512]{1,0:T(8,128)(2,1)S(1)}, u32[]{:S(2)}, u32[]{:S(2)}) collective-permute-start(bf16[64,512]{1,0:T(8,128)(2,1)S(1)} %bitcast.22), channel_id=1, source_target_pairs={{0,1},{1,0},{2,3},{3,2},{4,5},{5,4},{6,7},{7,6},{8,9},{9,8},{10,11... | collective-permute-start | bytes 196616 | tf_op jit(solution)/shard_map/ppermute | solution.py:200
  56.5 4.2 %collective-permute-start = (bf16[8,64,768]{2,1,0:T(8,128)(2,1)S(1)}, bf16[8,64,768]{2,1,0:T(8,128)(2,1)S(1)}, u32[]{:S(2)}, u32[]{:S(2)}) collective-permute-start(bf16[8,64,768]{2,1,0:T(8,128)(2,1)S(1)} %bitcast.16), channel_id=1, source_target_pairs={{0,1},{1,0},{2,3},{3,2},{4,5},{5,4},{6,7},{7,6},{8,9},{9,8},{10,11... | collective-permute-start | bytes 2359304 | tf_op jit(solution)/shard_map/ppermute | solution.py:221
  62.7 16.7 %all-to-all-start.1 = ((bf16[4,144,768]{2,1,0:T(8,128)(2,1)}), bf16[4,144,768]{2,1,0:T(8,128)(2,1)S(1)}, u32[]{:S(2)}, u32[]{:S(2)}) async-start(bf16[4,144,768]{2,1,0:T(8,128)(2,1)} %project.1), calls=%async_computation.1 | async-start | bytes 1769472 | tf_op jit(solution)/shard_map/all_to_all | solution.py:232
  67.8 11.6 %copy-start.3 = (s32[1,8]{1,0:T(1,128)S(1)}, s32[1,8]{1,0:T(1,128)}, u32[]{:S(2)}) copy-start(s32[1,8]{1,0:T(1,128)} %lengths_ref.3) | copy-start | bytes 100
  94.8 1.2 copy-start.1
  97.8 9.8 %copy-start.9 = (bf16[512]{0:T(512)(128)(2,1)S(1)}, bf16[512]{0:T(512)(128)(2,1)}, u32[]{:S(2)}) copy-start(bf16[512]{0:T(512)(128)(2,1)} %param.18) | copy-start | bytes 3076
  97.8 34.3 %copy-start.2 = (bf16[128,512]{1,0:T(8,128)(2,1)S(1)}, bf16[128,512]{1,0:T(8,128)(2,1)}, u32[]{:S(2)}) copy-start(bf16[128,512]{1,0:T(8,128)(2,1)} %rows_ref.1) | copy-start | bytes 393220
  97.8 34.3 %all-to-all-start.2 = ((bf16[32,128,128]{2,1,0:T(8,128)(2,1)}), bf16[32,128,128]{2,1,0:T(8,128)(2,1)S(1)}, u32[]{:S(2)}, u32[]{:S(2)}) async-start(bf16[32,128,128]{2,1,0:T(8,128)(2,1)} %output.1), calls=%async_computation.2 | async-start | bytes 2097152 | tf_op jit(solution)/shard_map/all_to_all | solution.py:253
  107.6 0.7 copy-start.10
  108.3 23.8 %copy-start.4 = (s32[128,1]{0,1:T(1,128)S(1)}, s32[128,1]{0,1:T(1,128)}, u32[]{:S(2)}) copy-start(s32[128,1]{0,1:T(1,128)} %param.12) | copy-start | bytes 1540
  133.7 23.2 %all-to-all-start.3 = ((bf16[64,2,512]{2,1,0:T(2,128)(2,1)}), bf16[64,2,512]{2,1,0:T(2,128)(2,1)S(1)}, u32[]{:S(2)}, u32[]{:S(2)}) async-start(bf16[64,2,512]{2,1,0:T(2,128)(2,1)} %all_to_all.20), calls=%async_computation.3 | async-start | bytes 262144 | tf_op jit(solution)/shard_map/all_to_all | solution.py:269
Sparse Core Ops, SparseCore 0:
  23.7 46.5 all-gather.2

commit v2 on v1

--- a/solution.py
+++ b/solution.py
@@ -60,8 +60,11 @@
     return start
 
 
-def project_kernel(core_ref, x_ref, own_ref, other_ref, gain_ref, out_ref, xs_ref, w_ref):
-    first = core_ref[0] == 0
+def project_kernel(
+    place_ref, x_ref, own_ref, other_ref, gain_ref, out0, out1, out2, out3, xs_ref, w_ref
+):
+    first = place_ref[0] == 0
+    outs = (out0, out1, out2, out3)
     for t in range(NT):
         own, other = own_ref[t], other_ref[t]
         w_ref[t * BLK : t * BLK + BLK // 2, :] = jnp.where(first, own, other)
@@ -69,8 +72,9 @@
     eye = eye_mask()
     for g in range(NX):
         square = jnp.zeros((ROWS, BLK), f32)
+        group = lax.rem(place_ref[1] + g, NX)
         for t in range(NT):
-            wide = x_ref[t * NX + g].astype(f32)
+            wide = x_ref[t * NX + group].astype(f32)
             square = square + wide * wide
             xs_ref[g * ROWS : (g + 1) * ROWS, t * BLK : (t + 1) * BLK] = (
                 wide * gain_ref[t : t + 1, :].astype(f32)
@@ -81,21 +85,22 @@
         low = line - high
         which = iota((EXTRA, ROWS), 0)
         tail = jnp.where(which == 0, high, jnp.where(which == 1, low, 0.0)).astype(bf16)
-        out_ref[g, ROWS:, :] = jnp.concatenate(
+        outs[g][ROWS:, :] = jnp.concatenate(
             [tail, jnp.zeros((EXTRA, PW - ROWS), bf16)], axis=1
         )
     for n in range(PW // 256):
         cols = slice(n * 256, (n + 1) * 256)
         part = jnp.dot(xs_ref[...], w_ref[:, cols], preferred_element_type=f32)
         for g in range(NX):
-            out_ref[g, :ROWS, cols] = part[g * ROWS : (g + 1) * ROWS].astype(bf16)
-
-
-def attend_kernel(lengths_ref, parts_ref, freq_ref, out_ref):
+            outs[g][:ROWS, cols] = part[g * ROWS : (g + 1) * ROWS].astype(bf16)
+
+
+def attend_kernel(lengths_ref, part0, part1, part2, part3, freq_ref, out_ref):
+    parts = (part0, part1, part2, part3)
     eye = eye_mask()
     line = jnp.zeros((EXTRA, ROWS), f32)
     for i in range(NX):
-        line = line + parts_ref[i, ROWS:, :ROWS].astype(f32)
+        line = line + parts[i][ROWS:, :ROWS].astype(f32)
     line = jnp.sum(line, axis=0, keepdims=True)
     total = jnp.sum(jnp.where(eye, line, 0.0), axis=1, keepdims=True)
     scale = lax.rsqrt(total * (1.0 / D) + norm_eps)
@@ -110,9 +115,9 @@
     sine = jnp.where(cols < HD // 2, -sine, sine)
 
     def columns(at):
-        summed = parts_ref[0, :ROWS, at : at + HD].astype(f32)
-        for i in range(1, NX):
-            summed = summed + parts_ref[i, :ROWS, at : at + HD].astype(f32)
+        summed = parts[0][:ROWS, at : at + HD].astype(f32)
+        for part in parts[1:]:
+            summed = summed + part[:ROWS, at : at + HD].astype(f32)
         return summed * scale
 
     def rope(v):
@@ -133,11 +138,16 @@
         out_ref[:, h * HD : (h + 1) * HD] = (weighted / sums).astype(bf16)
 
 
-def output_kernel(x_ref, w_ref, out_ref):
+def output_kernel(core_ref, x_ref, own_ref, other_ref, out_ref):
+    first = core_ref[0] == 0
     for n in range(NT // 2):
+        rows = []
+        for z in (2 * n, 2 * n + 1):
+            own, other = own_ref[z], other_ref[z]
+            rows += [jnp.where(first, own, other), jnp.where(first, other, own)]
         part = lax.dot_general(
             x_ref[...],
-            w_ref[n * 2 * BLK : (n + 1) * 2 * BLK, :],
+            jnp.concatenate(rows),
             (((1,), (1,)), ((), ())),
             preferred_element_type=f32,
         )
@@ -196,12 +206,8 @@
     me_t, me_x, me_c = lax.axis_index("tp"), lax.axis_index("x"), lax.axis_index("core")
     fsdp = ("z", "x", "core")
 
-    mine = out_weight.T
-    theirs = lax.ppermute(mine, "core", [(0, 1), (1, 0)])
-    both = jnp.where(
-        me_c == 0, jnp.concatenate([mine, theirs]), jnp.concatenate([theirs, mine])
-    )
-    out_rows = lax.all_gather(both, "z", axis=0, tiled=True)
+    swap = [(0, 1), (1, 0)]
+    core = me_c.reshape(1).astype(jnp.int32)
 
     sent = jnp.broadcast_to(
         decoded.reshape(ROWS, NX, BLK).transpose(1, 0, 2)[None], (NT, NX, ROWS, BLK)
@@ -218,18 +224,26 @@
         axis=1,
     )
     own = lax.all_gather(shard, "z", axis=0, tiled=False)
-    other = lax.ppermute(own, "core", [(0, 1), (1, 0)])
+    other = lax.ppermute(own, "core", swap)
     gain = lax.dynamic_slice_in_dim(attn_gain.reshape(NT, NX, BLK), me_x, 1, 1)[:, 0]
 
-    partial_sums = call(
+    out_sent = jnp.broadcast_to(out_weight.T[None], (NZ,) + out_weight.shape[::-1])
+    out_sent, tokens, own = lax.optimization_barrier((out_sent, tokens, own))
+    out_own = lax.all_to_all(out_sent, "z", split_axis=0, concat_axis=0, tiled=True)
+
+    block = jax.ShapeDtypeStruct((ROWS + EXTRA, PW), bf16)
+    place = jnp.stack([me_c, me_x]).astype(jnp.int32)
+    parts = call(
         project_kernel,
-        jax.ShapeDtypeStruct((NX, ROWS + EXTRA, PW), bf16),
+        (block,) * NX,
         [SMEM, VMEM, VMEM, VMEM, VMEM],
         [pltpu.VMEM((NX * ROWS, NT * BLK), bf16), pltpu.VMEM((NT * BLK, PW), bf16)],
         flops=2 * 512 * 1024 * 768,
         name="project",
-    )(me_c.reshape(1).astype(jnp.int32), tokens, own, other, gain)
-    summands = lax.all_to_all(partial_sums, "x", split_axis=0, concat_axis=0, tiled=True)
+    )(place, tokens, own, other, gain)
+    summands = [parts[0]] + [
+        lax.ppermute(parts[s], "x", [(i, (i + s) % NX) for i in range(NX)]) for s in range(1, NX)
+    ]
 
     half = jnp.arange(HD // 2, dtype=f32)
     freq = rope_base ** (-(half * 2.0 / HD))
@@ -237,19 +251,21 @@
     attended = call(
         attend_kernel,
         jax.ShapeDtypeStruct((ROWS, QW), bf16),
-        [SMEM, VMEM, VMEM],
+        [SMEM] + [VMEM] * (NX + 1),
         flops=2 * 128 * 128 * 128 * 8,
         name="attend",
-    )(lengths, summands, freq)
+    )(lengths, *summands, freq)
+    out_own, attended = lax.optimization_barrier((out_own, attended))
+    out_other = lax.ppermute(out_own, "core", swap)
 
     slab = lax.all_gather(attended, "x", axis=0, tiled=True)
     products = call(
         output_kernel,
         jax.ShapeDtypeStruct((NT * NX, ROWS, BLK), bf16),
-        [VMEM, VMEM],
+        [SMEM, VMEM, VMEM, VMEM],
         flops=2 * 512 * 512 * 1024,
         name="output",
-    )(slab, out_rows)
+    )(core, slab, out_own, out_other)
     terms = lax.all_to_all(products, ("tp", "x"), split_axis=0, concat_axis=0, tiled=True)
 
     placed, stat = call(

time: 165 us -> 157 us (0.952)
  between operations: 14.2 us -> 0.88 us
  starting transfers between devices: 37 us -> 47.8 us
  waiting for transfers between devices: 38.7 us -> 33.5 us
    all_to_all x1, waiting for transfers between devices: 11.5 us -> 0.01 us  [body(): lax.all_to_all(out_sent, 'z', split_axis=0, concat_axis=0, tiled=True)]
    ppermute x2 -> x5, starting transfers between devices: 3.83 us -> 12.5 us  [the longest x3 8.69 us: body(): lax.ppermute(parts[s], 'x', [(i, (i + s) % NX) for i in range(NX)])]
    ppermute x2 -> x5, waiting for transfers between devices: 3.34 us -> 8.82 us  [the longest x3 8.81 us: body(): lax.ppermute(parts[s], 'x', [(i, (i + s) % NX) for i in range(NX)])]
    all_to_all x1, starting transfers between devices: 7.88 us -> 10.8 us  [body(): lax.all_to_all(placed, fsdp, split_axis=0, concat_axis=0, tiled=True)]
  transfers between devices with their start and end apart: 7 -> 9, of which waited for: 4 -> 4; matrix products, arithmetic and copies ran while one was open for 1% -> 1% of each run, Pallas kernels for 2% -> 2%
where the time goes in v2:
time: 157 us; the launch traced here: 156 us
  blocking collectives  60.6 us (39%)
  starting transfers between devices  47.8 us (30%)
  waiting for transfers between devices  33.5 us (21%)
  Pallas kernels  6.32 us (4%)
  local copies, waits for them, and re-layouts  5.98 us (4%)
    all_gather x1, blocking collectives, body(): own = lax.all_gather(shard, 'z', axis=0, tiled=False)  32.6 us
    all_to_all x1, waiting for transfers between devices, body(): lax.all_to_all(products, ('tp', 'x'), split_axis=0, concat_axis=0, tiled=...  24.7 us
    psum x1, blocking collectives, body(): stat = lax.psum(stat[:, :RESP], 'tp')  14.7 us
    all_gather x1, blocking collectives, body(): slab = lax.all_gather(attended, 'x', axis=0, tiled=True)  13.3 us
    all_to_all x1, starting transfers between devices, body(): lax.all_to_all(placed, fsdp, split_axis=0, concat_axis=0, tiled=True)  10.8 us
    all_to_all x1, starting transfers between devices, body(): lax.all_to_all(sent, ('tp', 'x'), split_axis=0, concat_axis=0, tiled=True)  10.3 us
    all_to_all x1, starting transfers between devices, body(): lax.all_to_all(products, ('tp', 'x'), split_axis=0, concat_axis=0, tiled=...  10.1 us
    ppermute x3, waiting for transfers between devices, body(): lax.ppermute(parts[s], 'x', [(i, (i + s) % NX) for i in range(NX)])  8.81 us
  transfers between devices with their start and end apart: 9, of which 4 were waited for; matrix products, arithmetic and copies ran while one was open for 1% of the time, Pallas kernels for 2%

profile of v2, /device:TPU:6, one launch (start us, length us, event | category | flops | bytes accessed | tf_op | source)
XLA Modules:
  0.0 155.7 jit_solution(12231131326828997059)
XLA Ops:
  0.6 0.9 reshape.36
  1.6 1.2 broadcast_in_dim.7
  2.9 10.3 %all-to-all-start = ((bf16[32,128,128]{2,1,0:T(8,128)(2,1)}), bf16[32,128,128]{2,1,0:T(8,128)(2,1)S(1)}, u32[]{:S(2)}, u32[]{:S(2)}) async-start(bf16[32,128,128]{2,1,0:T(8,128)(2,1)} %bitcast.3), calls=%async_computation | async-start | bytes 2097152 | tf_op jit(solution)/shard_map/all_to_all | solution.py:215
  13.3 0.8 copy-done.4
  14.1 32.6 %all-gather = bf16[512,768]{1,0:T(8,128)(2,1)S(1)} all-gather(bf16[64,768]{1,0:T(8,128)(2,1)S(1)} %pad_maximum_fusion), channel_id=2, replica_groups=mesh['tp'=8,'z'=8,'x'=4,'core'=2] {'z'}, dimensions={0}, use_global_device_ids=true | all-gather | bytes 884736 | tf_op jit(solution)/shard_map/all_gather | solution.py:226
  46.6 1.9 %collective-permute-start = (bf16[8,64,768]{2,1,0:T(8,128)(2,1)S(1)}, bf16[8,64,768]{2,1,0:T(8,128)(2,1)S(1)}, u32[]{:S(2)}, u32[]{:S(2)}) collective-permute-start(bf16[8,64,768]{2,1,0:T(8,128)(2,1)S(1)} %bitcast.17), channel_id=1, source_target_pairs={{0,1},{1,0},{2,3},{3,2},{4,5},{5,4},{6,7},{7,6},{8,9},{9,8},{10,11... | collective-permute-start | bytes 2359304 | tf_op jit(solution)/shard_map/ppermute | solution.py:227
  48.5 0.8 broadcast_in_dim.6
  49.4 4.0 %all-to-all-start.1 = ((bf16[8,64,512]{2,1,0:T(8,128)(2,1)}), bf16[8,64,512]{2,1,0:T(8,128)(2,1)S(1)}, u32[]{:S(2)}, u32[]{:S(2)}) async-start(bf16[8,64,512]{2,1,0:T(8,128)(2,1)} %broadcast_in_dim.6), calls=%async_computation.1 | async-start | bytes 1048576 | tf_op jit(solution)/shard_map/all_to_all | solution.py:232
  53.6 1.7 %project.1 = (bf16[144,768]{1,0:T(8,128)(2,1)S(1)}, bf16[144,768]{1,0:T(8,128)(2,1)S(1)}, bf16[144,768]{1,0:T(8,128)(2,1)S(1)}, bf16[144,768]{1,0:T(8,128)(2,1)S(1)}) custom-call(s32[2]{0:T(128)S(1)} %pad_add_fusion.place_ref, bf16[32,128,128]{2,1,0:T(8,128)(2,1)S(1)} %all-to-all-done.x_ref, bf16[8,64,768]{2,1,0:T(8,128)(2,1)S(1)} %bitcast.18, ...), custom_call_target="tpu_custom_call" | custom-call | flops 805306368 | bytes 4194304 | tf_op jit(solution)/shard_map/project/pallas_call | solution.py:236
  55.2 2.1 %collective-permute-start.1 = (bf16[144,768]{1,0:T(8,128)(2,1)S(1)}, bf16[144,768]{1,0:T(8,128)(2,1)S(1)}, u32[]{:S(2)}, u32[]{:S(2)}) collective-permute-start(bf16[144,768]{1,0:T(8,128)(2,1)S(1)} %get-tuple-element.17), channel_id=1, source_target_pairs={{0,2},{2,4},{4,6},{6,0},{1,3},{3,5},{5,7},{7,1},{8,10},{10,12},{12... | collective-permute-start | bytes 663560 | tf_op jit(solution)/shard_map/ppermute | solution.py:245
  57.3 4.7 %collective-permute-start.2 = (bf16[144,768]{1,0:T(8,128)(2,1)S(1)}, bf16[144,768]{1,0:T(8,128)(2,1)S(1)}, u32[]{:S(2)}, u32[]{:S(2)}) collective-permute-start(bf16[144,768]{1,0:T(8,128)(2,1)S(1)} %get-tuple-element.18), channel_id=1, source_target_pairs={{0,4},{2,6},{4,0},{6,2},{1,5},{3,7},{5,1},{7,3},{8,12},{10,14},{12... | collective-permute-start | bytes 663560 | tf_op jit(solution)/shard_map/ppermute | solution.py:245
  62.0 2.0 %collective-permute-start.3 = (bf16[144,768]{1,0:T(8,128)(2,1)S(1)}, bf16[144,768]{1,0:T(8,128)(2,1)S(1)}, u32[]{:S(2)}, u32[]{:S(2)}) collective-permute-start(bf16[144,768]{1,0:T(8,128)(2,1)S(1)} %get-tuple-element.19), channel_id=1, source_target_pairs={{0,6},{2,0},{4,2},{6,4},{1,7},{3,1},{5,3},{7,5},{8,14},{10,8},{12,... | collective-permute-start | bytes 663560 | tf_op jit(solution)/shard_map/ppermute | solution.py:245
  64.0 1.3 collective-permute-done.1.part1
  65.4 3.4 %collective-permute-done.2.part2 = bf16[144,768]{1,0:T(8,128)(2,1)S(1)} collective-permute-done((bf16[144,768]{1,0:T(8,128)(2,1)S(1)}, bf16[144,768]{1,0:T(8,128)(2,1)S(1)}, u32[]{:S(2)}, u32[]{:S(2)}) %collective-permute-start.2) | collective-permute-done | bytes 221216 | tf_op jit(solution)/shard_map/ppermute | solution.py:245
  68.8 4.0 %collective-permute-done.3.part3 = bf16[144,768]{1,0:T(8,128)(2,1)S(1)} collective-permute-done((bf16[144,768]{1,0:T(8,128)(2,1)S(1)}, bf16[144,768]{1,0:T(8,128)(2,1)S(1)}, u32[]{:S(2)}, u32[]{:S(2)}) %collective-permute-start.3) | collective-permute-done | bytes 221216 | tf_op jit(solution)/shard_map/ppermute | solution.py:245
  72.9 2.0 %attend.1 = bf16[128,512]{1,0:T(8,128)(2,1)S(1)} custom-call(s32[1,8]{1,0:T(1,128)S(1)} %copy-done.2, bf16[144,768]{1,0:T(8,128)(2,1)S(1)} %get-tuple-element.16.part0, bf16[144,768]{1,0:T(8,128)(2,1)S(1)} %collective-permute-done.1.part1, bf16[144,768]{1,0:T(8,128)(2,1)S(1)} %collective-permute-done.2.part2, ...), custom_call_target="tpu_custom_call" | custom-call | flops 33554432 | bytes 4194304 | tf_op jit(solution)/shard_map/attend/pallas_call | solution.py:251
  74.9 1.9 %collective-permute-start.4 = (bf16[8,64,512]{2,1,0:T(8,128)(2,1)S(1)}, bf16[8,64,512]{2,1,0:T(8,128)(2,1)S(1)}, u32[]{:S(2)}, u32[]{:S(2)}) collective-permute-start(bf16[8,64,512]{2,1,0:T(8,128)(2,1)S(1)} %all-to-all-done.1.own_ref), channel_id=1, source_target_pairs={{0,1},{1,0},{2,3},{3,2},{4,5},{5,4},{6,7},{7,6},{8,9},{9,8},{10,11... | collective-permute-start | bytes 1572872 | tf_op jit(solution)/shard_map/ppermute | solution.py:259
  76.8 13.3 %all_gather.11.x_ref = bf16[512,512]{1,0:T(8,128)(2,1)S(1)} all-gather(bf16[128,512]{1,0:T(8,128)(2,1)S(1)} %attend.1), channel_id=1, replica_groups=mesh['tp'=8,'z'=8,'x'=4,'core'=2] {'x'}, dimensions={0}, use_global_device_ids=true | all-gather | bytes 655360 | tf_op jit(solution)/shard_map/all_gather | solution.py:261
  90.1 1.7 %output.1 = bf16[32,128,128]{2,1,0:T(8,128)(2,1)} custom-call(s32[1]{0:T(128)} %bitcast.core_ref, bf16[512,512]{1,0:T(8,128)(2,1)S(1)} %all_gather.11.x_ref, bf16[8,64,512]{2,1,0:T(8,128)(2,1)S(1)} %all-to-all-done.1.own_ref, bf16[8,64,512]{2,1,0:T(8,128)(2,1)S(1)} %collective-permute-done.4.other_ref), custom_call_target="tpu_custom_call" | custom-call | flops 536870912 | bytes 4194304 | tf_op jit(solution)/shard_map/output/pallas_call | solution.py:262
  91.8 10.1 %all-to-all-start.2 = ((bf16[32,128,128]{2,1,0:T(8,128)(2,1)}), bf16[32,128,128]{2,1,0:T(8,128)(2,1)S(1)}, u32[]{:S(2)}, u32[]{:S(2)}) async-start(bf16[32,128,128]{2,1,0:T(8,128)(2,1)} %output.1), calls=%async_computation.2 | async-start | bytes 2097152 | tf_op jit(solution)/shard_map/all_to_all | solution.py:269
  102.7 24.7 %all-to-all-done.2.parts_ref = bf16[32,128,128]{2,1,0:T(8,128)(2,1)S(1)} async-done(((bf16[32,128,128]{2,1,0:T(8,128)(2,1)}), bf16[32,128,128]{2,1,0:T(8,128)(2,1)S(1)}, u32[]{:S(2)}, u32[]{:S(2)}) %all-to-all-start.2) | async-done | bytes 1048608 | tf_op jit(solution)/shard_map/all_to_all | solution.py:269
  127.3 0.9 layer.1
  129.0 10.8 %all-to-all-start.3 = ((bf16[64,2,512]{2,1,0:T(2,128)(2,1)}), bf16[64,2,512]{2,1,0:T(2,128)(2,1)S(1)}, u32[]{:S(2)}, u32[]{:S(2)}) async-start(bf16[64,2,512]{2,1,0:T(2,128)(2,1)} %all_to_all.20), calls=%async_computation.3 | async-start | bytes 262144 | tf_op jit(solution)/shard_map/all_to_all | solution.py:285
  139.8 14.7 %psum.7 = f32[2,8]{1,0:T(2,128)S(1)} all-reduce(f32[2,8]{1,0:T(2,128)S(1)} %bitcast.20), channel_id=1, replica_groups=mesh['tp'=8,'z'=8,'x'=4,'core'=2] {'tp'}, use_global_device_ids=true, to_apply=%region_0.1 | all-reduce | flops 16 | bytes 128 | tf_op jit(solution)/shard_map/psum | solution.py:286
  (37 shorter events, 2.9 us)
Async XLA Ops:
  0.6 52.8 %copy-start = (bf16[4096]{0:T(1024)(128)(2,1)S(1)}, bf16[4096]{0:T(1024)(128)(2,1)}, u32[]{:S(2)}) copy-start(bf16[4096]{0:T(1024)(128)(2,1)} %param.13) | copy-start | bytes 24580
  2.9 10.4 %copy-start.6 = (bf16[64,256]{1,0:T(8,128)(2,1)S(1)}, bf16[64,256]{1,0:T(8,128)(2,1)}, u32[]{:S(2)}) copy-start(bf16[64,256]{1,0:T(8,128)(2,1)} %param.16) | copy-start | bytes 98308
  2.9 10.4 %copy-start.7 = (bf16[64,256]{1,0:T(8,128)(2,1)S(1)}, bf16[64,256]{1,0:T(8,128)(2,1)}, u32[]{:S(2)}) copy-start(bf16[64,256]{1,0:T(8,128)(2,1)} %param.15) | copy-start | bytes 98308
  2.9 45.7 %all-to-all-start = ((bf16[32,128,128]{2,1,0:T(8,128)(2,1)}), bf16[32,128,128]{2,1,0:T(8,128)(2,1)S(1)}, u32[]{:S(2)}, u32[]{:S(2)}) async-start(bf16[32,128,128]{2,1,0:T(8,128)(2,1)} %bitcast.3), calls=%async_computation | async-start | bytes 2097152 | tf_op jit(solution)/shard_map/all_to_all | solution.py:215
  13.2 0.8 copy-start.4
  14.0 34.5 %copy-start.5 = (bf16[512,64]{0,1:T(8,128)(2,1)S(1)}, bf16[512,64]{0,1:T(8,128)(2,1)}, u32[]{:S(2)}) copy-start(bf16[512,64]{0,1:T(8,128)(2,1)} %param.17) | copy-start | bytes 196612
  46.6 6.9 %collective-permute-start = (bf16[8,64,768]{2,1,0:T(8,128)(2,1)S(1)}, bf16[8,64,768]{2,1,0:T(8,128)(2,1)S(1)}, u32[]{:S(2)}, u32[]{:S(2)}) collective-permute-start(bf16[8,64,768]{2,1,0:T(8,128)(2,1)S(1)} %bitcast.17), channel_id=1, source_target_pairs={{0,1},{1,0},{2,3},{3,2},{4,5},{5,4},{6,7},{7,6},{8,9},{9,8},{10,11... | collective-permute-start | bytes 2359304 | tf_op jit(solution)/shard_map/ppermute | solution.py:227
  49.4 25.5 %all-to-all-start.1 = ((bf16[8,64,512]{2,1,0:T(8,128)(2,1)}), bf16[8,64,512]{2,1,0:T(8,128)(2,1)S(1)}, u32[]{:S(2)}, u32[]{:S(2)}) async-start(bf16[8,64,512]{2,1,0:T(8,128)(2,1)} %broadcast_in_dim.6), calls=%async_computation.1 | async-start | bytes 1048576 | tf_op jit(solution)/shard_map/all_to_all | solution.py:232
  55.2 10.2 %collective-permute-start.1 = (bf16[144,768]{1,0:T(8,128)(2,1)S(1)}, bf16[144,768]{1,0:T(8,128)(2,1)S(1)}, u32[]{:S(2)}, u32[]{:S(2)}) collective-permute-start(bf16[144,768]{1,0:T(8,128)(2,1)S(1)} %get-tuple-element.17), channel_id=1, source_target_pairs={{0,2},{2,4},{4,6},{6,0},{1,3},{3,5},{5,7},{7,1},{8,10},{10,12},{12... | collective-permute-start | bytes 663560 | tf_op jit(solution)/shard_map/ppermute | solution.py:245
  57.3 11.5 %collective-permute-start.2 = (bf16[144,768]{1,0:T(8,128)(2,1)S(1)}, bf16[144,768]{1,0:T(8,128)(2,1)S(1)}, u32[]{:S(2)}, u32[]{:S(2)}) collective-permute-start(bf16[144,768]{1,0:T(8,128)(2,1)S(1)} %get-tuple-element.18), channel_id=1, source_target_pairs={{0,4},{2,6},{4,0},{6,2},{1,5},{3,7},{5,1},{7,3},{8,12},{10,14},{12... | collective-permute-start | bytes 663560 | tf_op jit(solution)/shard_map/ppermute | solution.py:245
  62.0 10.9 %collective-permute-start.3 = (bf16[144,768]{1,0:T(8,128)(2,1)S(1)}, bf16[144,768]{1,0:T(8,128)(2,1)S(1)}, u32[]{:S(2)}, u32[]{:S(2)}) collective-permute-start(bf16[144,768]{1,0:T(8,128)(2,1)S(1)} %get-tuple-element.19), channel_id=1, source_target_pairs={{0,6},{2,0},{4,2},{6,4},{1,7},{3,1},{5,3},{7,5},{8,14},{10,8},{12,... | collective-permute-start | bytes 663560 | tf_op jit(solution)/shard_map/ppermute | solution.py:245
  64.0 8.8 %copy-start.2 = (s32[1,8]{1,0:T(1,128)S(1)}, s32[1,8]{1,0:T(1,128)}, u32[]{:S(2)}) copy-start(s32[1,8]{1,0:T(1,128)} %lengths_ref.3) | copy-start | bytes 100
  74.9 15.2 %collective-permute-start.4 = (bf16[8,64,512]{2,1,0:T(8,128)(2,1)S(1)}, bf16[8,64,512]{2,1,0:T(8,128)(2,1)S(1)}, u32[]{:S(2)}, u32[]{:S(2)}) collective-permute-start(bf16[8,64,512]{2,1,0:T(8,128)(2,1)S(1)} %all-to-all-done.1.own_ref), channel_id=1, source_target_pairs={{0,1},{1,0},{2,3},{3,2},{4,5},{5,4},{6,7},{7,6},{8,9},{9,8},{10,11... | collective-permute-start | bytes 1572872 | tf_op jit(solution)/shard_map/ppermute | solution.py:259
  91.8 10.1 %copy-start.8 = (bf16[512]{0:T(512)(128)(2,1)S(1)}, bf16[512]{0:T(512)(128)(2,1)}, u32[]{:S(2)}) copy-start(bf16[512]{0:T(512)(128)(2,1)} %param.18) | copy-start | bytes 3076
  91.8 35.5 %copy-start.1 = (bf16[128,512]{1,0:T(8,128)(2,1)S(1)}, bf16[128,512]{1,0:T(8,128)(2,1)}, u32[]{:S(2)}) copy-start(bf16[128,512]{1,0:T(8,128)(2,1)} %rows_ref.1) | copy-start | bytes 393220
  91.8 35.5 %all-to-all-start.2 = ((bf16[32,128,128]{2,1,0:T(8,128)(2,1)}), bf16[32,128,128]{2,1,0:T(8,128)(2,1)S(1)}, u32[]{:S(2)}, u32[]{:S(2)}) async-start(bf16[32,128,128]{2,1,0:T(8,128)(2,1)} %output.1), calls=%async_computation.2 | async-start | bytes 2097152 | tf_op jit(solution)/shard_map/all_to_all | solution.py:269
  102.0 0.7 copy-start.9
  102.7 24.7 %copy-start.3 = (s32[128,1]{0,1:T(1,128)S(1)}, s32[128,1]{0,1:T(1,128)}, u32[]{:S(2)}) copy-start(s32[128,1]{0,1:T(1,128)} %param.12) | copy-start | bytes 1540
  129.0 26.1 %all-to-all-start.3 = ((bf16[64,2,512]{2,1,0:T(2,128)(2,1)}), bf16[64,2,512]{2,1,0:T(2,128)(2,1)S(1)}, u32[]{:S(2)}, u32[]{:S(2)}) async-start(bf16[64,2,512]{2,1,0:T(2,128)(2,1)} %all_to_all.20), calls=%async_computation.3 | async-start | bytes 262144 | tf_op jit(solution)/shard_map/all_to_all | solution.py:285

commit v3 on v2

v3 whole, which is shorter than its diff:
```python
import jax
import jax.numpy as jnp
from jax import lax
from jax.experimental import pallas as pl
from jax.experimental.pallas import tpu as pltpu
from jax.sharding import Mesh, PartitionSpec as P

D = 4096
HD = 128
QH = 32
KVH = 2
NT, NZ, NX, NC = 8, 8, 4, 2
NQ, NB = 4, 2
TP = ("quad", "pair")
FSDP = ("z", "x", "core")
ORDER = (6, 3, 1, 2, 4, 7, 5, 0)
AT = tuple(ORDER.index(t) for t in range(NT))
ROWS = 128
FEAT = D // NT
BLK = 128
QW = QH * HD // NT
PW = QW + 2 * HD
HEADS = QW // HD
EXTRA = 16
RESP = 8
CAP = 2

norm_eps = 1e-06
rope_base = 1000000.0
neg_fill = -1e30

bf16 = jnp.bfloat16
f32 = jnp.float32

VMEM = pl.BlockSpec(memory_space=pltpu.VMEM)
ANY = pl.BlockSpec(memory_space=pl.ANY)
SMEM = pl.BlockSpec(memory_space=pltpu.SMEM)


def call(kernel, out_shape, in_specs, scratch=(), flops=0, name=None, vmem=24):
    return pl.pallas_call(
        kernel,
        out_shape=out_shape,
        in_specs=in_specs,
        out_specs=jax.tree.map(lambda _: VMEM, out_shape),
        scratch_shapes=list(scratch),
        compiler_params=pltpu.CompilerParams(vmem_limit_bytes=vmem * 1024 * 1024),
        cost_estimate=pl.CostEstimate(flops=flops, bytes_accessed=4 << 20, transcendentals=0),
        name=name,
    )


def iota(shape, axis):
    return lax.broadcasted_iota(jnp.int32, shape, axis)


def eye_mask():
    return iota((ROWS, ROWS), 0) == iota((ROWS, ROWS), 1)


def resp_starts(lengths_ref, rows):
    end = jnp.int32(0)
    start = jnp.zeros_like(rows)
    for j in range(RESP):
        end = end + lengths_ref[0, j]
        start = jnp.where(rows >= end, end, start)
    return start


def prepare_kernel(
    rows, query, key, value, out_w, sent, shard, out_sent, rows_ref, query_ref, kv_ref, out_ref, sems
):
    head = pl.ds(pl.multiple_of(lax.axis_index(TP) // (NT // KVH) * HD, HD), HD)
    moves = (
        (rows, rows_ref),
        (query, query_ref),
        (key.at[:, head], kv_ref.at[0]),
        (value.at[:, head], kv_ref.at[1]),
        (out_w, out_ref),
    )
    copies = [pltpu.make_async_copy(m[0], m[1], sems.at[i]) for i, m in enumerate(moves)]
    for copy in copies:
        copy.start()
    copies[0].wait()
    for g in range(NX):
        block = rows_ref[:, g * BLK : (g + 1) * BLK]
        for t in range(NT):
            sent[t * NX + g] = block
    for copy in copies[1:]:
        copy.wait()
    shard[:, :QW] = query_ref[...]
    shard[:, QW : QW + HD] = kv_ref[0]
    shard[:, QW + HD :] = kv_ref[1]
    for z in range(NZ):
        out_sent[z] = out_ref[...]


def table_kernel(lengths_ref, freq_ref, line_ref, cosine_ref, sine_ref, order_ref):
    rows = iota((ROWS, ROWS), 0)
    cols = iota((ROWS, ROWS), 1)
    angles = (rows - resp_starts(lengths_ref, rows)).astype(f32) * freq_ref[...]
    sine = jnp.sin(angles)
    cosine_ref[...] = jnp.cos(angles)
    sine_ref[...] = jnp.where(cols < HD // 2, -sine, sine)
    dest_line = line_ref[...]
    dest_column = jnp.sum(jnp.where(rows == cols, dest_line, 0), axis=1, keepdims=True)
    same = (dest_column == dest_line) & (rows < cols)
    rank = jnp.sum(same.astype(jnp.int32), axis=0, keepdims=True)
    order_ref[...] = (rows == CAP * dest_line + rank).astype(f32).astype(bf16)


def project_kernel(
    x_ref, own_ref, other_ref, gain_ref, out0, out1, out2, out3, xs_ref, w_ref
):
    first = lax.axis_index("core") == 0
    outs = (out0, out1, out2, out3)
    for t in range(NT):
        own, other = own_ref[t], other_ref[t]
        w_ref[t * BLK : t * BLK + BLK // 2, :] = jnp.where(first, own, other)
        w_ref[t * BLK + BLK // 2 : (t + 1) * BLK, :] = jnp.where(first, other, own)
    eye = eye_mask()
    for g in range(NX):
        square = jnp.zeros((ROWS, BLK), f32)
        group = lax.rem(lax.axis_index("x") + g, NX)
        for t in range(NT):
            wide = x_ref[AT[t] * NX + group].astype(f32)
            square = square + wide * wide
            xs_ref[g * ROWS : (g + 1) * ROWS, t * BLK : (t + 1) * BLK] = (
                wide * gain_ref[t : t + 1, :].astype(f32)
            ).astype(bf16)
        total = jnp.sum(square, axis=1, keepdims=True)
        line = jnp.sum(jnp.where(eye, total, 0.0), axis=0, keepdims=True)
        high = line.astype(bf16).astype(f32)
        low = line - high
        which = iota((EXTRA, ROWS), 0)
        tail = jnp.where(which == 0, high, jnp.where(which == 1, low, 0.0)).astype(bf16)
        outs[g][PW:, :] = tail
    for n in range(PW // 256):
        cols = slice(n * 256, (n + 1) * 256)
        part = jnp.dot(xs_ref[...], w_ref[:, cols], preferred_element_type=f32)
        for g in range(NX):
            rows = part[g * ROWS : (g + 1) * ROWS].astype(bf16)
            outs[g][n * 256 : n * 256 + ROWS, :] = rows[:, :HD]
            outs[g][n * 256 + ROWS : (n + 1) * 256, :] = rows[:, HD:]


def attend_kernel(lengths_ref, part0, part1, part2, part3, cosine_ref, sine_ref, out_ref):
    parts = (part0, part1, part2, part3)
    eye = eye_mask()
    line = jnp.zeros((EXTRA, ROWS), f32)
    for i in range(NX):
        line = line + parts[i][PW:, :].astype(f32)
    line = jnp.sum(line, axis=0, keepdims=True)
    total = jnp.sum(jnp.where(eye, line, 0.0), axis=1, keepdims=True)
    scale = lax.rsqrt(total * (1.0 / D) + norm_eps)

    rows = iota((ROWS, ROWS), 0)
    cols = iota((ROWS, ROWS), 1)
    start = resp_starts(lengths_ref, rows)
    allowed = (cols >= start) & (cols <= rows)
    cosine, sine = cosine_ref[...], sine_ref[...]

    def columns(at):
        summed = parts[0][at : at + HD, :].astype(f32)
        for part in parts[1:]:
            summed = summed + part[at : at + HD, :].astype(f32)
        return summed * scale

    def rope(v):
        return (v * cosine + pltpu.roll(v, HD // 2, 1) * sine).astype(bf16)

    keys = rope(columns(QW))
    values = columns(QW + HD).astype(bf16)
    for h in range(HEADS):
        queries = rope(columns(h * HD))
        scores = lax.dot_general(
            queries, keys, (((1,), (1,)), ((), ())), preferred_element_type=f32
        ) * (HD**-0.5)
        scores = jnp.where(allowed, scores, neg_fill)
        top = jnp.max(scores, axis=1, keepdims=True)
        probs = jnp.where(allowed, jnp.exp(scores - top), 0.0)
        sums = jnp.sum(probs, axis=1, keepdims=True)
        weighted = jnp.dot(probs.astype(bf16), values, preferred_element_type=f32)
        out_ref[:, h * HD : (h + 1) * HD] = (weighted / sums).astype(bf16)


def output_kernel(x_ref, own_ref, other_ref, out_ref):
    first = lax.axis_index("core") == 0
    for n in range(NT // 2):
        rows = []
        for z in (2 * n, 2 * n + 1):
            own, other = own_ref[z], other_ref[z]
            rows += [jnp.where(first, own, other), jnp.where(first, other, own)]
        part = lax.dot_general(
            x_ref[...],
            jnp.concatenate(rows),
            (((1,), (1,)), ((), ())),
            preferred_element_type=f32,
        )
        for g in range(NX):
            rows = part[g * ROWS : (g + 1) * ROWS].astype(bf16)
            out_ref[AT[2 * n] * NX + g] = rows[:, :BLK]
            out_ref[AT[2 * n + 1] * NX + g] = rows[:, BLK:]


def layer_kernel(
    lengths_ref, parts_ref, rows_ref, order_ref, final_ref, head_ref, out_ref, stat_ref
):
    square = jnp.zeros((ROWS, BLK), f32)
    product = jnp.zeros((ROWS, BLK), f32)
    for g in range(NX):
        cols = slice(g * BLK, (g + 1) * BLK)
        update = parts_ref[g].astype(f32)
        for t in range(1, NT):
            update = update + parts_ref[t * NX + g].astype(f32)
        layer = (rows_ref[:, cols].astype(f32) + update).astype(bf16)
        wide = layer.astype(f32)
        square = square + wide * wide
        product = product + wide * final_ref[:, cols].astype(f32) * head_ref[:, cols].astype(f32)
        out_ref[:, cols] = jnp.dot(order_ref[...], layer, preferred_element_type=f32).astype(bf16)

    lane = iota((1, BLK), 1)
    last = jnp.full((1, BLK), -1, jnp.int32)
    end = jnp.int32(0)
    for j in range(RESP):
        end = end + lengths_ref[0, j]
        last = jnp.where(lane == j, end - 1, last)
    pick = iota((ROWS, BLK), 0) == last
    for at, part in ((0, square), (1, product)):
        column = jnp.sum(part, axis=1, keepdims=True)
        stat_ref[at : at + 1, :] = jnp.sum(jnp.where(pick, column, 0.0), axis=0, keepdims=True)


def exchange(blocks):
    return lax.all_to_all(
        blocks,
        TP + ("x",),
        split_axis=0,
        concat_axis=0,
        tiled=True,
        axis_index_groups=[[t * NX + g for t in ORDER for g in range(NX)]],
    )


def body(
    decoded,
    lengths,
    destination,
    attn_gain,
    query_weight,
    key_weight,
    value_weight,
    out_weight,
    final_gain,
    head_weight,
):
    me_x = lax.axis_index("x")
    swap = [(0, 1), (1, 0)]

    sent, shard, out_sent = call(
        prepare_kernel,
        (
            jax.ShapeDtypeStruct((NT * NX, ROWS, BLK), bf16),
            jax.ShapeDtypeStruct((D // (NZ * NX * NC), PW), bf16),
            jax.ShapeDtypeStruct((NZ, D // (NZ * NX * NC), QW), bf16),
        ),
        [ANY] * 5,
        [
            pltpu.VMEM((ROWS, FEAT), bf16),
            pltpu.VMEM((D // (NZ * NX * NC), QW), bf16),
            pltpu.VMEM((2, D // (NZ * NX * NC), HD), bf16),
            pltpu.VMEM((D // (NZ * NX * NC), QW), bf16),
            pltpu.SemaphoreType.DMA((5,)),
        ],
        name="prepare",
        vmem=60,
    )(decoded, query_weight, key_weight, value_weight, out_weight.T)
    tokens = exchange(sent)
    own = lax.all_gather(shard, "z", axis=0, tiled=False)
    other = lax.ppermute(own, "core", swap)
    gain = lax.dynamic_slice_in_dim(attn_gain.reshape(NT, NX, BLK), me_x, 1, 1)[:, 0]

    out_sent, tokens, own = lax.optimization_barrier((out_sent, tokens, own))
    out_own = lax.all_to_all(out_sent, "z", split_axis=0, concat_axis=0, tiled=True)

    block = jax.ShapeDtypeStruct((PW + EXTRA, HD), bf16)
    parts = call(
        project_kernel,
        (block,) * NX,
        [VMEM] * 4,
        [pltpu.VMEM((NX * ROWS, NT * BLK), bf16), pltpu.VMEM((NT * BLK, PW), bf16)],
        flops=2 * 512 * 1024 * 768,
        name="project",
    )(tokens, own, other, gain)
    summands = [parts[0]] + [
        lax.ppermute(parts[s], "x", [(i, (i + s) % NX) for i in range(NX)]) for s in range(1, NX)
    ]

    half = jnp.arange(HD // 2, dtype=f32)
    freq = rope_base ** (-(half * 2.0 / HD))
    freq = jnp.concatenate([freq, freq])[None]
    own_part, after, line = lax.optimization_barrier(
        (summands[0], lengths, destination.reshape(1, ROWS))
    )
    cosine, sine, order = call(
        table_kernel,
        (jax.ShapeDtypeStruct((ROWS, HD), f32),) * 2 + (jax.ShapeDtypeStruct((ROWS, ROWS), bf16),),
        [SMEM, VMEM, VMEM],
        name="tables",
    )(after, freq, line)
    attended = call(
        attend_kernel,
        jax.ShapeDtypeStruct((ROWS, QW), bf16),
        [SMEM] + [VMEM] * (NX + 2),
        flops=2 * 128 * 128 * 128 * 8,
        name="attend",
    )(lengths, own_part, *summands[1:], cosine, sine)
    out_own, attended = lax.optimization_barrier((out_own, attended))
    out_other = lax.ppermute(out_own, "core", swap)

    slab = lax.all_gather(attended, "x", axis=0, tiled=True)
    products = call(
        output_kernel,
        jax.ShapeDtypeStruct((NT * NX, ROWS, BLK), bf16),
        [VMEM] * 3,
        flops=2 * 512 * 512 * 1024,
        name="output",
    )(slab, out_own, out_other)
    terms = exchange(products)

    placed, stat = call(
        layer_kernel,
        (
            jax.ShapeDtypeStruct((ROWS, FEAT), bf16),
            jax.ShapeDtypeStruct((2, BLK), f32),
        ),
        [SMEM] + [VMEM] * 5,
        flops=2 * 128 * 128 * 512,
        name="layer",
    )(
        lengths,
        terms,
        decoded,
        order,
        final_gain.reshape(1, FEAT),
        head_weight.reshape(1, FEAT),
    )
    hidden = lax.all_to_all(placed, FSDP, split_axis=0, concat_axis=0, tiled=True)
    stat = lax.psum(stat[:, :RESP], TP)
    rewards = lax.rsqrt(stat[0] / D + norm_eps) * stat[1]
    return (hidden, rewards)


def solution(mesh):
    grid = Mesh(mesh.devices.reshape(NQ, NB, NZ, NX, NC), TP + FSDP)
    return jax.shard_map(
        body,
        mesh=grid,
        in_specs=(
            P(FSDP, TP),
            P(FSDP, None),
            P(FSDP, None),
            P(),
            P(FSDP, TP),
            P(FSDP, None),
            P(FSDP, None),
            P(TP, FSDP),
            P(TP),
            P(TP),
        ),
        out_specs=(P(FSDP, TP), P(FSDP)),
        check_vma=False,
    )
```

time: 157 us -> 151 us (0.962)
  waiting for transfers between devices: 33.5 us -> 27.6 us
  local copies, waits for them, and re-layouts: 5.98 us -> 2.8 us
  Pallas kernels: 6.32 us -> 8.73 us
    all_to_all x3, waiting for transfers between devices: 24.7 us -> 20.9 us  [the longest x2 20.9 us: exchange(): lax.all_to_all(blocks, TP + ('x',), split_axis=0, concat_axis=0, tiled=Tr...]
    pallas_call x2 -> x4, Pallas kernels: 3.42 us -> 6.06 us  [the longest x1 2.27 us: body(): call(prepare_kernel, (jax.ShapeDtypeStruct((NT * NX, ROWS, BLK), bf16), j...]
    ppermute x3, waiting for transfers between devices: 8.81 us -> 6.63 us  [body(): lax.ppermute(parts[s], 'x', [(i, (i + s) % NX) for i in range(NX)])]
    broadcast_in_dim x2 -> x0, local copies, waits for them, and re-layouts: 2.08 us -> none  [the longest x1 1.23 us: body(): jnp.broadcast_to(decoded.reshape(ROWS, NX, BLK).transpose(1, 0, 2)[None],...]
    psum x1, blocking collectives: 14.7 us -> 16.5 us  [body(): stat = lax.psum(stat[:, :RESP], TP)]
  transfers between devices with their start and end apart: 9 -> 9, of which waited for: 4 -> 3; matrix products, arithmetic and copies ran while one was open for 1% -> 0% of each run, Pallas kernels for 2% -> 3%
where the time goes in v3:
time: 151 us
  blocking collectives  61.7 us (41%)
  starting transfers between devices  48.3 us (32%)
  waiting for transfers between devices  27.6 us (18%)
  Pallas kernels  8.73 us (6%)
  local copies, waits for them, and re-layouts  2.8 us (2%)
    all_gather x1, blocking collectives, body(): own = lax.all_gather(shard, 'z', axis=0, tiled=False)  31.8 us
    all_to_all x2, waiting for transfers between devices, exchange(): lax.all_to_all(blocks, TP + ('x',), split_axis=0, concat_axis=0, tiled=Tr...  20.9 us
    all_to_all x2, starting transfers between devices, exchange(): lax.all_to_all(blocks, TP + ('x',), split_axis=0, concat_axis=0, tiled=Tr...  20.7 us
    psum x1, blocking collectives, body(): stat = lax.psum(stat[:, :RESP], TP)  16.5 us
    all_gather x1, blocking collectives, body(): slab = lax.all_gather(attended, 'x', axis=0, tiled=True)  13.5 us
    all_to_all x1, starting transfers between devices, body(): lax.all_to_all(placed, FSDP, split_axis=0, concat_axis=0, tiled=True)  11.1 us
    ppermute x3, starting transfers between devices, body(): lax.ppermute(parts[s], 'x', [(i, (i + s) % NX) for i in range(NX)])  8.65 us
    ppermute x3, waiting for transfers between devices, body(): lax.ppermute(parts[s], 'x', [(i, (i + s) % NX) for i in range(NX)])  6.63 us
  transfers between devices with their start and end apart: 9, of which 3 were waited for; matrix products, arithmetic and copies ran while one was open for 0% of the time, Pallas kernels for 3%

profile of v3, /device:TPU:6, one launch (start us, length us, event | category | flops | bytes accessed | tf_op | source)
XLA Modules:
  0.0 150.6 jit_solution(3026970513080683968)
XLA Ops:
  0.6 2.3 %prepare.1 = (bf16[32,128,128]{2,1,0:T(8,128)(2,1)}, bf16[64,768]{1,0:T(8,128)(2,1)}, bf16[8,64,512]{2,1,0:T(8,128)(2,1)}) custom-call(bf16[128,512]{1,0:T(8,128)(2,1)} %rows_ref.1, bf16[64,512]{1,0:T(8,128)(2,1)} %query.1, bf16[64,256]{1,0:T(8,128)(2,1)} %key.1, bf16[64,256]{1,0:T(8,128)(2,1)} %value.1, bf16[64,512]{1,0:T(8,128)(2,1)} %bitcast.18), custom_call_target="tpu_custom_call" | custom-call | bytes 4194304 | tf_op jit(solution)/shard_map/prepare/pallas_call | solution.py:260
  2.9 11.1 %all-to-all-start = ((bf16[32,128,128]{2,1,0:T(8,128)(2,1)}), bf16[32,128,128]{2,1,0:T(8,128)(2,1)S(1)}, u32[]{:S(2)}, u32[]{:S(2)}) async-start(bf16[32,128,128]{2,1,0:T(8,128)(2,1)} %get-tuple-element.23), calls=%async_computation | async-start | bytes 2097152 | tf_op jit(solution)/shard_map/all_to_all | solution.py:235
  14.0 31.8 %all-gather = bf16[512,768]{1,0:T(8,128)(2,1)S(1)} all-gather(bf16[64,768]{1,0:T(8,128)(2,1)S(1)} %copy-done.4), channel_id=2, replica_groups=mesh['quad'=4,'pair'=2,'z'=8,'x'=4,'core'=2] {'z'}, dimensions={0}, use_global_device_ids=true | all-gather | bytes 884736 | tf_op jit(solution)/shard_map/all_gather | solution.py:279
  45.8 1.9 %collective-permute-start = (bf16[8,64,768]{2,1,0:T(8,128)(2,1)S(1)}, bf16[8,64,768]{2,1,0:T(8,128)(2,1)S(1)}, u32[]{:S(2)}, u32[]{:S(2)}) collective-permute-start(bf16[8,64,768]{2,1,0:T(8,128)(2,1)S(1)} %bitcast.13), channel_id=1, source_target_pairs={{0,1},{1,0},{2,3},{3,2},{4,5},{5,4},{6,7},{7,6},{8,9},{9,8},{10,11... | collective-permute-start | bytes 2359304 | tf_op jit(solution)/shard_map/ppermute | solution.py:280
  47.7 4.1 %all-to-all-start.1 = ((bf16[8,64,512]{2,1,0:T(8,128)(2,1)}), bf16[8,64,512]{2,1,0:T(8,128)(2,1)S(1)}, u32[]{:S(2)}, u32[]{:S(2)}) async-start(bf16[8,64,512]{2,1,0:T(8,128)(2,1)} %get-tuple-element.25), calls=%async_computation.1 | async-start | bytes 1048576 | tf_op jit(solution)/shard_map/all_to_all | solution.py:284
  51.8 1.1 project.1
  53.0 2.4 %collective-permute-start.1 = (bf16[784,128]{1,0:T(8,128)(2,1)S(1)}, bf16[784,128]{1,0:T(8,128)(2,1)S(1)}, u32[]{:S(2)}, u32[]{:S(2)}) collective-permute-start(bf16[784,128]{1,0:T(8,128)(2,1)S(1)} %get-tuple-element.30), channel_id=1, source_target_pairs={{0,2},{2,4},{4,6},{6,0},{1,3},{3,5},{5,7},{7,1},{8,10},{10,12},{12... | collective-permute-start | bytes 602120 | tf_op jit(solution)/shard_map/ppermute | solution.py:296
  55.5 4.3 %collective-permute-start.2 = (bf16[784,128]{1,0:T(8,128)(2,1)S(1)}, bf16[784,128]{1,0:T(8,128)(2,1)S(1)}, u32[]{:S(2)}, u32[]{:S(2)}) collective-permute-start(bf16[784,128]{1,0:T(8,128)(2,1)S(1)} %get-tuple-element.31), channel_id=1, source_target_pairs={{0,4},{2,6},{4,0},{6,2},{1,5},{3,7},{5,1},{7,3},{8,12},{10,14},{12... | collective-permute-start | bytes 602120 | tf_op jit(solution)/shard_map/ppermute | solution.py:296
  59.7 1.9 %collective-permute-start.3 = (bf16[784,128]{1,0:T(8,128)(2,1)S(1)}, bf16[784,128]{1,0:T(8,128)(2,1)S(1)}, u32[]{:S(2)}, u32[]{:S(2)}) collective-permute-start(bf16[784,128]{1,0:T(8,128)(2,1)S(1)} %get-tuple-element.32), channel_id=1, source_target_pairs={{0,6},{2,0},{4,2},{6,4},{1,7},{3,1},{5,3},{7,5},{8,14},{10,8},{12,... | collective-permute-start | bytes 602120 | tf_op jit(solution)/shard_map/ppermute | solution.py:296
  62.4 0.9 tables.1
  63.4 2.8 %collective-permute-done.2.part2 = bf16[784,128]{1,0:T(8,128)(2,1)S(1)} collective-permute-done((bf16[784,128]{1,0:T(8,128)(2,1)S(1)}, bf16[784,128]{1,0:T(8,128)(2,1)S(1)}, u32[]{:S(2)}, u32[]{:S(2)}) %collective-permute-start.2) | collective-permute-done | bytes 200736 | tf_op jit(solution)/shard_map/ppermute | solution.py:296
  66.2 3.8 %collective-permute-done.3.part3 = bf16[784,128]{1,0:T(8,128)(2,1)S(1)} collective-permute-done((bf16[784,128]{1,0:T(8,128)(2,1)S(1)}, bf16[784,128]{1,0:T(8,128)(2,1)S(1)}, u32[]{:S(2)}, u32[]{:S(2)}) %collective-permute-start.3) | collective-permute-done | bytes 200736 | tf_op jit(solution)/shard_map/ppermute | solution.py:296
  70.0 1.8 %attend.1 = bf16[128,512]{1,0:T(8,128)(2,1)S(1)} custom-call(s32[1,8]{1,0:T(1,128)S(1)} %copy-done.2, bf16[784,128]{1,0:T(8,128)(2,1)S(1)} %get-tuple-element.29.part0, bf16[784,128]{1,0:T(8,128)(2,1)S(1)} %collective-permute-done.1.part1, bf16[784,128]{1,0:T(8,128)(2,1)S(1)} %collective-permute-done.2.part2, ...), custom_call_target="tpu_custom_call" | custom-call | flops 33554432 | bytes 4194304 | tf_op jit(solution)/shard_map/attend/pallas_call | solution.py:311
  71.8 1.9 %collective-permute-start.4 = (bf16[8,64,512]{2,1,0:T(8,128)(2,1)S(1)}, bf16[8,64,512]{2,1,0:T(8,128)(2,1)S(1)}, u32[]{:S(2)}, u32[]{:S(2)}) collective-permute-start(bf16[8,64,512]{2,1,0:T(8,128)(2,1)S(1)} %all-to-all-done.1.own_ref), channel_id=1, source_target_pairs={{0,1},{1,0},{2,3},{3,2},{4,5},{5,4},{6,7},{7,6},{8,9},{9,8},{10,11... | collective-permute-start | bytes 1572872 | tf_op jit(solution)/shard_map/ppermute | solution.py:319
  73.8 13.5 %all_gather.11.x_ref = bf16[512,512]{1,0:T(8,128)(2,1)S(1)} all-gather(bf16[128,512]{1,0:T(8,128)(2,1)S(1)} %attend.1), channel_id=1, replica_groups=mesh['quad'=4,'pair'=2,'z'=8,'x'=4,'core'=2] {'x'}, dimensions={0}, use_global_device_ids=true | all-gather | bytes 655360 | tf_op jit(solution)/shard_map/all_gather | solution.py:321
  87.3 1.7 %output.1 = bf16[32,128,128]{2,1,0:T(8,128)(2,1)} custom-call(bf16[512,512]{1,0:T(8,128)(2,1)S(1)} %all_gather.11.x_ref, bf16[8,64,512]{2,1,0:T(8,128)(2,1)S(1)} %all-to-all-done.1.own_ref, bf16[8,64,512]{2,1,0:T(8,128)(2,1)S(1)} %collective-permute-done.4.other_ref), custom_call_target="tpu_custom_call" | custom-call | flops 536870912 | bytes 4194304 | tf_op jit(solution)/shard_map/output/pallas_call | solution.py:322
  89.0 9.6 %all-to-all-start.2 = ((bf16[32,128,128]{2,1,0:T(8,128)(2,1)}), bf16[32,128,128]{2,1,0:T(8,128)(2,1)S(1)}, u32[]{:S(2)}, u32[]{:S(2)}) async-start(bf16[32,128,128]{2,1,0:T(8,128)(2,1)} %output.1), calls=%async_computation.2 | async-start | bytes 2097152 | tf_op jit(solution)/shard_map/all_to_all | solution.py:235
  98.7 0.7 copy-done.6
  99.3 20.9 %all-to-all-done.2.parts_ref = bf16[32,128,128]{2,1,0:T(8,128)(2,1)S(1)} async-done(((bf16[32,128,128]{2,1,0:T(8,128)(2,1)}), bf16[32,128,128]{2,1,0:T(8,128)(2,1)S(1)}, u32[]{:S(2)}, u32[]{:S(2)}) %all-to-all-start.2) | async-done | bytes 1048608 | tf_op jit(solution)/shard_map/all_to_all | solution.py:235
  120.3 0.9 layer.1
  121.1 0.7 all_to_all.20
  121.8 11.1 %all-to-all-start.3 = ((bf16[64,2,512]{2,1,0:T(2,128)(2,1)}), bf16[64,2,512]{2,1,0:T(2,128)(2,1)S(1)}, u32[]{:S(2)}, u32[]{:S(2)}) async-start(bf16[64,2,512]{2,1,0:T(2,128)(2,1)} %all_to_all.20), calls=%async_computation.3 | async-start | bytes 262144 | tf_op jit(solution)/shard_map/all_to_all | solution.py:348
  132.9 16.5 %psum.7 = f32[2,8]{1,0:T(2,128)S(1)} all-reduce(f32[2,8]{1,0:T(2,128)S(1)} %bitcast.16), channel_id=1, replica_groups=mesh['quad'=4,'pair'=2,'z'=8,'x'=4,'core'=2] {'quad','pair'}, use_global_device_ids=true, to_apply=%region_0.0 | all-reduce | flops 16 | bytes 128 | tf_op jit(solution)/shard_map/psum | solution.py:349
  149.9 0.7 all_to_all.22
  (26 shorter events, 1.3 us)
Async XLA Ops:
  0.6 51.2 %copy-start = (bf16[4096]{0:T(1024)(128)(2,1)S(1)}, bf16[4096]{0:T(1024)(128)(2,1)}, u32[]{:S(2)}) copy-start(bf16[4096]{0:T(1024)(128)(2,1)} %param.13) | copy-start | bytes 24580
  2.9 11.1 %copy-start.4 = (bf16[64,768]{1,0:T(8,128)(2,1)S(1)}, bf16[64,768]{1,0:T(8,128)(2,1)}, u32[]{:S(2)}) copy-start(bf16[64,768]{1,0:T(8,128)(2,1)} %get-tuple-element.24) | copy-start | bytes 294916
  2.9 44.8 %all-to-all-start = ((bf16[32,128,128]{2,1,0:T(8,128)(2,1)}), bf16[32,128,128]{2,1,0:T(8,128)(2,1)S(1)}, u32[]{:S(2)}, u32[]{:S(2)}) async-start(bf16[32,128,128]{2,1,0:T(8,128)(2,1)} %get-tuple-element.23), calls=%async_computation | async-start | bytes 2097152 | tf_op jit(solution)/shard_map/all_to_all | solution.py:235
  45.8 6.0 %collective-permute-start = (bf16[8,64,768]{2,1,0:T(8,128)(2,1)S(1)}, bf16[8,64,768]{2,1,0:T(8,128)(2,1)S(1)}, u32[]{:S(2)}, u32[]{:S(2)}) collective-permute-start(bf16[8,64,768]{2,1,0:T(8,128)(2,1)S(1)} %bitcast.13), channel_id=1, source_target_pairs={{0,1},{1,0},{2,3},{3,2},{4,5},{5,4},{6,7},{7,6},{8,9},{9,8},{10,11... | collective-permute-start | bytes 2359304 | tf_op jit(solution)/shard_map/ppermute | solution.py:280
  47.7 24.1 %all-to-all-start.1 = ((bf16[8,64,512]{2,1,0:T(8,128)(2,1)}), bf16[8,64,512]{2,1,0:T(8,128)(2,1)S(1)}, u32[]{:S(2)}, u32[]{:S(2)}) async-start(bf16[8,64,512]{2,1,0:T(8,128)(2,1)} %get-tuple-element.25), calls=%async_computation.1 | async-start | bytes 1048576 | tf_op jit(solution)/shard_map/all_to_all | solution.py:284
  53.0 10.3 %collective-permute-start.1 = (bf16[784,128]{1,0:T(8,128)(2,1)S(1)}, bf16[784,128]{1,0:T(8,128)(2,1)S(1)}, u32[]{:S(2)}, u32[]{:S(2)}) collective-permute-start(bf16[784,128]{1,0:T(8,128)(2,1)S(1)} %get-tuple-element.30), channel_id=1, source_target_pairs={{0,2},{2,4},{4,6},{6,0},{1,3},{3,5},{5,7},{7,1},{8,10},{10,12},{12... | collective-permute-start | bytes 602120 | tf_op jit(solution)/shard_map/ppermute | solution.py:296
  55.5 10.7 %collective-permute-start.2 = (bf16[784,128]{1,0:T(8,128)(2,1)S(1)}, bf16[784,128]{1,0:T(8,128)(2,1)S(1)}, u32[]{:S(2)}, u32[]{:S(2)}) collective-permute-start(bf16[784,128]{1,0:T(8,128)(2,1)S(1)} %get-tuple-element.31), channel_id=1, source_target_pairs={{0,4},{2,6},{4,0},{6,2},{1,5},{3,7},{5,1},{7,3},{8,12},{10,14},{12... | collective-permute-start | bytes 602120 | tf_op jit(solution)/shard_map/ppermute | solution.py:296
  59.7 10.2 %collective-permute-start.3 = (bf16[784,128]{1,0:T(8,128)(2,1)S(1)}, bf16[784,128]{1,0:T(8,128)(2,1)S(1)}, u32[]{:S(2)}, u32[]{:S(2)}) collective-permute-start(bf16[784,128]{1,0:T(8,128)(2,1)S(1)} %get-tuple-element.32), channel_id=1, source_target_pairs={{0,6},{2,0},{4,2},{6,4},{1,7},{3,1},{5,3},{7,5},{8,14},{10,8},{12,... | collective-permute-start | bytes 602120 | tf_op jit(solution)/shard_map/ppermute | solution.py:296
  61.8 0.7 copy-start.2
  61.8 0.7 copy-start.3
  71.8 15.4 %collective-permute-start.4 = (bf16[8,64,512]{2,1,0:T(8,128)(2,1)S(1)}, bf16[8,64,512]{2,1,0:T(8,128)(2,1)S(1)}, u32[]{:S(2)}, u32[]{:S(2)}) collective-permute-start(bf16[8,64,512]{2,1,0:T(8,128)(2,1)S(1)} %all-to-all-done.1.own_ref), channel_id=1, source_target_pairs={{0,1},{1,0},{2,3},{3,2},{4,5},{5,4},{6,7},{7,6},{8,9},{9,8},{10,11... | collective-permute-start | bytes 1572872 | tf_op jit(solution)/shard_map/ppermute | solution.py:319
  89.0 9.6 %copy-start.5 = (bf16[512]{0:T(512)(128)(2,1)S(1)}, bf16[512]{0:T(512)(128)(2,1)}, u32[]{:S(2)}) copy-start(bf16[512]{0:T(512)(128)(2,1)} %param.18) | copy-start | bytes 3076
  89.0 31.3 %copy-start.1 = (bf16[128,512]{1,0:T(8,128)(2,1)S(1)}, bf16[128,512]{1,0:T(8,128)(2,1)}, u32[]{:S(2)}) copy-start(bf16[128,512]{1,0:T(8,128)(2,1)} %rows_ref.1) | copy-start | bytes 393220
  89.0 31.3 %all-to-all-start.2 = ((bf16[32,128,128]{2,1,0:T(8,128)(2,1)}), bf16[32,128,128]{2,1,0:T(8,128)(2,1)S(1)}, u32[]{:S(2)}, u32[]{:S(2)}) async-start(bf16[32,128,128]{2,1,0:T(8,128)(2,1)} %output.1), calls=%async_computation.2 | async-start | bytes 2097152 | tf_op jit(solution)/shard_map/all_to_all | solution.py:235
  98.6 0.7 copy-start.6
  121.8 28.1 %all-to-all-start.3 = ((bf16[64,2,512]{2,1,0:T(2,128)(2,1)}), bf16[64,2,512]{2,1,0:T(2,128)(2,1)S(1)}, u32[]{:S(2)}, u32[]{:S(2)}) async-start(bf16[64,2,512]{2,1,0:T(2,128)(2,1)} %all_to_all.20), calls=%async_computation.3 | async-start | bytes 262144 | tf_op jit(solution)/shard_map/all_to_all | solution.py:348

commit v4 on v3

--- a/solution.py
+++ b/solution.py
@@ -11,8 +11,9 @@
 KVH = 2
 NT, NZ, NX, NC = 8, 8, 4, 2
 NQ, NB = 4, 2
-TP = ("quad", "pair")
-FSDP = ("z", "x", "core")
+TP = ("tp",)
+Z = ("quad", "pair")
+FSDP = Z + ("x", "core")
 ORDER = (6, 3, 1, 2, 4, 7, 5, 0)
 AT = tuple(ORDER.index(t) for t in range(NT))
 ROWS = 128
@@ -106,7 +107,9 @@
     dest_column = jnp.sum(jnp.where(rows == cols, dest_line, 0), axis=1, keepdims=True)
     same = (dest_column == dest_line) & (rows < cols)
     rank = jnp.sum(same.astype(jnp.int32), axis=0, keepdims=True)
-    order_ref[...] = (rows == CAP * dest_line + rank).astype(f32).astype(bf16)
+    z, x, c = dest_line // (NX * NC), dest_line // NC % NX, dest_line % NC
+    place = (x * NZ + z) * NC + c
+    order_ref[...] = (rows == CAP * place + rank).astype(f32).astype(bf16)
 
 
 def project_kernel(
@@ -276,12 +279,13 @@
         vmem=60,
     )(decoded, query_weight, key_weight, value_weight, out_weight.T)
     tokens = exchange(sent)
-    own = lax.all_gather(shard, "z", axis=0, tiled=False)
+    own = lax.all_gather(lax.all_gather(shard, "pair"), "quad")
+    own = own.reshape((NZ,) + shard.shape)
     other = lax.ppermute(own, "core", swap)
     gain = lax.dynamic_slice_in_dim(attn_gain.reshape(NT, NX, BLK), me_x, 1, 1)[:, 0]
 
     out_sent, tokens, own = lax.optimization_barrier((out_sent, tokens, own))
-    out_own = lax.all_to_all(out_sent, "z", split_axis=0, concat_axis=0, tiled=True)
+    out_own = lax.all_to_all(out_sent, Z, split_axis=0, concat_axis=0, tiled=True)
 
     block = jax.ShapeDtypeStruct((PW + EXTRA, HD), bf16)
     parts = call(
@@ -293,7 +297,7 @@
         name="project",
     )(tokens, own, other, gain)
     summands = [parts[0]] + [
-        lax.ppermute(parts[s], "x", [(i, (i + s) % NX) for i in range(NX)]) for s in range(1, NX)
+        lax.ppermute(parts[s], "x", [(i, (i + s) % NX) for i in range(NX)]) for s in (2, 1, 3)
     ]
 
     half = jnp.arange(HD // 2, dtype=f32)
@@ -315,6 +319,7 @@
         flops=2 * 128 * 128 * 128 * 8,
         name="attend",
     )(lengths, own_part, *summands[1:], cosine, sine)
+
     out_own, attended = lax.optimization_barrier((out_own, attended))
     out_other = lax.ppermute(out_own, "core", swap)
 
@@ -345,14 +350,15 @@
         final_gain.reshape(1, FEAT),
         head_weight.reshape(1, FEAT),
     )
-    hidden = lax.all_to_all(placed, FSDP, split_axis=0, concat_axis=0, tiled=True)
+    hidden = lax.all_to_all(placed, ("x",) + Z + ("core",), split_axis=0, concat_axis=0, tiled=True)
+    hidden = hidden.reshape(NX, NZ, NC * CAP, FEAT).transpose(1, 0, 2, 3).reshape(ROWS, FEAT)
     stat = lax.psum(stat[:, :RESP], TP)
     rewards = lax.rsqrt(stat[0] / D + norm_eps) * stat[1]
     return (hidden, rewards)
 
 
 def solution(mesh):
-    grid = Mesh(mesh.devices.reshape(NQ, NB, NZ, NX, NC), TP + FSDP)
+    grid = Mesh(mesh.devices.reshape(NT, NQ, NB, NX, NC), TP + FSDP)
     return jax.shard_map(
         body,
         mesh=grid,

time: 151 us -> 150 us (level)
  blocking collectives: 61.7 us -> 58.9 us
  starting transfers between devices: 48.3 us -> 49.9 us
    all_gather x1 -> x2, blocking collectives: 31.8 us -> 29 us  [body(): own = lax.all_gather(lax.all_gather(shard, 'pair'), 'quad')]
where the time goes in v4:
time: 150 us; the launch traced here: 149 us
  blocking collectives  58.9 us (39%)
  starting transfers between devices  49.9 us (33%)
  waiting for transfers between devices  27.1 us (18%)
  Pallas kernels  8.74 us (6%)
  local copies, waits for them, and re-layouts  2.89 us (2%)
    all_gather x2, blocking collectives, body(): own = lax.all_gather(lax.all_gather(shard, 'pair'), 'quad')  29 us
    all_to_all x2, waiting for transfers between devices, exchange(): lax.all_to_all(blocks, TP + ('x',), split_axis=0, concat_axis=0, tiled=Tr...  21 us
    all_to_all x2, starting transfers between devices, exchange(): lax.all_to_all(blocks, TP + ('x',), split_axis=0, concat_axis=0, tiled=Tr...  20.7 us
    psum x1, blocking collectives, body(): stat = lax.psum(stat[:, :RESP], TP)  16.5 us
    all_gather x1, blocking collectives, body(): slab = lax.all_gather(attended, 'x', axis=0, tiled=True)  13.4 us
    all_to_all x1, starting transfers between devices, body(): lax.all_to_all(placed, ('x',) + Z + ('core',), split_axis=0, concat_axis=...  11.3 us
    ppermute x3, starting transfers between devices, body(): lax.ppermute(parts[s], 'x', [(i, (i + s) % NX) for i in range(NX)])  9.26 us
    ppermute x3, waiting for transfers between devices, body(): lax.ppermute(parts[s], 'x', [(i, (i + s) % NX) for i in range(NX)])  6.05 us
  transfers between devices with their start and end apart: 9, of which 3 were waited for; matrix products, arithmetic and copies ran while one was open for 0% of the time, Pallas kernels for 3%

profile of v4, /device:TPU:6, one launch (start us, length us, event | category | flops | bytes accessed | tf_op | source)
XLA Modules:
  0.0 148.9 jit_solution(884358305362666593)
XLA Ops:
  0.6 2.3 %prepare.1 = (bf16[32,128,128]{2,1,0:T(8,128)(2,1)}, bf16[64,768]{1,0:T(8,128)(2,1)}, bf16[8,64,512]{2,1,0:T(8,128)(2,1)}) custom-call(bf16[128,512]{1,0:T(8,128)(2,1)} %rows_ref.1, bf16[64,512]{1,0:T(8,128)(2,1)} %query.1, bf16[64,256]{1,0:T(8,128)(2,1)} %key.1, bf16[64,256]{1,0:T(8,128)(2,1)} %value.1, bf16[64,512]{1,0:T(8,128)(2,1)} %bitcast.21), custom_call_target="tpu_custom_call" | custom-call | bytes 4194304 | tf_op jit(solution)/shard_map/prepare/pallas_call | solution.py:263
  2.9 11.1 %all-to-all-start = ((bf16[32,128,128]{2,1,0:T(8,128)(2,1)}), bf16[32,128,128]{2,1,0:T(8,128)(2,1)S(1)}, u32[]{:S(2)}, u32[]{:S(2)}) async-start(bf16[32,128,128]{2,1,0:T(8,128)(2,1)} %get-tuple-element.23), calls=%async_computation | async-start | bytes 2097152 | tf_op jit(solution)/shard_map/all_to_all | solution.py:238
  14.0 5.3 %all-gather = bf16[128,768]{1,0:T(8,128)(2,1)S(1)} all-gather(bf16[64,768]{1,0:T(8,128)(2,1)S(1)} %copy-done.4), channel_id=2, replica_groups=mesh['tp'=8,'quad'=4,'pair'=2,'x'=4,'core'=2] {'pair'}, dimensions={0}, use_global_device_ids=true | all-gather | bytes 294912 | tf_op jit(solution)/shard_map/all_gather | solution.py:282
  19.3 23.7 %all-gather.1.own_ref = bf16[8,64,768]{2,1,0:T(8,128)(2,1)S(1)} all-gather(bf16[2,64,768]{2,1,0:T(8,128)(2,1)S(1)} %bitcast.19), channel_id=3, replica_groups=mesh['tp'=8,'quad'=4,'pair'=2,'x'=4,'core'=2] {'quad'}, dimensions={0}, use_global_device_ids=true | all-gather | bytes 983040 | tf_op jit(solution)/shard_map/all_gather | solution.py:282
  43.0 1.9 %collective-permute-start = (bf16[8,64,768]{2,1,0:T(8,128)(2,1)S(1)}, bf16[8,64,768]{2,1,0:T(8,128)(2,1)S(1)}, u32[]{:S(2)}, u32[]{:S(2)}) collective-permute-start(bf16[8,64,768]{2,1,0:T(8,128)(2,1)S(1)} %all-gather.1.own_ref), channel_id=1, source_target_pairs={{0,1},{1,0},{2,3},{3,2},{4,5},{5,4},{6,7},{7,6},{8,9},{9,8},{10,11... | collective-permute-start | bytes 2359304 | tf_op jit(solution)/shard_map/ppermute | solution.py:284
  45.0 4.7 %all-to-all-start.1 = ((bf16[8,64,512]{2,1,0:T(8,128)(2,1)}), bf16[8,64,512]{2,1,0:T(8,128)(2,1)S(1)}, u32[]{:S(2)}, u32[]{:S(2)}) async-start(bf16[8,64,512]{2,1,0:T(8,128)(2,1)} %get-tuple-element.25), calls=%async_computation.1 | async-start | bytes 1048576 | tf_op jit(solution)/shard_map/all_to_all | solution.py:288
  49.7 1.1 project.1
  50.9 3.3 %collective-permute-start.1 = (bf16[784,128]{1,0:T(8,128)(2,1)S(1)}, bf16[784,128]{1,0:T(8,128)(2,1)S(1)}, u32[]{:S(2)}, u32[]{:S(2)}) collective-permute-start(bf16[784,128]{1,0:T(8,128)(2,1)S(1)} %get-tuple-element.30), channel_id=1, source_target_pairs={{0,4},{2,6},{4,0},{6,2},{1,5},{3,7},{5,1},{7,3},{8,12},{10,14},{12... | collective-permute-start | bytes 602120 | tf_op jit(solution)/shard_map/ppermute | solution.py:300
  54.2 4.0 %collective-permute-start.2 = (bf16[784,128]{1,0:T(8,128)(2,1)S(1)}, bf16[784,128]{1,0:T(8,128)(2,1)S(1)}, u32[]{:S(2)}, u32[]{:S(2)}) collective-permute-start(bf16[784,128]{1,0:T(8,128)(2,1)S(1)} %get-tuple-element.31), channel_id=1, source_target_pairs={{0,2},{2,4},{4,6},{6,0},{1,3},{3,5},{5,7},{7,1},{8,10},{10,12},{12... | collective-permute-start | bytes 602120 | tf_op jit(solution)/shard_map/ppermute | solution.py:300
  58.3 1.9 %collective-permute-start.3 = (bf16[784,128]{1,0:T(8,128)(2,1)S(1)}, bf16[784,128]{1,0:T(8,128)(2,1)S(1)}, u32[]{:S(2)}, u32[]{:S(2)}) collective-permute-start(bf16[784,128]{1,0:T(8,128)(2,1)S(1)} %get-tuple-element.32), channel_id=1, source_target_pairs={{0,6},{2,0},{4,2},{6,4},{1,7},{3,1},{5,3},{7,5},{8,14},{10,8},{12,... | collective-permute-start | bytes 602120 | tf_op jit(solution)/shard_map/ppermute | solution.py:300
  61.0 0.9 tables.1
  61.9 1.6 %collective-permute-done.2.part2 = bf16[784,128]{1,0:T(8,128)(2,1)S(1)} collective-permute-done((bf16[784,128]{1,0:T(8,128)(2,1)S(1)}, bf16[784,128]{1,0:T(8,128)(2,1)S(1)}, u32[]{:S(2)}, u32[]{:S(2)}) %collective-permute-start.2) | collective-permute-done | bytes 200736 | tf_op jit(solution)/shard_map/ppermute | solution.py:300
  63.5 4.4 %collective-permute-done.3.part3 = bf16[784,128]{1,0:T(8,128)(2,1)S(1)} collective-permute-done((bf16[784,128]{1,0:T(8,128)(2,1)S(1)}, bf16[784,128]{1,0:T(8,128)(2,1)S(1)}, u32[]{:S(2)}, u32[]{:S(2)}) %collective-permute-start.3) | collective-permute-done | bytes 200736 | tf_op jit(solution)/shard_map/ppermute | solution.py:300
  67.9 1.8 %attend.1 = bf16[128,512]{1,0:T(8,128)(2,1)S(1)} custom-call(s32[1,8]{1,0:T(1,128)S(1)} %copy-done.2, bf16[784,128]{1,0:T(8,128)(2,1)S(1)} %get-tuple-element.29.part0, bf16[784,128]{1,0:T(8,128)(2,1)S(1)} %collective-permute-done.1.part1, bf16[784,128]{1,0:T(8,128)(2,1)S(1)} %collective-permute-done.2.part2, ...), custom_call_target="tpu_custom_call" | custom-call | flops 33554432 | bytes 4194304 | tf_op jit(solution)/shard_map/attend/pallas_call | solution.py:315
  69.8 1.9 %collective-permute-start.4 = (bf16[8,64,512]{2,1,0:T(8,128)(2,1)S(1)}, bf16[8,64,512]{2,1,0:T(8,128)(2,1)S(1)}, u32[]{:S(2)}, u32[]{:S(2)}) collective-permute-start(bf16[8,64,512]{2,1,0:T(8,128)(2,1)S(1)} %all-to-all-done.1.own_ref), channel_id=1, source_target_pairs={{0,1},{1,0},{2,3},{3,2},{4,5},{5,4},{6,7},{7,6},{8,9},{9,8},{10,11... | collective-permute-start | bytes 1572872 | tf_op jit(solution)/shard_map/ppermute | solution.py:324
  71.7 13.4 %all_gather.19.x_ref = bf16[512,512]{1,0:T(8,128)(2,1)S(1)} all-gather(bf16[128,512]{1,0:T(8,128)(2,1)S(1)} %attend.1), channel_id=1, replica_groups=mesh['tp'=8,'quad'=4,'pair'=2,'x'=4,'core'=2] {'x'}, dimensions={0}, use_global_device_ids=true | all-gather | bytes 655360 | tf_op jit(solution)/shard_map/all_gather | solution.py:326
  85.1 1.7 %output.1 = bf16[32,128,128]{2,1,0:T(8,128)(2,1)} custom-call(bf16[512,512]{1,0:T(8,128)(2,1)S(1)} %all_gather.19.x_ref, bf16[8,64,512]{2,1,0:T(8,128)(2,1)S(1)} %all-to-all-done.1.own_ref, bf16[8,64,512]{2,1,0:T(8,128)(2,1)S(1)} %collective-permute-done.4.other_ref), custom_call_target="tpu_custom_call" | custom-call | flops 536870912 | bytes 4194304 | tf_op jit(solution)/shard_map/output/pallas_call | solution.py:327
  86.8 9.6 %all-to-all-start.2 = ((bf16[32,128,128]{2,1,0:T(8,128)(2,1)}), bf16[32,128,128]{2,1,0:T(8,128)(2,1)S(1)}, u32[]{:S(2)}, u32[]{:S(2)}) async-start(bf16[32,128,128]{2,1,0:T(8,128)(2,1)} %output.1), calls=%async_computation.2 | async-start | bytes 2097152 | tf_op jit(solution)/shard_map/all_to_all | solution.py:238
  97.2 21.0 %all-to-all-done.2.parts_ref = bf16[32,128,128]{2,1,0:T(8,128)(2,1)S(1)} async-done(((bf16[32,128,128]{2,1,0:T(8,128)(2,1)}), bf16[32,128,128]{2,1,0:T(8,128)(2,1)S(1)}, u32[]{:S(2)}, u32[]{:S(2)}) %all-to-all-start.2) | async-done | bytes 1048608 | tf_op jit(solution)/shard_map/all_to_all | solution.py:238
  118.2 0.9 layer.1
  119.1 0.7 all_to_all.18
  119.8 11.3 %all-to-all-start.3 = ((bf16[64,2,512]{2,1,0:T(2,128)(2,1)}), bf16[64,2,512]{2,1,0:T(2,128)(2,1)S(1)}, u32[]{:S(2)}, u32[]{:S(2)}) async-start(bf16[64,2,512]{2,1,0:T(2,128)(2,1)} %all_to_all.18), calls=%async_computation.3 | async-start | bytes 262144 | tf_op jit(solution)/shard_map/all_to_all | solution.py:353
  131.1 16.5 %psum.7 = f32[2,8]{1,0:T(2,128)S(1)} all-reduce(f32[2,8]{1,0:T(2,128)S(1)} %bitcast.17), channel_id=1, replica_groups=mesh['tp'=8,'quad'=4,'pair'=2,'x'=4,'core'=2] {'tp'}, use_global_device_ids=true, to_apply=%region_0.0 | all-reduce | flops 16 | bytes 128 | tf_op jit(solution)/shard_map/psum | solution.py:355
  148.2 0.7 reshape.40
  (29 shorter events, 2.1 us)
Async XLA Ops:
  0.6 49.1 %copy-start = (bf16[4096]{0:T(1024)(128)(2,1)S(1)}, bf16[4096]{0:T(1024)(128)(2,1)}, u32[]{:S(2)}) copy-start(bf16[4096]{0:T(1024)(128)(2,1)} %param.13) | copy-start | bytes 24580
  2.9 11.1 %copy-start.4 = (bf16[64,768]{1,0:T(8,128)(2,1)S(1)}, bf16[64,768]{1,0:T(8,128)(2,1)}, u32[]{:S(2)}) copy-start(bf16[64,768]{1,0:T(8,128)(2,1)} %get-tuple-element.24) | copy-start | bytes 294916
  2.9 42.0 %all-to-all-start = ((bf16[32,128,128]{2,1,0:T(8,128)(2,1)}), bf16[32,128,128]{2,1,0:T(8,128)(2,1)S(1)}, u32[]{:S(2)}, u32[]{:S(2)}) async-start(bf16[32,128,128]{2,1,0:T(8,128)(2,1)} %get-tuple-element.23), calls=%async_computation | async-start | bytes 2097152 | tf_op jit(solution)/shard_map/all_to_all | solution.py:238
  43.0 6.7 %collective-permute-start = (bf16[8,64,768]{2,1,0:T(8,128)(2,1)S(1)}, bf16[8,64,768]{2,1,0:T(8,128)(2,1)S(1)}, u32[]{:S(2)}, u32[]{:S(2)}) collective-permute-start(bf16[8,64,768]{2,1,0:T(8,128)(2,1)S(1)} %all-gather.1.own_ref), channel_id=1, source_target_pairs={{0,1},{1,0},{2,3},{3,2},{4,5},{5,4},{6,7},{7,6},{8,9},{9,8},{10,11... | collective-permute-start | bytes 2359304 | tf_op jit(solution)/shard_map/ppermute | solution.py:284
  45.0 24.8 %all-to-all-start.1 = ((bf16[8,64,512]{2,1,0:T(8,128)(2,1)}), bf16[8,64,512]{2,1,0:T(8,128)(2,1)S(1)}, u32[]{:S(2)}, u32[]{:S(2)}) async-start(bf16[8,64,512]{2,1,0:T(8,128)(2,1)} %get-tuple-element.25), calls=%async_computation.1 | async-start | bytes 1048576 | tf_op jit(solution)/shard_map/all_to_all | solution.py:288
  50.9 11.0 %collective-permute-start.1 = (bf16[784,128]{1,0:T(8,128)(2,1)S(1)}, bf16[784,128]{1,0:T(8,128)(2,1)S(1)}, u32[]{:S(2)}, u32[]{:S(2)}) collective-permute-start(bf16[784,128]{1,0:T(8,128)(2,1)S(1)} %get-tuple-element.30), channel_id=1, source_target_pairs={{0,4},{2,6},{4,0},{6,2},{1,5},{3,7},{5,1},{7,3},{8,12},{10,14},{12... | collective-permute-start | bytes 602120 | tf_op jit(solution)/shard_map/ppermute | solution.py:300
  54.2 9.3 %collective-permute-start.2 = (bf16[784,128]{1,0:T(8,128)(2,1)S(1)}, bf16[784,128]{1,0:T(8,128)(2,1)S(1)}, u32[]{:S(2)}, u32[]{:S(2)}) collective-permute-start(bf16[784,128]{1,0:T(8,128)(2,1)S(1)} %get-tuple-element.31), channel_id=1, source_target_pairs={{0,2},{2,4},{4,6},{6,0},{1,3},{3,5},{5,7},{7,1},{8,10},{10,12},{12... | collective-permute-start | bytes 602120 | tf_op jit(solution)/shard_map/ppermute | solution.py:300
  58.3 9.7 %collective-permute-start.3 = (bf16[784,128]{1,0:T(8,128)(2,1)S(1)}, bf16[784,128]{1,0:T(8,128)(2,1)S(1)}, u32[]{:S(2)}, u32[]{:S(2)}) collective-permute-start(bf16[784,128]{1,0:T(8,128)(2,1)S(1)} %get-tuple-element.32), channel_id=1, source_target_pairs={{0,6},{2,0},{4,2},{6,4},{1,7},{3,1},{5,3},{7,5},{8,14},{10,8},{12,... | collective-permute-start | bytes 602120 | tf_op jit(solution)/shard_map/ppermute | solution.py:300
  60.3 0.7 copy-start.2
  60.3 0.7 copy-start.3
  69.8 15.3 %collective-permute-start.4 = (bf16[8,64,512]{2,1,0:T(8,128)(2,1)S(1)}, bf16[8,64,512]{2,1,0:T(8,128)(2,1)S(1)}, u32[]{:S(2)}, u32[]{:S(2)}) collective-permute-start(bf16[8,64,512]{2,1,0:T(8,128)(2,1)S(1)} %all-to-all-done.1.own_ref), channel_id=1, source_target_pairs={{0,1},{1,0},{2,3},{3,2},{4,5},{5,4},{6,7},{7,6},{8,9},{9,8},{10,11... | collective-permute-start | bytes 1572872 | tf_op jit(solution)/shard_map/ppermute | solution.py:324
  86.8 9.6 %copy-start.5 = (bf16[512]{0:T(512)(128)(2,1)S(1)}, bf16[512]{0:T(512)(128)(2,1)}, u32[]{:S(2)}) copy-start(bf16[512]{0:T(512)(128)(2,1)} %param.18) | copy-start | bytes 3076
  86.8 31.4 %copy-start.1 = (bf16[128,512]{1,0:T(8,128)(2,1)S(1)}, bf16[128,512]{1,0:T(8,128)(2,1)}, u32[]{:S(2)}) copy-start(bf16[128,512]{1,0:T(8,128)(2,1)} %rows_ref.1) | copy-start | bytes 393220
  86.8 31.4 %all-to-all-start.2 = ((bf16[32,128,128]{2,1,0:T(8,128)(2,1)}), bf16[32,128,128]{2,1,0:T(8,128)(2,1)S(1)}, u32[]{:S(2)}, u32[]{:S(2)}) async-start(bf16[32,128,128]{2,1,0:T(8,128)(2,1)} %output.1), calls=%async_computation.2 | async-start | bytes 2097152 | tf_op jit(solution)/shard_map/all_to_all | solution.py:238
  96.5 0.7 copy-start.6
  119.8 28.3 %all-to-all-start.3 = ((bf16[64,2,512]{2,1,0:T(2,128)(2,1)}), bf16[64,2,512]{2,1,0:T(2,128)(2,1)S(1)}, u32[]{:S(2)}, u32[]{:S(2)}) async-start(bf16[64,2,512]{2,1,0:T(2,128)(2,1)} %all_to_all.18), calls=%async_computation.3 | async-start | bytes 262144 | tf_op jit(solution)/shard_map/all_to_all | solution.py:353

commit v5 on v4

--- a/solution.py
+++ b/solution.py
@@ -11,7 +11,7 @@
 KVH = 2
 NT, NZ, NX, NC = 8, 8, 4, 2
 NQ, NB = 4, 2
-TP = ("tp",)
+TP = ("four", "two")
 Z = ("quad", "pair")
 FSDP = Z + ("x", "core")
 ORDER = (6, 3, 1, 2, 4, 7, 5, 0)
@@ -22,6 +22,7 @@
 QW = QH * HD // NT
 PW = QW + 2 * HD
 HEADS = QW // HD
+HALF = ROWS // NB
 EXTRA = 16
 RESP = 8
 CAP = 2
@@ -92,8 +93,8 @@
     shard[:, :QW] = query_ref[...]
     shard[:, QW : QW + HD] = kv_ref[0]
     shard[:, QW + HD :] = kv_ref[1]
-    for z in range(NZ):
-        out_sent[z] = out_ref[...]
+    for i in range(NB * NZ):
+        out_sent[i] = out_ref[...]
 
 
 def table_kernel(lengths_ref, freq_ref, line_ref, cosine_ref, sine_ref, order_ref):
@@ -184,24 +185,31 @@
         probs = jnp.where(allowed, jnp.exp(scores - top), 0.0)
         sums = jnp.sum(probs, axis=1, keepdims=True)
         weighted = jnp.dot(probs.astype(bf16), values, preferred_element_type=f32)
-        out_ref[:, h * HD : (h + 1) * HD] = (weighted / sums).astype(bf16)
+        result = (weighted / sums).astype(bf16)
+        for b in range(NB):
+            for g in range(NX):
+                out_ref[b * NX + g, :, h * HD : (h + 1) * HD] = result[b * HALF : (b + 1) * HALF]
 
 
 def output_kernel(x_ref, own_ref, other_ref, out_ref):
     first = lax.axis_index("core") == 0
     for n in range(NT // 2):
-        rows = []
-        for z in (2 * n, 2 * n + 1):
-            own, other = own_ref[z], other_ref[z]
-            rows += [jnp.where(first, own, other), jnp.where(first, other, own)]
-        part = lax.dot_general(
-            x_ref[...],
-            jnp.concatenate(rows),
-            (((1,), (1,)), ((), ())),
-            preferred_element_type=f32,
-        )
+        part = None
+        for b in range(NB):
+            rows = []
+            for z in (2 * n, 2 * n + 1):
+                own, other = own_ref[b * NZ + z], other_ref[b * NZ + z]
+                rows += [jnp.where(first, own, other), jnp.where(first, other, own)]
+            x = x_ref[b * NX : (b + 1) * NX].reshape(NX * HALF, QW)
+            term = lax.dot_general(
+                x,
+                jnp.concatenate(rows),
+                (((1,), (1,)), ((), ())),
+                preferred_element_type=f32,
+            )
+            part = term if part is None else part + term
         for g in range(NX):
-            rows = part[g * ROWS : (g + 1) * ROWS].astype(bf16)
+            rows = part[g * HALF : (g + 1) * HALF].astype(bf16)
             out_ref[AT[2 * n] * NX + g] = rows[:, :BLK]
             out_ref[AT[2 * n + 1] * NX + g] = rows[:, BLK:]
 
@@ -213,9 +221,13 @@
     product = jnp.zeros((ROWS, BLK), f32)
     for g in range(NX):
         cols = slice(g * BLK, (g + 1) * BLK)
-        update = parts_ref[g].astype(f32)
-        for t in range(1, NT):
-            update = update + parts_ref[t * NX + g].astype(f32)
+        halves = []
+        for b in range(NB):
+            half = parts_ref[AT[b] * NX + g].astype(f32)
+            for t in range(b + NB, NT, NB):
+                half = half + parts_ref[AT[t] * NX + g].astype(f32)
+            halves.append(half)
+        update = jnp.concatenate(halves)
         layer = (rows_ref[:, cols].astype(f32) + update).astype(bf16)
         wide = layer.astype(f32)
         square = square + wide * wide
@@ -265,7 +277,7 @@
         (
             jax.ShapeDtypeStruct((NT * NX, ROWS, BLK), bf16),
             jax.ShapeDtypeStruct((D // (NZ * NX * NC), PW), bf16),
-            jax.ShapeDtypeStruct((NZ, D // (NZ * NX * NC), QW), bf16),
+            jax.ShapeDtypeStruct((NB * NZ, D // (NZ * NX * NC), QW), bf16),
         ),
         [ANY] * 5,
         [
@@ -285,7 +297,7 @@
     gain = lax.dynamic_slice_in_dim(attn_gain.reshape(NT, NX, BLK), me_x, 1, 1)[:, 0]
 
     out_sent, tokens, own = lax.optimization_barrier((out_sent, tokens, own))
-    out_own = lax.all_to_all(out_sent, Z, split_axis=0, concat_axis=0, tiled=True)
+    out_own = lax.all_to_all(out_sent, ("two",) + Z, split_axis=0, concat_axis=0, tiled=True)
 
     block = jax.ShapeDtypeStruct((PW + EXTRA, HD), bf16)
     parts = call(
@@ -314,7 +326,7 @@
     )(after, freq, line)
     attended = call(
         attend_kernel,
-        jax.ShapeDtypeStruct((ROWS, QW), bf16),
+        jax.ShapeDtypeStruct((NB * NX, HALF, QW), bf16),
         [SMEM] + [VMEM] * (NX + 2),
         flops=2 * 128 * 128 * 128 * 8,
         name="attend",
@@ -323,10 +335,10 @@
     out_own, attended = lax.optimization_barrier((out_own, attended))
     out_other = lax.ppermute(out_own, "core", swap)
 
-    slab = lax.all_gather(attended, "x", axis=0, tiled=True)
+    slab = lax.all_to_all(attended, ("two", "x"), split_axis=0, concat_axis=0, tiled=True)
     products = call(
         output_kernel,
-        jax.ShapeDtypeStruct((NT * NX, ROWS, BLK), bf16),
+        jax.ShapeDtypeStruct((NT * NX, HALF, BLK), bf16),
         [VMEM] * 3,
         flops=2 * 512 * 512 * 1024,
         name="output",
@@ -358,7 +370,7 @@
 
 
 def solution(mesh):
-    grid = Mesh(mesh.devices.reshape(NT, NQ, NB, NX, NC), TP + FSDP)
+    grid = Mesh(mesh.devices.reshape(NQ, NB, NQ, NB, NX, NC), TP + FSDP)
     return jax.shard_map(
         body,
         mesh=grid,

time: 150 us -> 145 us (0.967)
  waiting for transfers between devices: 27.1 us -> 21.7 us
    all_gather x1 -> x0, blocking collectives: 13.4 us -> none  [body(): slab = lax.all_gather(attended, 'x', axis=0, tiled=True)]
    all_to_all x0 -> x1, blocking collectives: none -> 13.4 us  [body(): lax.all_to_all(attended, ('two', 'x'), split_axis=0, concat_axis=0, tiled...]
    all_to_all x2, waiting for transfers between devices: 21 us -> 12.8 us  [exchange(): lax.all_to_all(blocks, TP + ('x',), split_axis=0, concat_axis=0, tiled=Tr...]
    ppermute x1, waiting for transfers between devices: 0.01 us -> 2.34 us  [body(): other = lax.ppermute(own, 'core', swap)]
  transfers between devices with their start and end apart: 9 -> 9, of which waited for: 3 -> 5; matrix products, arithmetic and copies ran while one was open for 0% -> 0% of each run, Pallas kernels for 3% -> 3%
where the time goes in v5:
time: 145 us; the launch traced here: 144 us
  blocking collectives  59 us (41%)
  starting transfers between devices  49.2 us (34%)
  waiting for transfers between devices  21.7 us (15%)
  Pallas kernels  9.82 us (7%)
  local copies, waits for them, and re-layouts  2.89 us (2%)
    all_gather x2, blocking collectives, body(): own = lax.all_gather(lax.all_gather(shard, 'pair'), 'quad')  29 us
    all_to_all x2, starting transfers between devices, exchange(): lax.all_to_all(blocks, TP + ('x',), split_axis=0, concat_axis=0, tiled=Tr...  19.9 us
    psum x1, blocking collectives, body(): stat = lax.psum(stat[:, :RESP], TP)  16.6 us
    all_to_all x1, blocking collectives, body(): lax.all_to_all(attended, ('two', 'x'), split_axis=0, concat_axis=0, tiled...  13.4 us
    all_to_all x2, waiting for transfers between devices, exchange(): lax.all_to_all(blocks, TP + ('x',), split_axis=0, concat_axis=0, tiled=Tr...  12.8 us
    all_to_all x1, starting transfers between devices, body(): lax.all_to_all(placed, ('x',) + Z + ('core',), split_axis=0, concat_axis=...  10.4 us
    ppermute x3, starting transfers between devices, body(): lax.ppermute(parts[s], 'x', [(i, (i + s) % NX) for i in range(NX)])  9.26 us
    ppermute x3, waiting for transfers between devices, body(): lax.ppermute(parts[s], 'x', [(i, (i + s) % NX) for i in range(NX)])  5.97 us
  transfers between devices with their start and end apart: 9, of which 5 were waited for; matrix products, arithmetic and copies ran while one was open for 0% of the time, Pallas kernels for 3%

profile of v5, /device:TPU:6, one launch (start us, length us, event | category | flops | bytes accessed | tf_op | source)
XLA Modules:
  0.0 144.1 jit_solution(3292806722821573711)
XLA Ops:
  0.6 2.5 %prepare.1 = (bf16[32,128,128]{2,1,0:T(8,128)(2,1)}, bf16[64,768]{1,0:T(8,128)(2,1)}, bf16[16,64,512]{2,1,0:T(8,128)(2,1)}) custom-call(bf16[128,512]{1,0:T(8,128)(2,1)} %rows_ref.1, bf16[64,512]{1,0:T(8,128)(2,1)} %query.1, bf16[64,256]{1,0:T(8,128)(2,1)} %key.1, bf16[64,256]{1,0:T(8,128)(2,1)} %value.1, bf16[64,512]{1,0:T(8,128)(2,1)} %bitcast.21), custom_call_target="tpu_custom_call" | custom-call | bytes 4194304 | tf_op jit(solution)/shard_map/prepare/pallas_call | solution.py:275
  3.1 11.1 %all-to-all-start = ((bf16[32,128,128]{2,1,0:T(8,128)(2,1)}), bf16[32,128,128]{2,1,0:T(8,128)(2,1)S(1)}, u32[]{:S(2)}, u32[]{:S(2)}) async-start(bf16[32,128,128]{2,1,0:T(8,128)(2,1)} %get-tuple-element.23), calls=%async_computation | async-start | bytes 2097152 | tf_op jit(solution)/shard_map/all_to_all | solution.py:250
  14.2 5.3 %all-gather = bf16[128,768]{1,0:T(8,128)(2,1)S(1)} all-gather(bf16[64,768]{1,0:T(8,128)(2,1)S(1)} %copy-done.4), channel_id=2, replica_groups=mesh['four'=4,'two'=2,'quad'=4,'pair'=2,'x'=4,'core'=2] {'pair'}, dimensions={0}, use_global_device_ids=true | all-gather | bytes 294912 | tf_op jit(solution)/shard_map/all_gather | solution.py:294
  19.5 23.7 %all-gather.1.own_ref = bf16[8,64,768]{2,1,0:T(8,128)(2,1)S(1)} all-gather(bf16[2,64,768]{2,1,0:T(8,128)(2,1)S(1)} %bitcast.19), channel_id=3, replica_groups=mesh['four'=4,'two'=2,'quad'=4,'pair'=2,'x'=4,'core'=2] {'quad'}, dimensions={0}, use_global_device_ids=true | all-gather | bytes 983040 | tf_op jit(solution)/shard_map/all_gather | solution.py:294
  43.2 5.8 %all-to-all-start.1 = ((bf16[16,64,512]{2,1,0:T(8,128)(2,1)}), bf16[16,64,512]{2,1,0:T(8,128)(2,1)S(1)}, u32[]{:S(2)}, u32[]{:S(2)}) async-start(bf16[16,64,512]{2,1,0:T(8,128)(2,1)} %get-tuple-element.25), calls=%async_computation.1 | async-start | bytes 2097152 | tf_op jit(solution)/shard_map/all_to_all | solution.py:300
  49.0 1.9 %collective-permute-start = (bf16[8,64,768]{2,1,0:T(8,128)(2,1)S(1)}, bf16[8,64,768]{2,1,0:T(8,128)(2,1)}, u32[]{:S(2)}, u32[]{:S(2)}) collective-permute-start(bf16[8,64,768]{2,1,0:T(8,128)(2,1)S(1)} %all-gather.1.own_ref), channel_id=1, source_target_pairs={{0,1},{1,0},{2,3},{3,2},{4,5},{5,4},{6,7},{7,6},{8,9},{9,8},{10,11... | collective-permute-start | bytes 2359304 | tf_op jit(solution)/shard_map/ppermute | solution.py:296
  51.0 2.3 %collective-permute-done.other_ref = bf16[8,64,768]{2,1,0:T(8,128)(2,1)} collective-permute-done((bf16[8,64,768]{2,1,0:T(8,128)(2,1)S(1)}, bf16[8,64,768]{2,1,0:T(8,128)(2,1)}, u32[]{:S(2)}, u32[]{:S(2)}) %collective-permute-start) | collective-permute-done | bytes 786464 | tf_op jit(solution)/shard_map/ppermute | solution.py:296
  53.3 2.3 %project.1 = (bf16[784,128]{1,0:T(8,128)(2,1)S(1)}, bf16[784,128]{1,0:T(8,128)(2,1)S(1)}, bf16[784,128]{1,0:T(8,128)(2,1)S(1)}, bf16[784,128]{1,0:T(8,128)(2,1)S(1)}) custom-call(bf16[32,128,128]{2,1,0:T(8,128)(2,1)S(1)} %all-to-all-done.x_ref, bf16[8,64,768]{2,1,0:T(8,128)(2,1)S(1)} %all-gather.1.own_ref, ...), custom_call_target="tpu_custom_call" | custom-call | flops 805306368 | bytes 4194304 | tf_op jit(solution)/shard_map/project/pallas_call | solution.py:303
  55.6 3.4 %collective-permute-start.1 = (bf16[784,128]{1,0:T(8,128)(2,1)S(1)}, bf16[784,128]{1,0:T(8,128)(2,1)S(1)}, u32[]{:S(2)}, u32[]{:S(2)}) collective-permute-start(bf16[784,128]{1,0:T(8,128)(2,1)S(1)} %get-tuple-element.30), channel_id=1, source_target_pairs={{0,4},{2,6},{4,0},{6,2},{1,5},{3,7},{5,1},{7,3},{8,12},{10,14},{12... | collective-permute-start | bytes 602120 | tf_op jit(solution)/shard_map/ppermute | solution.py:312
  59.0 4.0 %collective-permute-start.2 = (bf16[784,128]{1,0:T(8,128)(2,1)S(1)}, bf16[784,128]{1,0:T(8,128)(2,1)S(1)}, u32[]{:S(2)}, u32[]{:S(2)}) collective-permute-start(bf16[784,128]{1,0:T(8,128)(2,1)S(1)} %get-tuple-element.31), channel_id=1, source_target_pairs={{0,2},{2,4},{4,6},{6,0},{1,3},{3,5},{5,7},{7,1},{8,10},{10,12},{12... | collective-permute-start | bytes 602120 | tf_op jit(solution)/shard_map/ppermute | solution.py:312
  63.0 1.9 %collective-permute-start.3 = (bf16[784,128]{1,0:T(8,128)(2,1)S(1)}, bf16[784,128]{1,0:T(8,128)(2,1)S(1)}, u32[]{:S(2)}, u32[]{:S(2)}) collective-permute-start(bf16[784,128]{1,0:T(8,128)(2,1)S(1)} %get-tuple-element.32), channel_id=1, source_target_pairs={{0,6},{2,0},{4,2},{6,4},{1,7},{3,1},{5,3},{7,5},{8,14},{10,8},{12,... | collective-permute-start | bytes 602120 | tf_op jit(solution)/shard_map/ppermute | solution.py:312
  65.7 0.9 tables.1
  66.6 3.4 %collective-permute-done.2.part2 = bf16[784,128]{1,0:T(8,128)(2,1)S(1)} collective-permute-done((bf16[784,128]{1,0:T(8,128)(2,1)S(1)}, bf16[784,128]{1,0:T(8,128)(2,1)S(1)}, u32[]{:S(2)}, u32[]{:S(2)}) %collective-permute-start.2) | collective-permute-done | bytes 200736 | tf_op jit(solution)/shard_map/ppermute | solution.py:312
  69.9 2.6 %collective-permute-done.3.part3 = bf16[784,128]{1,0:T(8,128)(2,1)S(1)} collective-permute-done((bf16[784,128]{1,0:T(8,128)(2,1)S(1)}, bf16[784,128]{1,0:T(8,128)(2,1)S(1)}, u32[]{:S(2)}, u32[]{:S(2)}) %collective-permute-start.3) | collective-permute-done | bytes 200736 | tf_op jit(solution)/shard_map/ppermute | solution.py:312
  72.6 1.8 %attend.1 = bf16[8,64,512]{2,1,0:T(8,128)(2,1)S(1)} custom-call(s32[1,8]{1,0:T(1,128)S(1)} %copy-done.2, bf16[784,128]{1,0:T(8,128)(2,1)S(1)} %get-tuple-element.29.part0, bf16[784,128]{1,0:T(8,128)(2,1)S(1)} %collective-permute-done.1.part1, bf16[784,128]{1,0:T(8,128)(2,1)S(1)} %collective-permute-done.2.part2, ...), custom_call_target="tpu_custom_call" | custom-call | flops 33554432 | bytes 4194304 | tf_op jit(solution)/shard_map/attend/pallas_call | solution.py:327
  75.0 1.9 %collective-permute-start.4 = (bf16[16,64,512]{2,1,0:T(8,128)(2,1)S(1)}, bf16[16,64,512]{2,1,0:T(8,128)(2,1)S(1)}, u32[]{:S(2)}, u32[]{:S(2)}) collective-permute-start(bf16[16,64,512]{2,1,0:T(8,128)(2,1)S(1)} %all-to-all-done.1.own_ref), channel_id=1, source_target_pairs={{0,1},{1,0},{2,3},{3,2},{4,5},{5,4},{6,7},{7,6},{8,9},{9,8},{10,11... | collective-permute-start | bytes 3145736 | tf_op jit(solution)/shard_map/ppermute | solution.py:336
  76.9 13.4 %all_to_all.29.x_ref = bf16[8,64,512]{2,1,0:T(8,128)(2,1)S(1)} all-to-all(bf16[8,64,512]{2,1,0:T(8,128)(2,1)S(1)} %attend.1), channel_id=1, replica_groups=mesh['four'=4,'two'=2,'quad'=4,'pair'=2,'x'=4,'core'=2] {'two','x'}, dimensions={0} | all-to-all | bytes 1048576 | tf_op jit(solution)/shard_map/all_to_all | solution.py:338
  90.3 1.6 %output.1 = bf16[32,64,128]{2,1,0:T(8,128)(2,1)} custom-call(bf16[8,64,512]{2,1,0:T(8,128)(2,1)S(1)} %all_to_all.29.x_ref, bf16[16,64,512]{2,1,0:T(8,128)(2,1)S(1)} %all-to-all-done.1.own_ref, bf16[16,64,512]{2,1,0:T(8,128)(2,1)S(1)} %collective-permute-done.4.other_ref), custom_call_target="tpu_custom_call" | custom-call | flops 536870912 | bytes 4194304 | tf_op jit(solution)/shard_map/output/pallas_call | solution.py:339
  91.8 8.8 %all-to-all-start.3 = ((bf16[32,64,128]{2,1,0:T(8,128)(2,1)}), bf16[32,64,128]{2,1,0:T(8,128)(2,1)S(1)}, u32[]{:S(2)}, u32[]{:S(2)}) async-start(bf16[32,64,128]{2,1,0:T(8,128)(2,1)} %output.1), calls=%async_computation.3 | async-start | bytes 1048576 | tf_op jit(solution)/shard_map/all_to_all | solution.py:250
  101.3 12.8 %all-to-all-done.3.parts_ref = bf16[32,64,128]{2,1,0:T(8,128)(2,1)S(1)} async-done(((bf16[32,64,128]{2,1,0:T(8,128)(2,1)}), bf16[32,64,128]{2,1,0:T(8,128)(2,1)S(1)}, u32[]{:S(2)}, u32[]{:S(2)}) %all-to-all-start.3) | async-done | bytes 524320 | tf_op jit(solution)/shard_map/all_to_all | solution.py:250
  114.1 0.8 layer.1
  114.9 0.7 all_to_all.22
  115.6 10.4 %all-to-all-start.4 = ((bf16[64,2,512]{2,1,0:T(2,128)(2,1)}), bf16[64,2,512]{2,1,0:T(2,128)(2,1)S(1)}, u32[]{:S(2)}, u32[]{:S(2)}) async-start(bf16[64,2,512]{2,1,0:T(2,128)(2,1)} %all_to_all.22), calls=%async_computation.4 | async-start | bytes 262144 | tf_op jit(solution)/shard_map/all_to_all | solution.py:365
  126.1 16.6 %psum.7 = f32[2,8]{1,0:T(2,128)S(1)} all-reduce(f32[2,8]{1,0:T(2,128)S(1)} %bitcast.17), channel_id=1, replica_groups=mesh['four'=4,'two'=2,'quad'=4,'pair'=2,'x'=4,'core'=2] {'four','two'}, use_global_device_ids=true, to_apply=%region_0.0 | all-reduce | flops 16 | bytes 128 | tf_op jit(solution)/shard_map/psum | solution.py:367
  (29 shorter events, 3.4 us)
Async XLA Ops:
  0.6 50.3 %copy-start = (bf16[4096]{0:T(1024)(128)(2,1)S(1)}, bf16[4096]{0:T(1024)(128)(2,1)}, u32[]{:S(2)}) copy-start(bf16[4096]{0:T(1024)(128)(2,1)} %param.13) | copy-start | bytes 24580
  3.1 11.1 %copy-start.4 = (bf16[64,768]{1,0:T(8,128)(2,1)S(1)}, bf16[64,768]{1,0:T(8,128)(2,1)}, u32[]{:S(2)}) copy-start(bf16[64,768]{1,0:T(8,128)(2,1)} %get-tuple-element.24) | copy-start | bytes 294916
  3.1 40.1 %all-to-all-start = ((bf16[32,128,128]{2,1,0:T(8,128)(2,1)}), bf16[32,128,128]{2,1,0:T(8,128)(2,1)S(1)}, u32[]{:S(2)}, u32[]{:S(2)}) async-start(bf16[32,128,128]{2,1,0:T(8,128)(2,1)} %get-tuple-element.23), calls=%async_computation | async-start | bytes 2097152 | tf_op jit(solution)/shard_map/all_to_all | solution.py:250
  43.2 31.7 %all-to-all-start.1 = ((bf16[16,64,512]{2,1,0:T(8,128)(2,1)}), bf16[16,64,512]{2,1,0:T(8,128)(2,1)S(1)}, u32[]{:S(2)}, u32[]{:S(2)}) async-start(bf16[16,64,512]{2,1,0:T(8,128)(2,1)} %get-tuple-element.25), calls=%async_computation.1 | async-start | bytes 2097152 | tf_op jit(solution)/shard_map/all_to_all | solution.py:300
  49.0 4.3 %collective-permute-start = (bf16[8,64,768]{2,1,0:T(8,128)(2,1)S(1)}, bf16[8,64,768]{2,1,0:T(8,128)(2,1)}, u32[]{:S(2)}, u32[]{:S(2)}) collective-permute-start(bf16[8,64,768]{2,1,0:T(8,128)(2,1)S(1)} %all-gather.1.own_ref), channel_id=1, source_target_pairs={{0,1},{1,0},{2,3},{3,2},{4,5},{5,4},{6,7},{7,6},{8,9},{9,8},{10,11... | collective-permute-start | bytes 2359304 | tf_op jit(solution)/shard_map/ppermute | solution.py:296
  55.6 11.0 %collective-permute-start.1 = (bf16[784,128]{1,0:T(8,128)(2,1)S(1)}, bf16[784,128]{1,0:T(8,128)(2,1)S(1)}, u32[]{:S(2)}, u32[]{:S(2)}) collective-permute-start(bf16[784,128]{1,0:T(8,128)(2,1)S(1)} %get-tuple-element.30), channel_id=1, source_target_pairs={{0,4},{2,6},{4,0},{6,2},{1,5},{3,7},{5,1},{7,3},{8,12},{10,14},{12... | collective-permute-start | bytes 602120 | tf_op jit(solution)/shard_map/ppermute | solution.py:312
  59.0 11.0 %collective-permute-start.2 = (bf16[784,128]{1,0:T(8,128)(2,1)S(1)}, bf16[784,128]{1,0:T(8,128)(2,1)S(1)}, u32[]{:S(2)}, u32[]{:S(2)}) collective-permute-start(bf16[784,128]{1,0:T(8,128)(2,1)S(1)} %get-tuple-element.31), channel_id=1, source_target_pairs={{0,2},{2,4},{4,6},{6,0},{1,3},{3,5},{5,7},{7,1},{8,10},{10,12},{12... | collective-permute-start | bytes 602120 | tf_op jit(solution)/shard_map/ppermute | solution.py:312
  63.0 9.6 %collective-permute-start.3 = (bf16[784,128]{1,0:T(8,128)(2,1)S(1)}, bf16[784,128]{1,0:T(8,128)(2,1)S(1)}, u32[]{:S(2)}, u32[]{:S(2)}) collective-permute-start(bf16[784,128]{1,0:T(8,128)(2,1)S(1)} %get-tuple-element.32), channel_id=1, source_target_pairs={{0,6},{2,0},{4,2},{6,4},{1,7},{3,1},{5,3},{7,5},{8,14},{10,8},{12,... | collective-permute-start | bytes 602120 | tf_op jit(solution)/shard_map/ppermute | solution.py:312
  65.0 0.7 copy-start.2
  65.0 0.7 copy-start.3
  75.0 15.3 %collective-permute-start.4 = (bf16[16,64,512]{2,1,0:T(8,128)(2,1)S(1)}, bf16[16,64,512]{2,1,0:T(8,128)(2,1)S(1)}, u32[]{:S(2)}, u32[]{:S(2)}) collective-permute-start(bf16[16,64,512]{2,1,0:T(8,128)(2,1)S(1)} %all-to-all-done.1.own_ref), channel_id=1, source_target_pairs={{0,1},{1,0},{2,3},{3,2},{4,5},{5,4},{6,7},{7,6},{8,9},{9,8},{10,11... | collective-permute-start | bytes 3145736 | tf_op jit(solution)/shard_map/ppermute | solution.py:336
  91.8 8.8 %copy-start.5 = (bf16[512]{0:T(512)(128)(2,1)S(1)}, bf16[512]{0:T(512)(128)(2,1)}, u32[]{:S(2)}) copy-start(bf16[512]{0:T(512)(128)(2,1)} %param.18) | copy-start | bytes 3076
  91.8 22.3 %copy-start.1 = (bf16[128,512]{1,0:T(8,128)(2,1)S(1)}, bf16[128,512]{1,0:T(8,128)(2,1)}, u32[]{:S(2)}) copy-start(bf16[128,512]{1,0:T(8,128)(2,1)} %rows_ref.1) | copy-start | bytes 393220
  91.8 22.3 %all-to-all-start.3 = ((bf16[32,64,128]{2,1,0:T(8,128)(2,1)}), bf16[32,64,128]{2,1,0:T(8,128)(2,1)S(1)}, u32[]{:S(2)}, u32[]{:S(2)}) async-start(bf16[32,64,128]{2,1,0:T(8,128)(2,1)} %output.1), calls=%async_computation.3 | async-start | bytes 1048576 | tf_op jit(solution)/shard_map/all_to_all | solution.py:250
  100.6 0.7 copy-start.6
  115.6 27.6 %all-to-all-start.4 = ((bf16[64,2,512]{2,1,0:T(2,128)(2,1)}), bf16[64,2,512]{2,1,0:T(2,128)(2,1)S(1)}, u32[]{:S(2)}, u32[]{:S(2)}) async-start(bf16[64,2,512]{2,1,0:T(2,128)(2,1)} %all_to_all.22), calls=%async_computation.4 | async-start | bytes 262144 | tf_op jit(solution)/shard_map/all_to_all | solution.py:365

commit v6 on v5

--- a/solution.py
+++ b/solution.py
@@ -14,7 +14,7 @@
 TP = ("four", "two")
 Z = ("quad", "pair")
 FSDP = Z + ("x", "core")
-ORDER = (6, 3, 1, 2, 4, 7, 5, 0)
+ORDER = (4, 6, 3, 7, 0, 1, 5, 2)
 AT = tuple(ORDER.index(t) for t in range(NT))
 ROWS = 128
 FEAT = D // NT
@@ -188,7 +188,7 @@
         result = (weighted / sums).astype(bf16)
         for b in range(NB):
             for g in range(NX):
-                out_ref[b * NX + g, :, h * HD : (h + 1) * HD] = result[b * HALF : (b + 1) * HALF]
+                out_ref[g * NB + b, :, h * HD : (h + 1) * HD] = result[b * HALF : (b + 1) * HALF]
 
 
 def output_kernel(x_ref, own_ref, other_ref, out_ref):
@@ -198,9 +198,9 @@
         for b in range(NB):
             rows = []
             for z in (2 * n, 2 * n + 1):
-                own, other = own_ref[b * NZ + z], other_ref[b * NZ + z]
+                own, other = own_ref[z * NB + b], other_ref[z * NB + b]
                 rows += [jnp.where(first, own, other), jnp.where(first, other, own)]
-            x = x_ref[b * NX : (b + 1) * NX].reshape(NX * HALF, QW)
+            x = jnp.concatenate([x_ref[g * NB + b] for g in range(NX)])
             term = lax.dot_general(
                 x,
                 jnp.concatenate(rows),
@@ -297,7 +297,7 @@
     gain = lax.dynamic_slice_in_dim(attn_gain.reshape(NT, NX, BLK), me_x, 1, 1)[:, 0]
 
     out_sent, tokens, own = lax.optimization_barrier((out_sent, tokens, own))
-    out_own = lax.all_to_all(out_sent, ("two",) + Z, split_axis=0, concat_axis=0, tiled=True)
+    out_own = lax.all_to_all(out_sent, Z + ("two",), split_axis=0, concat_axis=0, tiled=True)
 
     block = jax.ShapeDtypeStruct((PW + EXTRA, HD), bf16)
     parts = call(
@@ -309,7 +309,7 @@
         name="project",
     )(tokens, own, other, gain)
     summands = [parts[0]] + [
-        lax.ppermute(parts[s], "x", [(i, (i + s) % NX) for i in range(NX)]) for s in (2, 1, 3)
+        lax.ppermute(parts[s], "x", [(i, (i + s) % NX) for i in range(NX)]) for s in (2, 3, 1)
     ]
 
     half = jnp.arange(HD // 2, dtype=f32)
@@ -335,7 +335,7 @@
     out_own, attended = lax.optimization_barrier((out_own, attended))
     out_other = lax.ppermute(out_own, "core", swap)
 
-    slab = lax.all_to_all(attended, ("two", "x"), split_axis=0, concat_axis=0, tiled=True)
+    slab = lax.all_to_all(attended, ("x", "two"), split_axis=0, concat_axis=0, tiled=True)
     products = call(
         output_kernel,
         jax.ShapeDtypeStruct((NT * NX, HALF, BLK), bf16),

time: 145 us -> 143 us (0.986)
  waiting for transfers between devices: 21.7 us -> 18.7 us
    ppermute x3, waiting for transfers between devices: 5.97 us -> 2.61 us  [body(): lax.ppermute(parts[s], 'x', [(i, (i + s) % NX) for i in range(NX)])]
    all_to_all x2, starting transfers between devices: 19.9 us -> 22.8 us  [exchange(): lax.all_to_all(blocks, TP + ('x',), split_axis=0, concat_axis=0, tiled=Tr...]
    all_to_all x1, starting transfers between devices: 10.4 us -> 7.67 us  [body(): lax.all_to_all(placed, ('x',) + Z + ('core',), split_axis=0, concat_axis=...]
    all_to_all x1, waiting for transfers between devices: 0.58 us -> 2.72 us  [body(): lax.all_to_all(out_sent, Z + ('two',), split_axis=0, concat_axis=0, tiled...]
    all_to_all x2, waiting for transfers between devices: 12.8 us -> 11 us  [exchange(): lax.all_to_all(blocks, TP + ('x',), split_axis=0, concat_axis=0, tiled=Tr...]
    all_to_all x1, blocking collectives: 13.4 us -> 15 us  [body(): lax.all_to_all(attended, ('x', 'two'), split_axis=0, concat_axis=0, tiled...]
  transfers between devices with their start and end apart: 9 -> 9, of which waited for: 5 -> 4; matrix products, arithmetic and copies ran while one was open for 0% -> 0% of each run, Pallas kernels for 3% -> 4%
where the time goes in v6:
time: 143 us; the launch traced here: 142 us
  blocking collectives  60 us (42%)
  starting transfers between devices  49.3 us (34%)
  waiting for transfers between devices  18.7 us (13%)
  Pallas kernels  9.81 us (7%)
  local copies, waits for them, and re-layouts  2.89 us (2%)
    all_gather x2, blocking collectives, body(): own = lax.all_gather(lax.all_gather(shard, 'pair'), 'quad')  27.9 us
    all_to_all x2, starting transfers between devices, exchange(): lax.all_to_all(blocks, TP + ('x',), split_axis=0, concat_axis=0, tiled=Tr...  22.8 us
    psum x1, blocking collectives, body(): stat = lax.psum(stat[:, :RESP], TP)  17.1 us
    all_to_all x1, blocking collectives, body(): lax.all_to_all(attended, ('x', 'two'), split_axis=0, concat_axis=0, tiled...  15 us
    all_to_all x2, waiting for transfers between devices, exchange(): lax.all_to_all(blocks, TP + ('x',), split_axis=0, concat_axis=0, tiled=Tr...  11 us
    ppermute x3, starting transfers between devices, body(): lax.ppermute(parts[s], 'x', [(i, (i + s) % NX) for i in range(NX)])  10.4 us
    all_to_all x1, starting transfers between devices, body(): lax.all_to_all(placed, ('x',) + Z + ('core',), split_axis=0, concat_axis=...  7.67 us
    all_to_all x1, starting transfers between devices, body(): lax.all_to_all(out_sent, Z + ('two',), split_axis=0, concat_axis=0, tiled...  4.55 us
  transfers between devices with their start and end apart: 9, of which 4 were waited for; matrix products, arithmetic and copies ran while one was open for 0% of the time, Pallas kernels for 4%

profile of v6, /device:TPU:6, one launch (start us, length us, event | category | flops | bytes accessed | tf_op | source)
XLA Modules:
  0.0 142.2 jit_solution(17414602416227539934)
XLA Ops:
  0.6 2.5 %prepare.1 = (bf16[32,128,128]{2,1,0:T(8,128)(2,1)}, bf16[64,768]{1,0:T(8,128)(2,1)}, bf16[16,64,512]{2,1,0:T(8,128)(2,1)}) custom-call(bf16[128,512]{1,0:T(8,128)(2,1)} %rows_ref.1, bf16[64,512]{1,0:T(8,128)(2,1)} %query.1, bf16[64,256]{1,0:T(8,128)(2,1)} %key.1, bf16[64,256]{1,0:T(8,128)(2,1)} %value.1, bf16[64,512]{1,0:T(8,128)(2,1)} %bitcast.21), custom_call_target="tpu_custom_call" | custom-call | bytes 4194304 | tf_op jit(solution)/shard_map/prepare/pallas_call | solution.py:275
  3.1 12.8 %all-to-all-start = ((bf16[32,128,128]{2,1,0:T(8,128)(2,1)}), bf16[32,128,128]{2,1,0:T(8,128)(2,1)S(1)}, u32[]{:S(2)}, u32[]{:S(2)}) async-start(bf16[32,128,128]{2,1,0:T(8,128)(2,1)} %get-tuple-element.23), calls=%async_computation | async-start | bytes 2097152 | tf_op jit(solution)/shard_map/all_to_all | solution.py:250
  15.9 5.3 %all-gather = bf16[128,768]{1,0:T(8,128)(2,1)S(1)} all-gather(bf16[64,768]{1,0:T(8,128)(2,1)S(1)} %copy-done.4), channel_id=2, replica_groups=mesh['four'=4,'two'=2,'quad'=4,'pair'=2,'x'=4,'core'=2] {'pair'}, dimensions={0}, use_global_device_ids=true | all-gather | bytes 294912 | tf_op jit(solution)/shard_map/all_gather | solution.py:294
  21.2 22.6 %all-gather.1.own_ref = bf16[8,64,768]{2,1,0:T(8,128)(2,1)S(1)} all-gather(bf16[2,64,768]{2,1,0:T(8,128)(2,1)S(1)} %bitcast.19), channel_id=3, replica_groups=mesh['four'=4,'two'=2,'quad'=4,'pair'=2,'x'=4,'core'=2] {'quad'}, dimensions={0}, use_global_device_ids=true | all-gather | bytes 983040 | tf_op jit(solution)/shard_map/all_gather | solution.py:294
  43.8 4.5 %all-to-all-start.1 = ((bf16[16,64,512]{2,1,0:T(8,128)(2,1)}), bf16[16,64,512]{2,1,0:T(8,128)(2,1)S(1)}, u32[]{:S(2)}, u32[]{:S(2)}) async-start(bf16[16,64,512]{2,1,0:T(8,128)(2,1)} %get-tuple-element.25), calls=%async_computation.1 | async-start | bytes 2097152 | tf_op jit(solution)/shard_map/all_to_all | solution.py:300
  48.4 1.9 %collective-permute-start = (bf16[8,64,768]{2,1,0:T(8,128)(2,1)S(1)}, bf16[8,64,768]{2,1,0:T(8,128)(2,1)}, u32[]{:S(2)}, u32[]{:S(2)}) collective-permute-start(bf16[8,64,768]{2,1,0:T(8,128)(2,1)S(1)} %all-gather.1.own_ref), channel_id=1, source_target_pairs={{0,1},{1,0},{2,3},{3,2},{4,5},{5,4},{6,7},{7,6},{8,9},{9,8},{10,11... | collective-permute-start | bytes 2359304 | tf_op jit(solution)/shard_map/ppermute | solution.py:296
  50.4 2.3 %collective-permute-done.other_ref = bf16[8,64,768]{2,1,0:T(8,128)(2,1)} collective-permute-done((bf16[8,64,768]{2,1,0:T(8,128)(2,1)S(1)}, bf16[8,64,768]{2,1,0:T(8,128)(2,1)}, u32[]{:S(2)}, u32[]{:S(2)}) %collective-permute-start) | collective-permute-done | bytes 786464 | tf_op jit(solution)/shard_map/ppermute | solution.py:296
  52.7 2.3 %project.1 = (bf16[784,128]{1,0:T(8,128)(2,1)S(1)}, bf16[784,128]{1,0:T(8,128)(2,1)S(1)}, bf16[784,128]{1,0:T(8,128)(2,1)S(1)}, bf16[784,128]{1,0:T(8,128)(2,1)S(1)}) custom-call(bf16[32,128,128]{2,1,0:T(8,128)(2,1)S(1)} %all-to-all-done.x_ref, bf16[8,64,768]{2,1,0:T(8,128)(2,1)S(1)} %all-gather.1.own_ref, ...), custom_call_target="tpu_custom_call" | custom-call | flops 805306368 | bytes 4194304 | tf_op jit(solution)/shard_map/project/pallas_call | solution.py:303
  55.0 3.4 %collective-permute-start.1 = (bf16[784,128]{1,0:T(8,128)(2,1)S(1)}, bf16[784,128]{1,0:T(8,128)(2,1)S(1)}, u32[]{:S(2)}, u32[]{:S(2)}) collective-permute-start(bf16[784,128]{1,0:T(8,128)(2,1)S(1)} %get-tuple-element.30), channel_id=1, source_target_pairs={{0,4},{2,6},{4,0},{6,2},{1,5},{3,7},{5,1},{7,3},{8,12},{10,14},{12... | collective-permute-start | bytes 602120 | tf_op jit(solution)/shard_map/ppermute | solution.py:312
  58.4 2.6 %collective-permute-start.2 = (bf16[784,128]{1,0:T(8,128)(2,1)S(1)}, bf16[784,128]{1,0:T(8,128)(2,1)S(1)}, u32[]{:S(2)}, u32[]{:S(2)}) collective-permute-start(bf16[784,128]{1,0:T(8,128)(2,1)S(1)} %get-tuple-element.31), channel_id=1, source_target_pairs={{0,6},{2,0},{4,2},{6,4},{1,7},{3,1},{5,3},{7,5},{8,14},{10,8},{12,... | collective-permute-start | bytes 602120 | tf_op jit(solution)/shard_map/ppermute | solution.py:312
  61.0 4.4 %collective-permute-start.3 = (bf16[784,128]{1,0:T(8,128)(2,1)S(1)}, bf16[784,128]{1,0:T(8,128)(2,1)S(1)}, u32[]{:S(2)}, u32[]{:S(2)}) collective-permute-start(bf16[784,128]{1,0:T(8,128)(2,1)S(1)} %get-tuple-element.32), channel_id=1, source_target_pairs={{0,2},{2,4},{4,6},{6,0},{1,3},{3,5},{5,7},{7,1},{8,10},{10,12},{12... | collective-permute-start | bytes 602120 | tf_op jit(solution)/shard_map/ppermute | solution.py:312
  66.2 0.9 tables.1
  67.1 2.6 %collective-permute-done.2.part2 = bf16[784,128]{1,0:T(8,128)(2,1)S(1)} collective-permute-done((bf16[784,128]{1,0:T(8,128)(2,1)S(1)}, bf16[784,128]{1,0:T(8,128)(2,1)S(1)}, u32[]{:S(2)}, u32[]{:S(2)}) %collective-permute-start.2) | collective-permute-done | bytes 200736 | tf_op jit(solution)/shard_map/ppermute | solution.py:312
  69.7 1.8 %attend.1 = bf16[8,64,512]{2,1,0:T(8,128)(2,1)S(1)} custom-call(s32[1,8]{1,0:T(1,128)S(1)} %copy-done.2, bf16[784,128]{1,0:T(8,128)(2,1)S(1)} %get-tuple-element.29.part0, bf16[784,128]{1,0:T(8,128)(2,1)S(1)} %collective-permute-done.1.part1, bf16[784,128]{1,0:T(8,128)(2,1)S(1)} %collective-permute-done.2.part2, ...), custom_call_target="tpu_custom_call" | custom-call | flops 33554432 | bytes 4194304 | tf_op jit(solution)/shard_map/attend/pallas_call | solution.py:327
  71.6 2.7 %all-to-all-done.1.own_ref = bf16[16,64,512]{2,1,0:T(8,128)(2,1)S(1)} async-done(((bf16[16,64,512]{2,1,0:T(8,128)(2,1)}), bf16[16,64,512]{2,1,0:T(8,128)(2,1)S(1)}, u32[]{:S(2)}, u32[]{:S(2)}) %all-to-all-start.1) | async-done | bytes 1048608 | tf_op jit(solution)/shard_map/all_to_all | solution.py:300
  74.3 1.9 %collective-permute-start.4 = (bf16[16,64,512]{2,1,0:T(8,128)(2,1)S(1)}, bf16[16,64,512]{2,1,0:T(8,128)(2,1)S(1)}, u32[]{:S(2)}, u32[]{:S(2)}) collective-permute-start(bf16[16,64,512]{2,1,0:T(8,128)(2,1)S(1)} %all-to-all-done.1.own_ref), channel_id=1, source_target_pairs={{0,1},{1,0},{2,3},{3,2},{4,5},{5,4},{6,7},{7,6},{8,9},{9,8},{10,11... | collective-permute-start | bytes 3145736 | tf_op jit(solution)/shard_map/ppermute | solution.py:336
  76.2 15.0 %all_to_all.29.x_ref = bf16[8,64,512]{2,1,0:T(8,128)(2,1)S(1)} all-to-all(bf16[8,64,512]{2,1,0:T(8,128)(2,1)S(1)} %attend.1), channel_id=1, replica_groups=mesh['four'=4,'two'=2,'quad'=4,'pair'=2,'x'=4,'core'=2] {'x','two'}, dimensions={0} | all-to-all | bytes 1048576 | tf_op jit(solution)/shard_map/all_to_all | solution.py:338
  91.2 1.5 %output.1 = bf16[32,64,128]{2,1,0:T(8,128)(2,1)} custom-call(bf16[8,64,512]{2,1,0:T(8,128)(2,1)S(1)} %all_to_all.29.x_ref, bf16[16,64,512]{2,1,0:T(8,128)(2,1)S(1)} %all-to-all-done.1.own_ref, bf16[16,64,512]{2,1,0:T(8,128)(2,1)S(1)} %collective-permute-done.4.other_ref), custom_call_target="tpu_custom_call" | custom-call | flops 536870912 | bytes 4194304 | tf_op jit(solution)/shard_map/output/pallas_call | solution.py:339
  92.8 10.0 %all-to-all-start.3 = ((bf16[32,64,128]{2,1,0:T(8,128)(2,1)}), bf16[32,64,128]{2,1,0:T(8,128)(2,1)S(1)}, u32[]{:S(2)}, u32[]{:S(2)}) async-start(bf16[32,64,128]{2,1,0:T(8,128)(2,1)} %output.1), calls=%async_computation.3 | async-start | bytes 1048576 | tf_op jit(solution)/shard_map/all_to_all | solution.py:250
  103.5 11.0 %all-to-all-done.3.parts_ref = bf16[32,64,128]{2,1,0:T(8,128)(2,1)S(1)} async-done(((bf16[32,64,128]{2,1,0:T(8,128)(2,1)}), bf16[32,64,128]{2,1,0:T(8,128)(2,1)S(1)}, u32[]{:S(2)}, u32[]{:S(2)}) %all-to-all-start.3) | async-done | bytes 524320 | tf_op jit(solution)/shard_map/all_to_all | solution.py:250
  114.6 0.8 layer.1
  115.4 0.7 all_to_all.22
  116.1 7.7 %all-to-all-start.4 = ((bf16[64,2,512]{2,1,0:T(2,128)(2,1)}), bf16[64,2,512]{2,1,0:T(2,128)(2,1)S(1)}, u32[]{:S(2)}, u32[]{:S(2)}) async-start(bf16[64,2,512]{2,1,0:T(2,128)(2,1)} %all_to_all.22), calls=%async_computation.4 | async-start | bytes 262144 | tf_op jit(solution)/shard_map/all_to_all | solution.py:365
  123.8 17.1 %psum.7 = f32[2,8]{1,0:T(2,128)S(1)} all-reduce(f32[2,8]{1,0:T(2,128)S(1)} %bitcast.17), channel_id=1, replica_groups=mesh['four'=4,'two'=2,'quad'=4,'pair'=2,'x'=4,'core'=2] {'four','two'}, use_global_device_ids=true, to_apply=%region_0.0 | all-reduce | flops 16 | bytes 128 | tf_op jit(solution)/shard_map/psum | solution.py:367
  (29 shorter events, 2.8 us)
Async XLA Ops:
  0.6 49.7 %copy-start = (bf16[4096]{0:T(1024)(128)(2,1)S(1)}, bf16[4096]{0:T(1024)(128)(2,1)}, u32[]{:S(2)}) copy-start(bf16[4096]{0:T(1024)(128)(2,1)} %param.13) | copy-start | bytes 24580
  3.1 12.8 %copy-start.4 = (bf16[64,768]{1,0:T(8,128)(2,1)S(1)}, bf16[64,768]{1,0:T(8,128)(2,1)}, u32[]{:S(2)}) copy-start(bf16[64,768]{1,0:T(8,128)(2,1)} %get-tuple-element.24) | copy-start | bytes 294916
  3.1 40.7 %all-to-all-start = ((bf16[32,128,128]{2,1,0:T(8,128)(2,1)}), bf16[32,128,128]{2,1,0:T(8,128)(2,1)S(1)}, u32[]{:S(2)}, u32[]{:S(2)}) async-start(bf16[32,128,128]{2,1,0:T(8,128)(2,1)} %get-tuple-element.23), calls=%async_computation | async-start | bytes 2097152 | tf_op jit(solution)/shard_map/all_to_all | solution.py:250
  43.8 30.4 %all-to-all-start.1 = ((bf16[16,64,512]{2,1,0:T(8,128)(2,1)}), bf16[16,64,512]{2,1,0:T(8,128)(2,1)S(1)}, u32[]{:S(2)}, u32[]{:S(2)}) async-start(bf16[16,64,512]{2,1,0:T(8,128)(2,1)} %get-tuple-element.25), calls=%async_computation.1 | async-start | bytes 2097152 | tf_op jit(solution)/shard_map/all_to_all | solution.py:300
  48.4 4.3 %collective-permute-start = (bf16[8,64,768]{2,1,0:T(8,128)(2,1)S(1)}, bf16[8,64,768]{2,1,0:T(8,128)(2,1)}, u32[]{:S(2)}, u32[]{:S(2)}) collective-permute-start(bf16[8,64,768]{2,1,0:T(8,128)(2,1)S(1)} %all-gather.1.own_ref), channel_id=1, source_target_pairs={{0,1},{1,0},{2,3},{3,2},{4,5},{5,4},{6,7},{7,6},{8,9},{9,8},{10,11... | collective-permute-start | bytes 2359304 | tf_op jit(solution)/shard_map/ppermute | solution.py:296
  55.0 12.1 %collective-permute-start.1 = (bf16[784,128]{1,0:T(8,128)(2,1)S(1)}, bf16[784,128]{1,0:T(8,128)(2,1)S(1)}, u32[]{:S(2)}, u32[]{:S(2)}) collective-permute-start(bf16[784,128]{1,0:T(8,128)(2,1)S(1)} %get-tuple-element.30), channel_id=1, source_target_pairs={{0,4},{2,6},{4,0},{6,2},{1,5},{3,7},{5,1},{7,3},{8,12},{10,14},{12... | collective-permute-start | bytes 602120 | tf_op jit(solution)/shard_map/ppermute | solution.py:312
  58.4 11.4 %collective-permute-start.2 = (bf16[784,128]{1,0:T(8,128)(2,1)S(1)}, bf16[784,128]{1,0:T(8,128)(2,1)S(1)}, u32[]{:S(2)}, u32[]{:S(2)}) collective-permute-start(bf16[784,128]{1,0:T(8,128)(2,1)S(1)} %get-tuple-element.31), channel_id=1, source_target_pairs={{0,6},{2,0},{4,2},{6,4},{1,7},{3,1},{5,3},{7,5},{8,14},{10,8},{12,... | collective-permute-start | bytes 602120 | tf_op jit(solution)/shard_map/ppermute | solution.py:312
  61.0 8.7 %collective-permute-start.3 = (bf16[784,128]{1,0:T(8,128)(2,1)S(1)}, bf16[784,128]{1,0:T(8,128)(2,1)S(1)}, u32[]{:S(2)}, u32[]{:S(2)}) collective-permute-start(bf16[784,128]{1,0:T(8,128)(2,1)S(1)} %get-tuple-element.32), channel_id=1, source_target_pairs={{0,2},{2,4},{4,6},{6,0},{1,3},{3,5},{5,7},{7,1},{8,10},{10,12},{12... | collective-permute-start | bytes 602120 | tf_op jit(solution)/shard_map/ppermute | solution.py:312
  65.5 0.7 copy-start.2
  65.5 0.7 copy-start.3
  74.3 17.0 %collective-permute-start.4 = (bf16[16,64,512]{2,1,0:T(8,128)(2,1)S(1)}, bf16[16,64,512]{2,1,0:T(8,128)(2,1)S(1)}, u32[]{:S(2)}, u32[]{:S(2)}) collective-permute-start(bf16[16,64,512]{2,1,0:T(8,128)(2,1)S(1)} %all-to-all-done.1.own_ref), channel_id=1, source_target_pairs={{0,1},{1,0},{2,3},{3,2},{4,5},{5,4},{6,7},{7,6},{8,9},{9,8},{10,11... | collective-permute-start | bytes 3145736 | tf_op jit(solution)/shard_map/ppermute | solution.py:336
  92.8 10.1 %copy-start.5 = (bf16[512]{0:T(512)(128)(2,1)S(1)}, bf16[512]{0:T(512)(128)(2,1)}, u32[]{:S(2)}) copy-start(bf16[512]{0:T(512)(128)(2,1)} %param.18) | copy-start | bytes 3076
  92.8 21.8 %copy-start.1 = (bf16[128,512]{1,0:T(8,128)(2,1)S(1)}, bf16[128,512]{1,0:T(8,128)(2,1)}, u32[]{:S(2)}) copy-start(bf16[128,512]{1,0:T(8,128)(2,1)} %rows_ref.1) | copy-start | bytes 393220
  92.8 21.8 %all-to-all-start.3 = ((bf16[32,64,128]{2,1,0:T(8,128)(2,1)}), bf16[32,64,128]{2,1,0:T(8,128)(2,1)S(1)}, u32[]{:S(2)}, u32[]{:S(2)}) async-start(bf16[32,64,128]{2,1,0:T(8,128)(2,1)} %output.1), calls=%async_computation.3 | async-start | bytes 1048576 | tf_op jit(solution)/shard_map/all_to_all | solution.py:250
  102.9 0.7 copy-start.6
  116.1 25.3 %all-to-all-start.4 = ((bf16[64,2,512]{2,1,0:T(2,128)(2,1)}), bf16[64,2,512]{2,1,0:T(2,128)(2,1)S(1)}, u32[]{:S(2)}, u32[]{:S(2)}) async-start(bf16[64,2,512]{2,1,0:T(2,128)(2,1)} %all_to_all.22), calls=%async_computation.4 | async-start | bytes 262144 | tf_op jit(solution)/shard_map/all_to_all | solution.py:365

commit v7 on v6

--- a/solution.py
+++ b/solution.py
@@ -114,24 +114,27 @@
 
 
 def project_kernel(
-    x_ref, own_ref, other_ref, gain_ref, out0, out1, out2, out3, xs_ref, w_ref
+    x_ref, own_ref, other_ref, gain_ref, out0, out1, out2, out3, xs_ref
 ):
     first = lax.axis_index("core") == 0
     outs = (out0, out1, out2, out3)
-    for t in range(NT):
-        own, other = own_ref[t], other_ref[t]
-        w_ref[t * BLK : t * BLK + BLK // 2, :] = jnp.where(first, own, other)
-        w_ref[t * BLK + BLK // 2 : (t + 1) * BLK, :] = jnp.where(first, other, own)
+    left = iota((ROWS, BLK), 1) < BLK // 2
     eye = eye_mask()
     for g in range(NX):
         square = jnp.zeros((ROWS, BLK), f32)
         group = lax.rem(lax.axis_index("x") + g, NX)
-        for t in range(NT):
-            wide = x_ref[AT[t] * NX + group].astype(f32)
-            square = square + wide * wide
-            xs_ref[g * ROWS : (g + 1) * ROWS, t * BLK : (t + 1) * BLK] = (
-                wide * gain_ref[t : t + 1, :].astype(f32)
-            ).astype(bf16)
+        for t in range(0, NT, 2):
+            pair = []
+            for u in (t, t + 1):
+                wide = x_ref[AT[u] * NX + group].astype(f32)
+                square = square + wide * wide
+                pair.append(wide * gain_ref[u : u + 1, :].astype(f32))
+            zero = jnp.where(left, pair[0], pltpu.roll(pair[1], BLK // 2, 1))
+            one = jnp.where(left, pltpu.roll(pair[0], BLK // 2, 1), pair[1])
+            rows, at = slice(g * ROWS, (g + 1) * ROWS), t * BLK // 2
+            half = NT * BLK // 2
+            xs_ref[rows, at : at + BLK] = jnp.where(first, zero, one).astype(bf16)
+            xs_ref[rows, half + at : half + at + BLK] = jnp.where(first, one, zero).astype(bf16)
         total = jnp.sum(square, axis=1, keepdims=True)
         line = jnp.sum(jnp.where(eye, total, 0.0), axis=0, keepdims=True)
         high = line.astype(bf16).astype(f32)
@@ -141,7 +144,12 @@
         outs[g][PW:, :] = tail
     for n in range(PW // 256):
         cols = slice(n * 256, (n + 1) * 256)
-        part = jnp.dot(xs_ref[...], w_ref[:, cols], preferred_element_type=f32)
+        half = NT * BLK // 2
+        part = jnp.dot(
+            xs_ref[:, :half], own_ref[:, :, cols].reshape(half, 256), preferred_element_type=f32
+        ) + jnp.dot(
+            xs_ref[:, half:], other_ref[:, :, cols].reshape(half, 256), preferred_element_type=f32
+        )
         for g in range(NX):
             rows = part[g * ROWS : (g + 1) * ROWS].astype(bf16)
             outs[g][n * 256 : n * 256 + ROWS, :] = rows[:, :HD]
@@ -304,7 +312,7 @@
         project_kernel,
         (block,) * NX,
         [VMEM] * 4,
-        [pltpu.VMEM((NX * ROWS, NT * BLK), bf16), pltpu.VMEM((NT * BLK, PW), bf16)],
+        [pltpu.VMEM((NX * ROWS, NT * BLK), bf16)],
         flops=2 * 512 * 1024 * 768,
         name="project",
     )(tokens, own, other, gain)

time: 143 us -> 143 us (level)
  no operation moved by 1% of the time
where the time goes in v7:
time: 143 us; the launch traced here: 142 us
  blocking collectives  60 us (42%)
  starting transfers between devices  49.5 us (35%)
  waiting for transfers between devices  18.6 us (13%)
  Pallas kernels  9.94 us (7%)
  local copies, waits for them, and re-layouts  2.89 us (2%)
    all_gather x2, blocking collectives, body(): own = lax.all_gather(lax.all_gather(shard, 'pair'), 'quad')  27.9 us
    all_to_all x2, starting transfers between devices, exchange(): lax.all_to_all(blocks, TP + ('x',), split_axis=0, concat_axis=0, tiled=Tr...  22.8 us
    psum x1, blocking collectives, body(): stat = lax.psum(stat[:, :RESP], TP)  17 us
    all_to_all x1, blocking collectives, body(): lax.all_to_all(attended, ('x', 'two'), split_axis=0, concat_axis=0, tiled...  15 us
    all_to_all x2, waiting for transfers between devices, exchange(): lax.all_to_all(blocks, TP + ('x',), split_axis=0, concat_axis=0, tiled=Tr...  11 us
    ppermute x3, starting transfers between devices, body(): lax.ppermute(parts[s], 'x', [(i, (i + s) % NX) for i in range(NX)])  10.4 us
    all_to_all x1, starting transfers between devices, body(): lax.all_to_all(placed, ('x',) + Z + ('core',), split_axis=0, concat_axis=...  7.86 us
    all_to_all x1, starting transfers between devices, body(): lax.all_to_all(out_sent, Z + ('two',), split_axis=0, concat_axis=0, tiled...  4.55 us
  transfers between devices with their start and end apart: 9, of which 4 were waited for; matrix products, arithmetic and copies ran while one was open for 0% of the time, Pallas kernels for 4%

profile of v7, /device:TPU:6, one launch (start us, length us, event | category | flops | bytes accessed | tf_op | source)
XLA Modules:
  0.0 142.3 jit_solution(5748776258368796555)
XLA Ops:
  0.6 2.5 %prepare.1 = (bf16[32,128,128]{2,1,0:T(8,128)(2,1)}, bf16[64,768]{1,0:T(8,128)(2,1)}, bf16[16,64,512]{2,1,0:T(8,128)(2,1)}) custom-call(bf16[128,512]{1,0:T(8,128)(2,1)} %rows_ref.1, bf16[64,512]{1,0:T(8,128)(2,1)} %query.1, bf16[64,256]{1,0:T(8,128)(2,1)} %key.1, bf16[64,256]{1,0:T(8,128)(2,1)} %value.1, bf16[64,512]{1,0:T(8,128)(2,1)} %bitcast.21), custom_call_target="tpu_custom_call" | custom-call | bytes 4194304 | tf_op jit(solution)/shard_map/prepare/pallas_call | solution.py:283
  3.1 12.8 %all-to-all-start = ((bf16[32,128,128]{2,1,0:T(8,128)(2,1)}), bf16[32,128,128]{2,1,0:T(8,128)(2,1)S(1)}, u32[]{:S(2)}, u32[]{:S(2)}) async-start(bf16[32,128,128]{2,1,0:T(8,128)(2,1)} %get-tuple-element.23), calls=%async_computation | async-start | bytes 2097152 | tf_op jit(solution)/shard_map/all_to_all | solution.py:258
  15.9 5.3 %all-gather = bf16[128,768]{1,0:T(8,128)(2,1)S(1)} all-gather(bf16[64,768]{1,0:T(8,128)(2,1)S(1)} %copy-done.4), channel_id=2, replica_groups=mesh['four'=4,'two'=2,'quad'=4,'pair'=2,'x'=4,'core'=2] {'pair'}, dimensions={0}, use_global_device_ids=true | all-gather | bytes 294912 | tf_op jit(solution)/shard_map/all_gather | solution.py:302
  21.2 22.6 %all-gather.1.own_ref = bf16[8,64,768]{2,1,0:T(8,128)(2,1)S(1)} all-gather(bf16[2,64,768]{2,1,0:T(8,128)(2,1)S(1)} %bitcast.19), channel_id=3, replica_groups=mesh['four'=4,'two'=2,'quad'=4,'pair'=2,'x'=4,'core'=2] {'quad'}, dimensions={0}, use_global_device_ids=true | all-gather | bytes 983040 | tf_op jit(solution)/shard_map/all_gather | solution.py:302
  43.8 4.5 %all-to-all-start.1 = ((bf16[16,64,512]{2,1,0:T(8,128)(2,1)}), bf16[16,64,512]{2,1,0:T(8,128)(2,1)S(1)}, u32[]{:S(2)}, u32[]{:S(2)}) async-start(bf16[16,64,512]{2,1,0:T(8,128)(2,1)} %get-tuple-element.25), calls=%async_computation.1 | async-start | bytes 2097152 | tf_op jit(solution)/shard_map/all_to_all | solution.py:308
  48.4 1.9 %collective-permute-start = (bf16[8,64,768]{2,1,0:T(8,128)(2,1)S(1)}, bf16[8,64,768]{2,1,0:T(8,128)(2,1)}, u32[]{:S(2)}, u32[]{:S(2)}) collective-permute-start(bf16[8,64,768]{2,1,0:T(8,128)(2,1)S(1)} %all-gather.1.own_ref), channel_id=1, source_target_pairs={{0,1},{1,0},{2,3},{3,2},{4,5},{5,4},{6,7},{7,6},{8,9},{9,8},{10,11... | collective-permute-start | bytes 2359304 | tf_op jit(solution)/shard_map/ppermute | solution.py:304
  50.4 2.3 %collective-permute-done.other_ref = bf16[8,64,768]{2,1,0:T(8,128)(2,1)} collective-permute-done((bf16[8,64,768]{2,1,0:T(8,128)(2,1)S(1)}, bf16[8,64,768]{2,1,0:T(8,128)(2,1)}, u32[]{:S(2)}, u32[]{:S(2)}) %collective-permute-start) | collective-permute-done | bytes 786464 | tf_op jit(solution)/shard_map/ppermute | solution.py:304
  52.7 2.4 %project.1 = (bf16[784,128]{1,0:T(8,128)(2,1)S(1)}, bf16[784,128]{1,0:T(8,128)(2,1)S(1)}, bf16[784,128]{1,0:T(8,128)(2,1)S(1)}, bf16[784,128]{1,0:T(8,128)(2,1)S(1)}) custom-call(bf16[32,128,128]{2,1,0:T(8,128)(2,1)S(1)} %all-to-all-done.x_ref, bf16[8,64,768]{2,1,0:T(8,128)(2,1)S(1)} %all-gather.1.own_ref, ...), custom_call_target="tpu_custom_call" | custom-call | flops 805306368 | bytes 4194304 | tf_op jit(solution)/shard_map/project/pallas_call | solution.py:311
  55.1 3.4 %collective-permute-start.1 = (bf16[784,128]{1,0:T(8,128)(2,1)S(1)}, bf16[784,128]{1,0:T(8,128)(2,1)S(1)}, u32[]{:S(2)}, u32[]{:S(2)}) collective-permute-start(bf16[784,128]{1,0:T(8,128)(2,1)S(1)} %get-tuple-element.30), channel_id=1, source_target_pairs={{0,4},{2,6},{4,0},{6,2},{1,5},{3,7},{5,1},{7,3},{8,12},{10,14},{12... | collective-permute-start | bytes 602120 | tf_op jit(solution)/shard_map/ppermute | solution.py:320
  58.5 2.6 %collective-permute-start.2 = (bf16[784,128]{1,0:T(8,128)(2,1)S(1)}, bf16[784,128]{1,0:T(8,128)(2,1)S(1)}, u32[]{:S(2)}, u32[]{:S(2)}) collective-permute-start(bf16[784,128]{1,0:T(8,128)(2,1)S(1)} %get-tuple-element.31), channel_id=1, source_target_pairs={{0,6},{2,0},{4,2},{6,4},{1,7},{3,1},{5,3},{7,5},{8,14},{10,8},{12,... | collective-permute-start | bytes 602120 | tf_op jit(solution)/shard_map/ppermute | solution.py:320
  61.2 4.4 %collective-permute-start.3 = (bf16[784,128]{1,0:T(8,128)(2,1)S(1)}, bf16[784,128]{1,0:T(8,128)(2,1)S(1)}, u32[]{:S(2)}, u32[]{:S(2)}) collective-permute-start(bf16[784,128]{1,0:T(8,128)(2,1)S(1)} %get-tuple-element.32), channel_id=1, source_target_pairs={{0,2},{2,4},{4,6},{6,0},{1,3},{3,5},{5,7},{7,1},{8,10},{10,12},{12... | collective-permute-start | bytes 602120 | tf_op jit(solution)/shard_map/ppermute | solution.py:320
  66.3 0.9 tables.1
  67.3 2.6 %collective-permute-done.2.part2 = bf16[784,128]{1,0:T(8,128)(2,1)S(1)} collective-permute-done((bf16[784,128]{1,0:T(8,128)(2,1)S(1)}, bf16[784,128]{1,0:T(8,128)(2,1)S(1)}, u32[]{:S(2)}, u32[]{:S(2)}) %collective-permute-start.2) | collective-permute-done | bytes 200736 | tf_op jit(solution)/shard_map/ppermute | solution.py:320
  69.9 1.8 %attend.1 = bf16[8,64,512]{2,1,0:T(8,128)(2,1)S(1)} custom-call(s32[1,8]{1,0:T(1,128)S(1)} %copy-done.2, bf16[784,128]{1,0:T(8,128)(2,1)S(1)} %get-tuple-element.29.part0, bf16[784,128]{1,0:T(8,128)(2,1)S(1)} %collective-permute-done.1.part1, bf16[784,128]{1,0:T(8,128)(2,1)S(1)} %collective-permute-done.2.part2, ...), custom_call_target="tpu_custom_call" | custom-call | flops 33554432 | bytes 4194304 | tf_op jit(solution)/shard_map/attend/pallas_call | solution.py:335
  71.7 2.6 %all-to-all-done.1.own_ref = bf16[16,64,512]{2,1,0:T(8,128)(2,1)S(1)} async-done(((bf16[16,64,512]{2,1,0:T(8,128)(2,1)}), bf16[16,64,512]{2,1,0:T(8,128)(2,1)S(1)}, u32[]{:S(2)}, u32[]{:S(2)}) %all-to-all-start.1) | async-done | bytes 1048608 | tf_op jit(solution)/shard_map/all_to_all | solution.py:308
  74.3 1.9 %collective-permute-start.4 = (bf16[16,64,512]{2,1,0:T(8,128)(2,1)S(1)}, bf16[16,64,512]{2,1,0:T(8,128)(2,1)S(1)}, u32[]{:S(2)}, u32[]{:S(2)}) collective-permute-start(bf16[16,64,512]{2,1,0:T(8,128)(2,1)S(1)} %all-to-all-done.1.own_ref), channel_id=1, source_target_pairs={{0,1},{1,0},{2,3},{3,2},{4,5},{5,4},{6,7},{7,6},{8,9},{9,8},{10,11... | collective-permute-start | bytes 3145736 | tf_op jit(solution)/shard_map/ppermute | solution.py:344
  76.2 15.0 %all_to_all.29.x_ref = bf16[8,64,512]{2,1,0:T(8,128)(2,1)S(1)} all-to-all(bf16[8,64,512]{2,1,0:T(8,128)(2,1)S(1)} %attend.1), channel_id=1, replica_groups=mesh['four'=4,'two'=2,'quad'=4,'pair'=2,'x'=4,'core'=2] {'x','two'}, dimensions={0} | all-to-all | bytes 1048576 | tf_op jit(solution)/shard_map/all_to_all | solution.py:346
  91.2 1.5 %output.1 = bf16[32,64,128]{2,1,0:T(8,128)(2,1)} custom-call(bf16[8,64,512]{2,1,0:T(8,128)(2,1)S(1)} %all_to_all.29.x_ref, bf16[16,64,512]{2,1,0:T(8,128)(2,1)S(1)} %all-to-all-done.1.own_ref, bf16[16,64,512]{2,1,0:T(8,128)(2,1)S(1)} %collective-permute-done.4.other_ref), custom_call_target="tpu_custom_call" | custom-call | flops 536870912 | bytes 4194304 | tf_op jit(solution)/shard_map/output/pallas_call | solution.py:347
  92.8 10.0 %all-to-all-start.3 = ((bf16[32,64,128]{2,1,0:T(8,128)(2,1)}), bf16[32,64,128]{2,1,0:T(8,128)(2,1)S(1)}, u32[]{:S(2)}, u32[]{:S(2)}) async-start(bf16[32,64,128]{2,1,0:T(8,128)(2,1)} %output.1), calls=%async_computation.3 | async-start | bytes 1048576 | tf_op jit(solution)/shard_map/all_to_all | solution.py:258
  103.5 11.0 %all-to-all-done.3.parts_ref = bf16[32,64,128]{2,1,0:T(8,128)(2,1)S(1)} async-done(((bf16[32,64,128]{2,1,0:T(8,128)(2,1)}), bf16[32,64,128]{2,1,0:T(8,128)(2,1)S(1)}, u32[]{:S(2)}, u32[]{:S(2)}) %all-to-all-start.3) | async-done | bytes 524320 | tf_op jit(solution)/shard_map/all_to_all | solution.py:258
  114.6 0.8 layer.1
  115.4 0.7 all_to_all.22
  116.1 7.9 %all-to-all-start.4 = ((bf16[64,2,512]{2,1,0:T(2,128)(2,1)}), bf16[64,2,512]{2,1,0:T(2,128)(2,1)S(1)}, u32[]{:S(2)}, u32[]{:S(2)}) async-start(bf16[64,2,512]{2,1,0:T(2,128)(2,1)} %all_to_all.22), calls=%async_computation.4 | async-start | bytes 262144 | tf_op jit(solution)/shard_map/all_to_all | solution.py:373
  124.0 17.0 %psum.7 = f32[2,8]{1,0:T(2,128)S(1)} all-reduce(f32[2,8]{1,0:T(2,128)S(1)} %bitcast.17), channel_id=1, replica_groups=mesh['four'=4,'two'=2,'quad'=4,'pair'=2,'x'=4,'core'=2] {'four','two'}, use_global_device_ids=true, to_apply=%region_0.0 | all-reduce | flops 16 | bytes 128 | tf_op jit(solution)/shard_map/psum | solution.py:375
  (29 shorter events, 2.8 us)
Async XLA Ops:
  0.6 49.7 %copy-start = (bf16[4096]{0:T(1024)(128)(2,1)S(1)}, bf16[4096]{0:T(1024)(128)(2,1)}, u32[]{:S(2)}) copy-start(bf16[4096]{0:T(1024)(128)(2,1)} %param.13) | copy-start | bytes 24580
  3.1 12.8 %copy-start.4 = (bf16[64,768]{1,0:T(8,128)(2,1)S(1)}, bf16[64,768]{1,0:T(8,128)(2,1)}, u32[]{:S(2)}) copy-start(bf16[64,768]{1,0:T(8,128)(2,1)} %get-tuple-element.24) | copy-start | bytes 294916
  3.1 40.7 %all-to-all-start = ((bf16[32,128,128]{2,1,0:T(8,128)(2,1)}), bf16[32,128,128]{2,1,0:T(8,128)(2,1)S(1)}, u32[]{:S(2)}, u32[]{:S(2)}) async-start(bf16[32,128,128]{2,1,0:T(8,128)(2,1)} %get-tuple-element.23), calls=%async_computation | async-start | bytes 2097152 | tf_op jit(solution)/shard_map/all_to_all | solution.py:258
  43.8 30.4 %all-to-all-start.1 = ((bf16[16,64,512]{2,1,0:T(8,128)(2,1)}), bf16[16,64,512]{2,1,0:T(8,128)(2,1)S(1)}, u32[]{:S(2)}, u32[]{:S(2)}) async-start(bf16[16,64,512]{2,1,0:T(8,128)(2,1)} %get-tuple-element.25), calls=%async_computation.1 | async-start | bytes 2097152 | tf_op jit(solution)/shard_map/all_to_all | solution.py:308
  48.4 4.3 %collective-permute-start = (bf16[8,64,768]{2,1,0:T(8,128)(2,1)S(1)}, bf16[8,64,768]{2,1,0:T(8,128)(2,1)}, u32[]{:S(2)}, u32[]{:S(2)}) collective-permute-start(bf16[8,64,768]{2,1,0:T(8,128)(2,1)S(1)} %all-gather.1.own_ref), channel_id=1, source_target_pairs={{0,1},{1,0},{2,3},{3,2},{4,5},{5,4},{6,7},{7,6},{8,9},{9,8},{10,11... | collective-permute-start | bytes 2359304 | tf_op jit(solution)/shard_map/ppermute | solution.py:304
  55.1 12.1 %collective-permute-start.1 = (bf16[784,128]{1,0:T(8,128)(2,1)S(1)}, bf16[784,128]{1,0:T(8,128)(2,1)S(1)}, u32[]{:S(2)}, u32[]{:S(2)}) collective-permute-start(bf16[784,128]{1,0:T(8,128)(2,1)S(1)} %get-tuple-element.30), channel_id=1, source_target_pairs={{0,4},{2,6},{4,0},{6,2},{1,5},{3,7},{5,1},{7,3},{8,12},{10,14},{12... | collective-permute-start | bytes 602120 | tf_op jit(solution)/shard_map/ppermute | solution.py:320
  58.5 11.4 %collective-permute-start.2 = (bf16[784,128]{1,0:T(8,128)(2,1)S(1)}, bf16[784,128]{1,0:T(8,128)(2,1)S(1)}, u32[]{:S(2)}, u32[]{:S(2)}) collective-permute-start(bf16[784,128]{1,0:T(8,128)(2,1)S(1)} %get-tuple-element.31), channel_id=1, source_target_pairs={{0,6},{2,0},{4,2},{6,4},{1,7},{3,1},{5,3},{7,5},{8,14},{10,8},{12,... | collective-permute-start | bytes 602120 | tf_op jit(solution)/shard_map/ppermute | solution.py:320
  61.2 8.7 %collective-permute-start.3 = (bf16[784,128]{1,0:T(8,128)(2,1)S(1)}, bf16[784,128]{1,0:T(8,128)(2,1)S(1)}, u32[]{:S(2)}, u32[]{:S(2)}) collective-permute-start(bf16[784,128]{1,0:T(8,128)(2,1)S(1)} %get-tuple-element.32), channel_id=1, source_target_pairs={{0,2},{2,4},{4,6},{6,0},{1,3},{3,5},{5,7},{7,1},{8,10},{10,12},{12... | collective-permute-start | bytes 602120 | tf_op jit(solution)/shard_map/ppermute | solution.py:320
  65.7 0.7 copy-start.2
  65.7 0.7 copy-start.3
  74.3 17.0 %collective-permute-start.4 = (bf16[16,64,512]{2,1,0:T(8,128)(2,1)S(1)}, bf16[16,64,512]{2,1,0:T(8,128)(2,1)S(1)}, u32[]{:S(2)}, u32[]{:S(2)}) collective-permute-start(bf16[16,64,512]{2,1,0:T(8,128)(2,1)S(1)} %all-to-all-done.1.own_ref), channel_id=1, source_target_pairs={{0,1},{1,0},{2,3},{3,2},{4,5},{5,4},{6,7},{7,6},{8,9},{9,8},{10,11... | collective-permute-start | bytes 3145736 | tf_op jit(solution)/shard_map/ppermute | solution.py:344
  92.8 10.1 %copy-start.5 = (bf16[512]{0:T(512)(128)(2,1)S(1)}, bf16[512]{0:T(512)(128)(2,1)}, u32[]{:S(2)}) copy-start(bf16[512]{0:T(512)(128)(2,1)} %param.18) | copy-start | bytes 3076
  92.8 21.8 %copy-start.1 = (bf16[128,512]{1,0:T(8,128)(2,1)S(1)}, bf16[128,512]{1,0:T(8,128)(2,1)}, u32[]{:S(2)}) copy-start(bf16[128,512]{1,0:T(8,128)(2,1)} %rows_ref.1) | copy-start | bytes 393220
  92.8 21.8 %all-to-all-start.3 = ((bf16[32,64,128]{2,1,0:T(8,128)(2,1)}), bf16[32,64,128]{2,1,0:T(8,128)(2,1)S(1)}, u32[]{:S(2)}, u32[]{:S(2)}) async-start(bf16[32,64,128]{2,1,0:T(8,128)(2,1)} %output.1), calls=%async_computation.3 | async-start | bytes 1048576 | tf_op jit(solution)/shard_map/all_to_all | solution.py:258
  102.9 0.7 copy-start.6
  116.1 25.4 %all-to-all-start.4 = ((bf16[64,2,512]{2,1,0:T(2,128)(2,1)}), bf16[64,2,512]{2,1,0:T(2,128)(2,1)S(1)}, u32[]{:S(2)}, u32[]{:S(2)}) async-start(bf16[64,2,512]{2,1,0:T(2,128)(2,1)} %all_to_all.22), calls=%async_computation.4 | async-start | bytes 262144 | tf_op jit(solution)/shard_map/all_to_all | solution.py:373

commit v8 on v6

--- a/solution.py
+++ b/solution.py
@@ -188,7 +188,7 @@
         result = (weighted / sums).astype(bf16)
         for b in range(NB):
             for g in range(NX):
-                out_ref[g * NB + b, :, h * HD : (h + 1) * HD] = result[b * HALF : (b + 1) * HALF]
+                out_ref[b * NX + g, :, h * HD : (h + 1) * HD] = result[b * HALF : (b + 1) * HALF]
 
 
 def output_kernel(x_ref, own_ref, other_ref, out_ref):
@@ -200,7 +200,7 @@
             for z in (2 * n, 2 * n + 1):
                 own, other = own_ref[z * NB + b], other_ref[z * NB + b]
                 rows += [jnp.where(first, own, other), jnp.where(first, other, own)]
-            x = jnp.concatenate([x_ref[g * NB + b] for g in range(NX)])
+            x = x_ref[b * NX : (b + 1) * NX].reshape(NX * HALF, QW)
             term = lax.dot_general(
                 x,
                 jnp.concatenate(rows),
@@ -335,7 +335,7 @@
     out_own, attended = lax.optimization_barrier((out_own, attended))
     out_other = lax.ppermute(out_own, "core", swap)
 
-    slab = lax.all_to_all(attended, ("x", "two"), split_axis=0, concat_axis=0, tiled=True)
+    slab = lax.all_to_all(attended, ("two", "x"), split_axis=0, concat_axis=0, tiled=True)
     products = call(
         output_kernel,
         jax.ShapeDtypeStruct((NT * NX, HALF, BLK), bf16),

time: 143 us -> 143 us (level)
  no operation moved by 1% of the time
where the time goes in v8:
time: 143 us; the launch traced here: 142 us
  blocking collectives  60 us (42%)
  starting transfers between devices  49 us (34%)
  waiting for transfers between devices  19.3 us (13%)
  Pallas kernels  9.82 us (7%)
  local copies, waits for them, and re-layouts  2.89 us (2%)
    all_gather x2, blocking collectives, body(): own = lax.all_gather(lax.all_gather(shard, 'pair'), 'quad')  27.9 us
    all_to_all x2, starting transfers between devices, exchange(): lax.all_to_all(blocks, TP + ('x',), split_axis=0, concat_axis=0, tiled=Tr...  22.9 us
    psum x1, blocking collectives, body(): stat = lax.psum(stat[:, :RESP], TP)  17.1 us
    all_to_all x1, blocking collectives, body(): lax.all_to_all(attended, ('two', 'x'), split_axis=0, concat_axis=0, tiled...  14.9 us
    all_to_all x2, waiting for transfers between devices, exchange(): lax.all_to_all(blocks, TP + ('x',), split_axis=0, concat_axis=0, tiled=Tr...  11.6 us
    ppermute x3, starting transfers between devices, body(): lax.ppermute(parts[s], 'x', [(i, (i + s) % NX) for i in range(NX)])  10.4 us
    all_to_all x1, starting transfers between devices, body(): lax.all_to_all(placed, ('x',) + Z + ('core',), split_axis=0, concat_axis=...  7.28 us
    all_to_all x1, starting transfers between devices, body(): lax.all_to_all(out_sent, Z + ('two',), split_axis=0, concat_axis=0, tiled...  4.55 us
  transfers between devices with their start and end apart: 9, of which 4 were waited for; matrix products, arithmetic and copies ran while one was open for 0% of the time, Pallas kernels for 4%

profile of v8, /device:TPU:6, one launch (start us, length us, event | category | flops | bytes accessed | tf_op | source)
XLA Modules:
  0.0 142.4 jit_solution(1981585534471312198)
XLA Ops:
  0.6 2.5 %prepare.1 = (bf16[32,128,128]{2,1,0:T(8,128)(2,1)}, bf16[64,768]{1,0:T(8,128)(2,1)}, bf16[16,64,512]{2,1,0:T(8,128)(2,1)}) custom-call(bf16[128,512]{1,0:T(8,128)(2,1)} %rows_ref.1, bf16[64,512]{1,0:T(8,128)(2,1)} %query.1, bf16[64,256]{1,0:T(8,128)(2,1)} %key.1, bf16[64,256]{1,0:T(8,128)(2,1)} %value.1, bf16[64,512]{1,0:T(8,128)(2,1)} %bitcast.21), custom_call_target="tpu_custom_call" | custom-call | bytes 4194304 | tf_op jit(solution)/shard_map/prepare/pallas_call | solution.py:275
  3.1 12.8 %all-to-all-start = ((bf16[32,128,128]{2,1,0:T(8,128)(2,1)}), bf16[32,128,128]{2,1,0:T(8,128)(2,1)S(1)}, u32[]{:S(2)}, u32[]{:S(2)}) async-start(bf16[32,128,128]{2,1,0:T(8,128)(2,1)} %get-tuple-element.23), calls=%async_computation | async-start | bytes 2097152 | tf_op jit(solution)/shard_map/all_to_all | solution.py:250
  15.9 5.3 %all-gather = bf16[128,768]{1,0:T(8,128)(2,1)S(1)} all-gather(bf16[64,768]{1,0:T(8,128)(2,1)S(1)} %copy-done.4), channel_id=2, replica_groups=mesh['four'=4,'two'=2,'quad'=4,'pair'=2,'x'=4,'core'=2] {'pair'}, dimensions={0}, use_global_device_ids=true | all-gather | bytes 294912 | tf_op jit(solution)/shard_map/all_gather | solution.py:294
  21.2 22.6 %all-gather.1.own_ref = bf16[8,64,768]{2,1,0:T(8,128)(2,1)S(1)} all-gather(bf16[2,64,768]{2,1,0:T(8,128)(2,1)S(1)} %bitcast.19), channel_id=3, replica_groups=mesh['four'=4,'two'=2,'quad'=4,'pair'=2,'x'=4,'core'=2] {'quad'}, dimensions={0}, use_global_device_ids=true | all-gather | bytes 983040 | tf_op jit(solution)/shard_map/all_gather | solution.py:294
  43.8 4.5 %all-to-all-start.1 = ((bf16[16,64,512]{2,1,0:T(8,128)(2,1)}), bf16[16,64,512]{2,1,0:T(8,128)(2,1)S(1)}, u32[]{:S(2)}, u32[]{:S(2)}) async-start(bf16[16,64,512]{2,1,0:T(8,128)(2,1)} %get-tuple-element.25), calls=%async_computation.1 | async-start | bytes 2097152 | tf_op jit(solution)/shard_map/all_to_all | solution.py:300
  48.4 1.9 %collective-permute-start = (bf16[8,64,768]{2,1,0:T(8,128)(2,1)S(1)}, bf16[8,64,768]{2,1,0:T(8,128)(2,1)}, u32[]{:S(2)}, u32[]{:S(2)}) collective-permute-start(bf16[8,64,768]{2,1,0:T(8,128)(2,1)S(1)} %all-gather.1.own_ref), channel_id=1, source_target_pairs={{0,1},{1,0},{2,3},{3,2},{4,5},{5,4},{6,7},{7,6},{8,9},{9,8},{10,11... | collective-permute-start | bytes 2359304 | tf_op jit(solution)/shard_map/ppermute | solution.py:296
  50.4 2.3 %collective-permute-done.other_ref = bf16[8,64,768]{2,1,0:T(8,128)(2,1)} collective-permute-done((bf16[8,64,768]{2,1,0:T(8,128)(2,1)S(1)}, bf16[8,64,768]{2,1,0:T(8,128)(2,1)}, u32[]{:S(2)}, u32[]{:S(2)}) %collective-permute-start) | collective-permute-done | bytes 786464 | tf_op jit(solution)/shard_map/ppermute | solution.py:296
  52.7 2.3 %project.1 = (bf16[784,128]{1,0:T(8,128)(2,1)S(1)}, bf16[784,128]{1,0:T(8,128)(2,1)S(1)}, bf16[784,128]{1,0:T(8,128)(2,1)S(1)}, bf16[784,128]{1,0:T(8,128)(2,1)S(1)}) custom-call(bf16[32,128,128]{2,1,0:T(8,128)(2,1)S(1)} %all-to-all-done.x_ref, bf16[8,64,768]{2,1,0:T(8,128)(2,1)S(1)} %all-gather.1.own_ref, ...), custom_call_target="tpu_custom_call" | custom-call | flops 805306368 | bytes 4194304 | tf_op jit(solution)/shard_map/project/pallas_call | solution.py:303
  55.0 3.4 %collective-permute-start.1 = (bf16[784,128]{1,0:T(8,128)(2,1)S(1)}, bf16[784,128]{1,0:T(8,128)(2,1)S(1)}, u32[]{:S(2)}, u32[]{:S(2)}) collective-permute-start(bf16[784,128]{1,0:T(8,128)(2,1)S(1)} %get-tuple-element.30), channel_id=1, source_target_pairs={{0,4},{2,6},{4,0},{6,2},{1,5},{3,7},{5,1},{7,3},{8,12},{10,14},{12... | collective-permute-start | bytes 602120 | tf_op jit(solution)/shard_map/ppermute | solution.py:312
  58.4 2.6 %collective-permute-start.2 = (bf16[784,128]{1,0:T(8,128)(2,1)S(1)}, bf16[784,128]{1,0:T(8,128)(2,1)S(1)}, u32[]{:S(2)}, u32[]{:S(2)}) collective-permute-start(bf16[784,128]{1,0:T(8,128)(2,1)S(1)} %get-tuple-element.31), channel_id=1, source_target_pairs={{0,6},{2,0},{4,2},{6,4},{1,7},{3,1},{5,3},{7,5},{8,14},{10,8},{12,... | collective-permute-start | bytes 602120 | tf_op jit(solution)/shard_map/ppermute | solution.py:312
  61.0 4.4 %collective-permute-start.3 = (bf16[784,128]{1,0:T(8,128)(2,1)S(1)}, bf16[784,128]{1,0:T(8,128)(2,1)S(1)}, u32[]{:S(2)}, u32[]{:S(2)}) collective-permute-start(bf16[784,128]{1,0:T(8,128)(2,1)S(1)} %get-tuple-element.32), channel_id=1, source_target_pairs={{0,2},{2,4},{4,6},{6,0},{1,3},{3,5},{5,7},{7,1},{8,10},{10,12},{12... | collective-permute-start | bytes 602120 | tf_op jit(solution)/shard_map/ppermute | solution.py:312
  66.2 0.9 tables.1
  67.1 2.6 %collective-permute-done.2.part2 = bf16[784,128]{1,0:T(8,128)(2,1)S(1)} collective-permute-done((bf16[784,128]{1,0:T(8,128)(2,1)S(1)}, bf16[784,128]{1,0:T(8,128)(2,1)S(1)}, u32[]{:S(2)}, u32[]{:S(2)}) %collective-permute-start.2) | collective-permute-done | bytes 200736 | tf_op jit(solution)/shard_map/ppermute | solution.py:312
  69.7 1.8 %attend.1 = bf16[8,64,512]{2,1,0:T(8,128)(2,1)S(1)} custom-call(s32[1,8]{1,0:T(1,128)S(1)} %copy-done.2, bf16[784,128]{1,0:T(8,128)(2,1)S(1)} %get-tuple-element.29.part0, bf16[784,128]{1,0:T(8,128)(2,1)S(1)} %collective-permute-done.1.part1, bf16[784,128]{1,0:T(8,128)(2,1)S(1)} %collective-permute-done.2.part2, ...), custom_call_target="tpu_custom_call" | custom-call | flops 33554432 | bytes 4194304 | tf_op jit(solution)/shard_map/attend/pallas_call | solution.py:327
  71.6 2.7 %all-to-all-done.1.own_ref = bf16[16,64,512]{2,1,0:T(8,128)(2,1)S(1)} async-done(((bf16[16,64,512]{2,1,0:T(8,128)(2,1)}), bf16[16,64,512]{2,1,0:T(8,128)(2,1)S(1)}, u32[]{:S(2)}, u32[]{:S(2)}) %all-to-all-start.1) | async-done | bytes 1048608 | tf_op jit(solution)/shard_map/all_to_all | solution.py:300
  74.3 1.9 %collective-permute-start.4 = (bf16[16,64,512]{2,1,0:T(8,128)(2,1)S(1)}, bf16[16,64,512]{2,1,0:T(8,128)(2,1)S(1)}, u32[]{:S(2)}, u32[]{:S(2)}) collective-permute-start(bf16[16,64,512]{2,1,0:T(8,128)(2,1)S(1)} %all-to-all-done.1.own_ref), channel_id=1, source_target_pairs={{0,1},{1,0},{2,3},{3,2},{4,5},{5,4},{6,7},{7,6},{8,9},{9,8},{10,11... | collective-permute-start | bytes 3145736 | tf_op jit(solution)/shard_map/ppermute | solution.py:336
  76.2 14.9 %all_to_all.29.x_ref = bf16[8,64,512]{2,1,0:T(8,128)(2,1)S(1)} all-to-all(bf16[8,64,512]{2,1,0:T(8,128)(2,1)S(1)} %attend.1), channel_id=1, replica_groups=mesh['four'=4,'two'=2,'quad'=4,'pair'=2,'x'=4,'core'=2] {'two','x'}, dimensions={0} | all-to-all | bytes 1048576 | tf_op jit(solution)/shard_map/all_to_all | solution.py:338
  91.1 1.6 %output.1 = bf16[32,64,128]{2,1,0:T(8,128)(2,1)} custom-call(bf16[8,64,512]{2,1,0:T(8,128)(2,1)S(1)} %all_to_all.29.x_ref, bf16[16,64,512]{2,1,0:T(8,128)(2,1)S(1)} %all-to-all-done.1.own_ref, bf16[16,64,512]{2,1,0:T(8,128)(2,1)S(1)} %collective-permute-done.4.other_ref), custom_call_target="tpu_custom_call" | custom-call | flops 536870912 | bytes 4194304 | tf_op jit(solution)/shard_map/output/pallas_call | solution.py:339
  92.7 10.1 %all-to-all-start.3 = ((bf16[32,64,128]{2,1,0:T(8,128)(2,1)}), bf16[32,64,128]{2,1,0:T(8,128)(2,1)S(1)}, u32[]{:S(2)}, u32[]{:S(2)}) async-start(bf16[32,64,128]{2,1,0:T(8,128)(2,1)} %output.1), calls=%async_computation.3 | async-start | bytes 1048576 | tf_op jit(solution)/shard_map/all_to_all | solution.py:250
  103.5 11.6 %all-to-all-done.3.parts_ref = bf16[32,64,128]{2,1,0:T(8,128)(2,1)S(1)} async-done(((bf16[32,64,128]{2,1,0:T(8,128)(2,1)}), bf16[32,64,128]{2,1,0:T(8,128)(2,1)S(1)}, u32[]{:S(2)}, u32[]{:S(2)}) %all-to-all-start.3) | async-done | bytes 524320 | tf_op jit(solution)/shard_map/all_to_all | solution.py:250
  115.1 0.8 layer.1
  115.9 0.7 all_to_all.22
  116.6 7.3 %all-to-all-start.4 = ((bf16[64,2,512]{2,1,0:T(2,128)(2,1)}), bf16[64,2,512]{2,1,0:T(2,128)(2,1)S(1)}, u32[]{:S(2)}, u32[]{:S(2)}) async-start(bf16[64,2,512]{2,1,0:T(2,128)(2,1)} %all_to_all.22), calls=%async_computation.4 | async-start | bytes 262144 | tf_op jit(solution)/shard_map/all_to_all | solution.py:365
  123.9 17.1 %psum.7 = f32[2,8]{1,0:T(2,128)S(1)} all-reduce(f32[2,8]{1,0:T(2,128)S(1)} %bitcast.17), channel_id=1, replica_groups=mesh['four'=4,'two'=2,'quad'=4,'pair'=2,'x'=4,'core'=2] {'four','two'}, use_global_device_ids=true, to_apply=%region_0.0 | all-reduce | flops 16 | bytes 128 | tf_op jit(solution)/shard_map/psum | solution.py:367
  (29 shorter events, 2.8 us)
Async XLA Ops:
  0.6 49.7 %copy-start = (bf16[4096]{0:T(1024)(128)(2,1)S(1)}, bf16[4096]{0:T(1024)(128)(2,1)}, u32[]{:S(2)}) copy-start(bf16[4096]{0:T(1024)(128)(2,1)} %param.13) | copy-start | bytes 24580
  3.1 12.8 %copy-start.4 = (bf16[64,768]{1,0:T(8,128)(2,1)S(1)}, bf16[64,768]{1,0:T(8,128)(2,1)}, u32[]{:S(2)}) copy-start(bf16[64,768]{1,0:T(8,128)(2,1)} %get-tuple-element.24) | copy-start | bytes 294916
  3.1 40.7 %all-to-all-start = ((bf16[32,128,128]{2,1,0:T(8,128)(2,1)}), bf16[32,128,128]{2,1,0:T(8,128)(2,1)S(1)}, u32[]{:S(2)}, u32[]{:S(2)}) async-start(bf16[32,128,128]{2,1,0:T(8,128)(2,1)} %get-tuple-element.23), calls=%async_computation | async-start | bytes 2097152 | tf_op jit(solution)/shard_map/all_to_all | solution.py:250
  43.8 30.4 %all-to-all-start.1 = ((bf16[16,64,512]{2,1,0:T(8,128)(2,1)}), bf16[16,64,512]{2,1,0:T(8,128)(2,1)S(1)}, u32[]{:S(2)}, u32[]{:S(2)}) async-start(bf16[16,64,512]{2,1,0:T(8,128)(2,1)} %get-tuple-element.25), calls=%async_computation.1 | async-start | bytes 2097152 | tf_op jit(solution)/shard_map/all_to_all | solution.py:300
  48.4 4.3 %collective-permute-start = (bf16[8,64,768]{2,1,0:T(8,128)(2,1)S(1)}, bf16[8,64,768]{2,1,0:T(8,128)(2,1)}, u32[]{:S(2)}, u32[]{:S(2)}) collective-permute-start(bf16[8,64,768]{2,1,0:T(8,128)(2,1)S(1)} %all-gather.1.own_ref), channel_id=1, source_target_pairs={{0,1},{1,0},{2,3},{3,2},{4,5},{5,4},{6,7},{7,6},{8,9},{9,8},{10,11... | collective-permute-start | bytes 2359304 | tf_op jit(solution)/shard_map/ppermute | solution.py:296
  55.0 12.1 %collective-permute-start.1 = (bf16[784,128]{1,0:T(8,128)(2,1)S(1)}, bf16[784,128]{1,0:T(8,128)(2,1)S(1)}, u32[]{:S(2)}, u32[]{:S(2)}) collective-permute-start(bf16[784,128]{1,0:T(8,128)(2,1)S(1)} %get-tuple-element.30), channel_id=1, source_target_pairs={{0,4},{2,6},{4,0},{6,2},{1,5},{3,7},{5,1},{7,3},{8,12},{10,14},{12... | collective-permute-start | bytes 602120 | tf_op jit(solution)/shard_map/ppermute | solution.py:312
  58.4 11.4 %collective-permute-start.2 = (bf16[784,128]{1,0:T(8,128)(2,1)S(1)}, bf16[784,128]{1,0:T(8,128)(2,1)S(1)}, u32[]{:S(2)}, u32[]{:S(2)}) collective-permute-start(bf16[784,128]{1,0:T(8,128)(2,1)S(1)} %get-tuple-element.31), channel_id=1, source_target_pairs={{0,6},{2,0},{4,2},{6,4},{1,7},{3,1},{5,3},{7,5},{8,14},{10,8},{12,... | collective-permute-start | bytes 602120 | tf_op jit(solution)/shard_map/ppermute | solution.py:312
  61.0 8.7 %collective-permute-start.3 = (bf16[784,128]{1,0:T(8,128)(2,1)S(1)}, bf16[784,128]{1,0:T(8,128)(2,1)S(1)}, u32[]{:S(2)}, u32[]{:S(2)}) collective-permute-start(bf16[784,128]{1,0:T(8,128)(2,1)S(1)} %get-tuple-element.32), channel_id=1, source_target_pairs={{0,2},{2,4},{4,6},{6,0},{1,3},{3,5},{5,7},{7,1},{8,10},{10,12},{12... | collective-permute-start | bytes 602120 | tf_op jit(solution)/shard_map/ppermute | solution.py:312
  65.5 0.7 copy-start.2
  65.5 0.7 copy-start.3
  74.3 16.9 %collective-permute-start.4 = (bf16[16,64,512]{2,1,0:T(8,128)(2,1)S(1)}, bf16[16,64,512]{2,1,0:T(8,128)(2,1)S(1)}, u32[]{:S(2)}, u32[]{:S(2)}) collective-permute-start(bf16[16,64,512]{2,1,0:T(8,128)(2,1)S(1)} %all-to-all-done.1.own_ref), channel_id=1, source_target_pairs={{0,1},{1,0},{2,3},{3,2},{4,5},{5,4},{6,7},{7,6},{8,9},{9,8},{10,11... | collective-permute-start | bytes 3145736 | tf_op jit(solution)/shard_map/ppermute | solution.py:336
  92.7 10.1 %copy-start.5 = (bf16[512]{0:T(512)(128)(2,1)S(1)}, bf16[512]{0:T(512)(128)(2,1)}, u32[]{:S(2)}) copy-start(bf16[512]{0:T(512)(128)(2,1)} %param.18) | copy-start | bytes 3076
  92.7 22.4 %copy-start.1 = (bf16[128,512]{1,0:T(8,128)(2,1)S(1)}, bf16[128,512]{1,0:T(8,128)(2,1)}, u32[]{:S(2)}) copy-start(bf16[128,512]{1,0:T(8,128)(2,1)} %rows_ref.1) | copy-start | bytes 393220
  92.7 22.4 %all-to-all-start.3 = ((bf16[32,64,128]{2,1,0:T(8,128)(2,1)}), bf16[32,64,128]{2,1,0:T(8,128)(2,1)S(1)}, u32[]{:S(2)}, u32[]{:S(2)}) async-start(bf16[32,64,128]{2,1,0:T(8,128)(2,1)} %output.1), calls=%async_computation.3 | async-start | bytes 1048576 | tf_op jit(solution)/shard_map/all_to_all | solution.py:250
  102.9 0.7 copy-start.6
  116.6 24.9 %all-to-all-start.4 = ((bf16[64,2,512]{2,1,0:T(2,128)(2,1)}), bf16[64,2,512]{2,1,0:T(2,128)(2,1)S(1)}, u32[]{:S(2)}, u32[]{:S(2)}) async-start(bf16[64,2,512]{2,1,0:T(2,128)(2,1)} %all_to_all.22), calls=%async_computation.4 | async-start | bytes 262144 | tf_op jit(solution)/shard_map/all_to_all | solution.py:365
